TPU v7x, 512 devices: a whole 4x8x8 slice. The times are simulated.
512 devices in a mesh: section: 4 (over x), dom: 128 (over y, z, core).
Axes of the slice: x: 4, y: 8, z: 8, core: 2. Of those that a mesh axis runs over, the one named last changes fastest.
Arguments:
- stacked: bfloat16 [4, 16384, 1024], P('section', 'dom'), may hold values from -6 to 6
- edges: int32 [16384, 256], P('dom'), may hold values 0 or 1
- picks: int32 [256, 3], P('dom'), may hold values from 0 to 2
- self_w: bfloat16 [4, 1024, 1024], P('section'), may hold values from -0.1875 to 0.1875
- neigh_w: bfloat16 [4, 1024, 1024], P('section'), may hold values from -0.75 to 0.75
Outputs:
- embeddings: bfloat16 [4, 16384, 1024], P('section', 'dom')
Inputs may be any that keep to these rules, and one draw needn't show every extreme that they name: `picks`: A value of 2 means that the destination block has no tile from that direction; smaller values name a slab of the peer partition.
All inputs are finite; a program needn't handle non-finite values. No bound on the sum of `edges` on one device may be relied on, other than what follows from the above.
Results may differ from a plain program's by a relative error of at most 0.006.
Values may be sent and summed in bfloat16 or wider, within the bound.
No kernel may reach another device: no remote copies, remote signals or barrier semaphores. Data moves between devices by JAX's collectives and lax.ppermute only.
A program may use at most 64 MiB of HBM per device.

v0:
```python
import jax
import jax.numpy as jnp
from jax import lax
from jax.sharding import PartitionSpec as P

BLOCK = 64


peer_offsets = (-1, 1, 2)


def passed_along(block, axis, distance):
    devices = range(lax.axis_size(axis))
    route = [((i - distance) % len(devices), i) for i in devices]
    return lax.ppermute(block, axis, route)


def from_behind(value, axis, steps):
    count = lax.axis_size(axis)
    initial, last = (max(0, -steps), min(count, count - steps))
    return lax.ppermute(value, axis, [(source, source + steps) for source in range(initial, last)])


def tile_term(edge_rows, position, source_rows):
    tile_mask = edge_rows[:, position * BLOCK : (position + 1) * BLOCK]
    product = jnp.dot(
        tile_mask.astype(jnp.bfloat16), source_rows, preferred_element_type=jnp.float32
    )
    return (product, jnp.sum(tile_mask.astype(jnp.float32), axis=1))


def per_device(stacked, edges, picks, self_w, neigh_w):
    node_rows = stacked.shape[1]
    feature_width = stacked.shape[2]
    slab_count = node_rows // BLOCK
    section_index = lax.axis_index("section")
    weight_self = self_w[0]
    weight_neigh = neigh_w[0]
    asked = []
    for position in range(3):
        asked.append(passed_along(picks[:, position], "dom", peer_offsets[position]))

    def chosen(buffer, position, slab_now):
        wanted = lax.dynamic_index_in_dim(asked[position], slab_now, 0, keepdims=False)
        wanted = jnp.minimum(wanted, slab_count - 1)
        return lax.dynamic_slice_in_dim(buffer, wanted * BLOCK, BLOCK, 0)

    def fetch(buffer, slab_now):
        lower = passed_along(chosen(buffer, 0, slab_now), "dom", 1)
        uppers = []
        for position in (1, 2):
            uppers.append(
                passed_along(chosen(buffer, position, slab_now), "dom", -peer_offsets[position])
            )
        return (lower, uppers[0], uppers[1])

    def one_step(step_now, carry):
        buffer, result, incoming = carry
        slab_raw = step_now - section_index
        active = (slab_raw >= 0) & (slab_raw < slab_count)
        slab_now = jnp.clip(slab_raw, 0, slab_count - 1)
        refresh = active & (section_index > 0)
        start_row = slab_now * BLOCK
        current = lax.dynamic_slice_in_dim(buffer, start_row, BLOCK, 0)
        own_rows = jnp.where(refresh, incoming, current)
        buffer = lax.dynamic_update_slice_in_dim(buffer, own_rows, start_row, 0)
        edge_rows = lax.dynamic_slice_in_dim(edges, start_row, BLOCK, 0)
        live_row = lax.dynamic_index_in_dim(picks, slab_now, 0, keepdims=False) < slab_count
        received = fetch(buffer, slab_now)
        local_sum, local_count = tile_term(edge_rows, 0, own_rows)
        self_part = jnp.dot(own_rows, weight_self, preferred_element_type=jnp.float32)
        summed = local_sum
        degree = 1.0 + local_count
        for position in range(3):
            term, counted = tile_term(edge_rows, position + 1, received[position])
            summed = summed + jnp.where(live_row[position], term, 0.0)
            degree = degree + jnp.where(live_row[position], counted, 0.0)
        mean_rows = (summed / degree[:, None]).astype(jnp.bfloat16)
        hidden = self_part + jnp.dot(mean_rows, weight_neigh, preferred_element_type=jnp.float32)
        produced = jnp.maximum(hidden, 0.0).astype(jnp.bfloat16)
        previous = lax.dynamic_slice_in_dim(result, start_row, BLOCK, 0)
        result = lax.dynamic_update_slice_in_dim(
            result, jnp.where(active, produced, previous), start_row, 0
        )
        incoming = from_behind(produced, "section", 1)
        return (buffer, result, incoming)

    initial = (
        stacked[0],
        jnp.zeros_like(stacked[0]),
        jnp.zeros((BLOCK, feature_width), jnp.bfloat16),
    )
    final = lax.fori_loop(0, slab_count + lax.axis_size("section") - 1, one_step, initial)
    return final[1][None]


def solution(mesh):
    in_specs = (
        P("section", "dom", None),
        P("dom", None),
        P("dom", None),
        P("section", None, None),
        P("section", None, None),
    )
    out_specs = P("section", "dom", None)
    return jax.shard_map(
        per_device, mesh=mesh, in_specs=in_specs, out_specs=out_specs, check_vma=False
    )
```

profile of v0, /device:TPU:7, one launch (start us, length us, event | category | flops | bytes accessed | tf_op | source)
XLA Modules:
  0.0 197.8 jit_solution(16663670118005565187)
XLA Ops:
  2.0 2.6 %collective-permute-start.4 = (s32[2]{0:T(128)S(1)}, s32[2]{0:T(128)S(1)}, u32[]{:S(2)}, u32[]{:S(2)}) collective-permute-start(s32[2]{0:T(128)S(1)} %get-tuple-element.264), channel_id=1, source_target_pairs={{1,0},{2,1},{3,2},{4,3},{5,4},{6,5},{7,6},{8,7},{9,8},{10,9},{11,1... | collective-permute-start | bytes 32 | tf_op jit(solution)/shard_map/ppermute | solution.py:15
  4.5 3.9 %collective-permute-start.5 = (s32[2]{0:T(128)S(1)}, s32[2]{0:T(128)S(1)}, u32[]{:S(2)}, u32[]{:S(2)}) collective-permute-start(s32[2]{0:T(128)S(1)} %get-tuple-element.263), channel_id=1, source_target_pairs={{127,0},{0,1},{1,2},{2,3},{3,4},{4,5},{5,6},{6,7},{7,8},{8,9},{9,1... | collective-permute-start | bytes 32 | tf_op jit(solution)/shard_map/ppermute | solution.py:15
  8.5 4.0 %collective-permute-start.6 = (s32[2]{0:T(128)S(1)}, s32[2]{0:T(128)S(1)}, u32[]{:S(2)}, u32[]{:S(2)}) collective-permute-start(s32[2]{0:T(128)S(1)} %get-tuple-element.262), channel_id=1, source_target_pairs={{126,0},{127,1},{0,2},{1,3},{2,4},{3,5},{4,6},{5,7},{6,8},{7,9},{8... | collective-permute-start | bytes 32 | tf_op jit(solution)/shard_map/ppermute | solution.py:15
  12.5 6.0 %collective-permute-done.5 = s32[2]{0:T(128)S(1)} collective-permute-done((s32[2]{0:T(128)S(1)}, s32[2]{0:T(128)S(1)}, u32[]{:S(2)}, u32[]{:S(2)}) %collective-permute-start.5) | collective-permute-done | bytes 40 | tf_op jit(solution)/shard_map/ppermute | solution.py:15
  18.4 6.9 %collective-permute-done.6 = s32[2]{0:T(128)S(1)} collective-permute-done((s32[2]{0:T(128)S(1)}, s32[2]{0:T(128)S(1)}, u32[]{:S(2)}, u32[]{:S(2)}) %collective-permute-start.6) | collective-permute-done | bytes 40 | tf_op jit(solution)/shard_map/ppermute | solution.py:15
  26.1 171.7 %while.18 = (s32[]{:T(128)}, bf16[128,1024]{1,0:T(8,128)(2,1)S(1)}, bf16[128,1024]{1,0:T(8,128)(2,1)}, bf16[64,1024]{1,0:T(8,128)(2,1)S(1)}, s32[]{:T(128)}, /*i...) while((s32[]{:T(128)}, bf16[128,1024]{1,0:T(8,128)(2,1)S(1)}, ...), condition=%wide.region_5.6_spmd, body=%wide.region_0.5_spmd.sunk | while | flops 302891200 | bytes 19863640 | solution.py:93
  30.1 1.9 collective-permute-start
  32.0 3.2 %collective-permute-start.1 = (bf16[64,1024]{1,0:T(8,128)(2,1)S(1)}, bf16[64,1024]{1,0:T(8,128)(2,1)S(1)}, u32[]{:S(2)}, u32[]{:S(2)}) collective-permute-start(bf16[64,1024]{1,0:T(8,128)(2,1)S(1)} %get-tuple-element.398), channel_id=1, source_target_pairs={{1,0},{2,1},{3,2},{4,3},{5,4},{6,5},{7,6},{8,7},{9,8},{10,9},{11,1... | collective-permute-start | bytes 393224 | tf_op jit(solution)/shard_map/while/body/eval_jaxpr/ppermute | solution.py:15
  35.2 6.6 %collective-permute-start.2 = (bf16[64,1024]{1,0:T(8,128)(2,1)S(1)}, bf16[64,1024]{1,0:T(8,128)(2,1)S(1)}, u32[]{:S(2)}, u32[]{:S(2)}) collective-permute-start(bf16[64,1024]{1,0:T(8,128)(2,1)S(1)} %get-tuple-element.400), channel_id=1, source_target_pairs={{2,0},{3,1},{4,2},{5,3},{6,4},{7,5},{8,6},{9,7},{10,8},{11,9},{12,... | collective-permute-start | bytes 393224 | tf_op jit(solution)/shard_map/while/body/eval_jaxpr/ppermute | solution.py:15
  44.1 2.2 %fusion.47 = f32[64,1024]{1,0:T(8,128)S(1)} fusion(bf16[64,1024]{1,0:T(8,128)(2,1)S(1)} %get-tuple-element.395, bf16[1024,1024]{1,0:T(8,128)(2,1)} %get-tuple-element.460), kind=kOutput, calls=%fused_computation.43.clone.1 | convolution fusion | flops 134217728 | bytes 2490368 | tf_op jit(solution)/shard_map/while/body/eval_jaxpr/dot_general | solution.py:71
  51.0 2.9 %select_dynamic-update-slice_fusion.2 = (bf16[128,1024]{1,0:T(8,128)(2,1)}, bf16[64,1024]{1,0:T(8,128)(2,1)S(1)}) fusion(bf16[128,1024]{1,0:T(8,128)(2,1)} %get-tuple-element.433, s32[]{:T(128)S(6)} %select_n.272, pred[]{:T(512)S(6)} %and.19, f32[64,1024]{1,0:T(8,128)S(1)} %fusion.47, bf16[1024,1024]{1,0:T(8,128)(2,1)S(1)} %copy-done, ...), kind=kOutput, calls=%fused_computation.11.clone.1 | convolution fusion | flops 143134720 | bytes 3181568 | tf_op jit(solution)/shard_map/while/body/eval_jaxpr/dot_general | solution.py:79
  55.2 5.3 %collective-permute-done.3 = bf16[64,1024]{1,0:T(8,128)(2,1)S(1)} collective-permute-done((bf16[64,1024]{1,0:T(8,128)(2,1)S(1)}, bf16[64,1024]{1,0:T(8,128)(2,1)S(1)}, u32[]{:S(2)}, u32[]{:S(2)}) %collective-permute-start.3) | collective-permute-done | bytes 131104 | tf_op jit(solution)/shard_map/while/body/eval_jaxpr/ppermute | solution.py:21
  64.4 4.2 %collective-permute-start = (bf16[64,1024]{1,0:T(8,128)(2,1)S(1)}, bf16[64,1024]{1,0:T(8,128)(2,1)}, u32[]{:S(2)}, u32[]{:S(2)}) collective-permute-start(bf16[64,1024]{1,0:T(8,128)(2,1)S(1)} %get-tuple-element.396), channel_id=1, source_target_pairs={{127,0},{0,1},{1,2},{2,3},{3,4},{4,5},{5,6},{6,7},{7,8},{8,9},{9,1... | collective-permute-start | bytes 393224 | tf_op jit(solution)/shard_map/while/body/eval_jaxpr/ppermute | solution.py:15
  70.6 5.5 %collective-permute-start.2 = (bf16[64,1024]{1,0:T(8,128)(2,1)S(1)}, bf16[64,1024]{1,0:T(8,128)(2,1)S(1)}, u32[]{:S(2)}, u32[]{:S(2)}) collective-permute-start(bf16[64,1024]{1,0:T(8,128)(2,1)S(1)} %get-tuple-element.400), channel_id=1, source_target_pairs={{2,0},{3,1},{4,2},{5,3},{6,4},{7,5},{8,6},{9,7},{10,8},{11,9},{12,... | collective-permute-start | bytes 393224 | tf_op jit(solution)/shard_map/while/body/eval_jaxpr/ppermute | solution.py:15
  78.4 2.2 %fusion.47 = f32[64,1024]{1,0:T(8,128)S(1)} fusion(bf16[64,1024]{1,0:T(8,128)(2,1)S(1)} %get-tuple-element.395, bf16[1024,1024]{1,0:T(8,128)(2,1)} %get-tuple-element.460), kind=kOutput, calls=%fused_computation.43.clone.1 | convolution fusion | flops 134217728 | bytes 2490368 | tf_op jit(solution)/shard_map/while/body/eval_jaxpr/dot_general | solution.py:71
  85.4 2.9 %select_dynamic-update-slice_fusion.2 = (bf16[128,1024]{1,0:T(8,128)(2,1)}, bf16[64,1024]{1,0:T(8,128)(2,1)S(1)}) fusion(bf16[128,1024]{1,0:T(8,128)(2,1)} %get-tuple-element.433, s32[]{:T(128)S(6)} %select_n.272, pred[]{:T(512)S(6)} %and.19, f32[64,1024]{1,0:T(8,128)S(1)} %fusion.47, bf16[1024,1024]{1,0:T(8,128)(2,1)S(1)} %copy-done, ...), kind=kOutput, calls=%fused_computation.11.clone.1 | convolution fusion | flops 143134720 | bytes 3181568 | tf_op jit(solution)/shard_map/while/body/eval_jaxpr/dot_general | solution.py:79
  89.5 5.3 %collective-permute-done.3 = bf16[64,1024]{1,0:T(8,128)(2,1)S(1)} collective-permute-done((bf16[64,1024]{1,0:T(8,128)(2,1)S(1)}, bf16[64,1024]{1,0:T(8,128)(2,1)S(1)}, u32[]{:S(2)}, u32[]{:S(2)}) %collective-permute-start.3) | collective-permute-done | bytes 131104 | tf_op jit(solution)/shard_map/while/body/eval_jaxpr/ppermute | solution.py:21
  98.8 4.2 %collective-permute-start = (bf16[64,1024]{1,0:T(8,128)(2,1)S(1)}, bf16[64,1024]{1,0:T(8,128)(2,1)}, u32[]{:S(2)}, u32[]{:S(2)}) collective-permute-start(bf16[64,1024]{1,0:T(8,128)(2,1)S(1)} %get-tuple-element.396), channel_id=1, source_target_pairs={{127,0},{0,1},{1,2},{2,3},{3,4},{4,5},{5,6},{6,7},{7,8},{8,9},{9,1... | collective-permute-start | bytes 393224 | tf_op jit(solution)/shard_map/while/body/eval_jaxpr/ppermute | solution.py:15
  104.9 5.5 %collective-permute-start.2 = (bf16[64,1024]{1,0:T(8,128)(2,1)S(1)}, bf16[64,1024]{1,0:T(8,128)(2,1)S(1)}, u32[]{:S(2)}, u32[]{:S(2)}) collective-permute-start(bf16[64,1024]{1,0:T(8,128)(2,1)S(1)} %get-tuple-element.400), channel_id=1, source_target_pairs={{2,0},{3,1},{4,2},{5,3},{6,4},{7,5},{8,6},{9,7},{10,8},{11,9},{12,... | collective-permute-start | bytes 393224 | tf_op jit(solution)/shard_map/while/body/eval_jaxpr/ppermute | solution.py:15
  112.7 2.2 %fusion.47 = f32[64,1024]{1,0:T(8,128)S(1)} fusion(bf16[64,1024]{1,0:T(8,128)(2,1)S(1)} %get-tuple-element.395, bf16[1024,1024]{1,0:T(8,128)(2,1)} %get-tuple-element.460), kind=kOutput, calls=%fused_computation.43.clone.1 | convolution fusion | flops 134217728 | bytes 2490368 | tf_op jit(solution)/shard_map/while/body/eval_jaxpr/dot_general | solution.py:71
  119.7 2.9 %select_dynamic-update-slice_fusion.2 = (bf16[128,1024]{1,0:T(8,128)(2,1)}, bf16[64,1024]{1,0:T(8,128)(2,1)S(1)}) fusion(bf16[128,1024]{1,0:T(8,128)(2,1)} %get-tuple-element.433, s32[]{:T(128)S(6)} %select_n.272, pred[]{:T(512)S(6)} %and.19, f32[64,1024]{1,0:T(8,128)S(1)} %fusion.47, bf16[1024,1024]{1,0:T(8,128)(2,1)S(1)} %copy-done, ...), kind=kOutput, calls=%fused_computation.11.clone.1 | convolution fusion | flops 143134720 | bytes 3181568 | tf_op jit(solution)/shard_map/while/body/eval_jaxpr/dot_general | solution.py:79
  123.9 5.3 %collective-permute-done.3 = bf16[64,1024]{1,0:T(8,128)(2,1)S(1)} collective-permute-done((bf16[64,1024]{1,0:T(8,128)(2,1)S(1)}, bf16[64,1024]{1,0:T(8,128)(2,1)S(1)}, u32[]{:S(2)}, u32[]{:S(2)}) %collective-permute-start.3) | collective-permute-done | bytes 131104 | tf_op jit(solution)/shard_map/while/body/eval_jaxpr/ppermute | solution.py:21
  133.1 4.2 %collective-permute-start = (bf16[64,1024]{1,0:T(8,128)(2,1)S(1)}, bf16[64,1024]{1,0:T(8,128)(2,1)}, u32[]{:S(2)}, u32[]{:S(2)}) collective-permute-start(bf16[64,1024]{1,0:T(8,128)(2,1)S(1)} %get-tuple-element.396), channel_id=1, source_target_pairs={{127,0},{0,1},{1,2},{2,3},{3,4},{4,5},{5,6},{6,7},{7,8},{8,9},{9,1... | collective-permute-start | bytes 393224 | tf_op jit(solution)/shard_map/while/body/eval_jaxpr/ppermute | solution.py:15
  139.2 5.5 %collective-permute-start.2 = (bf16[64,1024]{1,0:T(8,128)(2,1)S(1)}, bf16[64,1024]{1,0:T(8,128)(2,1)S(1)}, u32[]{:S(2)}, u32[]{:S(2)}) collective-permute-start(bf16[64,1024]{1,0:T(8,128)(2,1)S(1)} %get-tuple-element.400), channel_id=1, source_target_pairs={{2,0},{3,1},{4,2},{5,3},{6,4},{7,5},{8,6},{9,7},{10,8},{11,9},{12,... | collective-permute-start | bytes 393224 | tf_op jit(solution)/shard_map/while/body/eval_jaxpr/ppermute | solution.py:15
  147.1 2.2 %fusion.47 = f32[64,1024]{1,0:T(8,128)S(1)} fusion(bf16[64,1024]{1,0:T(8,128)(2,1)S(1)} %get-tuple-element.395, bf16[1024,1024]{1,0:T(8,128)(2,1)} %get-tuple-element.460), kind=kOutput, calls=%fused_computation.43.clone.1 | convolution fusion | flops 134217728 | bytes 2490368 | tf_op jit(solution)/shard_map/while/body/eval_jaxpr/dot_general | solution.py:71
  154.0 2.9 %select_dynamic-update-slice_fusion.2 = (bf16[128,1024]{1,0:T(8,128)(2,1)}, bf16[64,1024]{1,0:T(8,128)(2,1)S(1)}) fusion(bf16[128,1024]{1,0:T(8,128)(2,1)} %get-tuple-element.433, s32[]{:T(128)S(6)} %select_n.272, pred[]{:T(512)S(6)} %and.19, f32[64,1024]{1,0:T(8,128)S(1)} %fusion.47, bf16[1024,1024]{1,0:T(8,128)(2,1)S(1)} %copy-done, ...), kind=kOutput, calls=%fused_computation.11.clone.1 | convolution fusion | flops 143134720 | bytes 3181568 | tf_op jit(solution)/shard_map/while/body/eval_jaxpr/dot_general | solution.py:79
  158.2 5.3 %collective-permute-done.3 = bf16[64,1024]{1,0:T(8,128)(2,1)S(1)} collective-permute-done((bf16[64,1024]{1,0:T(8,128)(2,1)S(1)}, bf16[64,1024]{1,0:T(8,128)(2,1)S(1)}, u32[]{:S(2)}, u32[]{:S(2)}) %collective-permute-start.3) | collective-permute-done | bytes 131104 | tf_op jit(solution)/shard_map/while/body/eval_jaxpr/ppermute | solution.py:21
  167.4 4.2 %collective-permute-start = (bf16[64,1024]{1,0:T(8,128)(2,1)S(1)}, bf16[64,1024]{1,0:T(8,128)(2,1)}, u32[]{:S(2)}, u32[]{:S(2)}) collective-permute-start(bf16[64,1024]{1,0:T(8,128)(2,1)S(1)} %get-tuple-element.396), channel_id=1, source_target_pairs={{127,0},{0,1},{1,2},{2,3},{3,4},{4,5},{5,6},{6,7},{7,8},{8,9},{9,1... | collective-permute-start | bytes 393224 | tf_op jit(solution)/shard_map/while/body/eval_jaxpr/ppermute | solution.py:15
  173.6 5.5 %collective-permute-start.2 = (bf16[64,1024]{1,0:T(8,128)(2,1)S(1)}, bf16[64,1024]{1,0:T(8,128)(2,1)S(1)}, u32[]{:S(2)}, u32[]{:S(2)}) collective-permute-start(bf16[64,1024]{1,0:T(8,128)(2,1)S(1)} %get-tuple-element.400), channel_id=1, source_target_pairs={{2,0},{3,1},{4,2},{5,3},{6,4},{7,5},{8,6},{9,7},{10,8},{11,9},{12,... | collective-permute-start | bytes 393224 | tf_op jit(solution)/shard_map/while/body/eval_jaxpr/ppermute | solution.py:15
  181.4 2.2 %fusion.47 = f32[64,1024]{1,0:T(8,128)S(1)} fusion(bf16[64,1024]{1,0:T(8,128)(2,1)S(1)} %get-tuple-element.395, bf16[1024,1024]{1,0:T(8,128)(2,1)} %get-tuple-element.460), kind=kOutput, calls=%fused_computation.43.clone.1 | convolution fusion | flops 134217728 | bytes 2490368 | tf_op jit(solution)/shard_map/while/body/eval_jaxpr/dot_general | solution.py:71
  188.4 2.9 %select_dynamic-update-slice_fusion.2 = (bf16[128,1024]{1,0:T(8,128)(2,1)}, bf16[64,1024]{1,0:T(8,128)(2,1)S(1)}) fusion(bf16[128,1024]{1,0:T(8,128)(2,1)} %get-tuple-element.433, s32[]{:T(128)S(6)} %select_n.272, pred[]{:T(512)S(6)} %and.19, f32[64,1024]{1,0:T(8,128)S(1)} %fusion.47, bf16[1024,1024]{1,0:T(8,128)(2,1)S(1)} %copy-done, ...), kind=kOutput, calls=%fused_computation.11.clone.1 | convolution fusion | flops 143134720 | bytes 3181568 | tf_op jit(solution)/shard_map/while/body/eval_jaxpr/dot_general | solution.py:79
  192.5 5.3 %collective-permute-done.3 = bf16[64,1024]{1,0:T(8,128)(2,1)S(1)} collective-permute-done((bf16[64,1024]{1,0:T(8,128)(2,1)S(1)}, bf16[64,1024]{1,0:T(8,128)(2,1)S(1)}, u32[]{:S(2)}, u32[]{:S(2)}) %collective-permute-start.3) | collective-permute-done | bytes 131104 | tf_op jit(solution)/shard_map/while/body/eval_jaxpr/ppermute | solution.py:21
  (109 shorter events, 61.6 us)
Async XLA Ops:
  2.0 10.5 %collective-permute-start.4 = (s32[2]{0:T(128)S(1)}, s32[2]{0:T(128)S(1)}, u32[]{:S(2)}, u32[]{:S(2)}) collective-permute-start(s32[2]{0:T(128)S(1)} %get-tuple-element.264), channel_id=1, source_target_pairs={{1,0},{2,1},{3,2},{4,3},{5,4},{6,5},{7,6},{8,7},{9,8},{10,9},{11,1... | collective-permute-start | bytes 32 | tf_op jit(solution)/shard_map/ppermute | solution.py:15
  4.5 13.9 %collective-permute-start.5 = (s32[2]{0:T(128)S(1)}, s32[2]{0:T(128)S(1)}, u32[]{:S(2)}, u32[]{:S(2)}) collective-permute-start(s32[2]{0:T(128)S(1)} %get-tuple-element.263), channel_id=1, source_target_pairs={{127,0},{0,1},{1,2},{2,3},{3,4},{4,5},{5,6},{6,7},{7,8},{8,9},{9,1... | collective-permute-start | bytes 32 | tf_op jit(solution)/shard_map/ppermute | solution.py:15
  8.5 16.9 %collective-permute-start.6 = (s32[2]{0:T(128)S(1)}, s32[2]{0:T(128)S(1)}, u32[]{:S(2)}, u32[]{:S(2)}) collective-permute-start(s32[2]{0:T(128)S(1)} %get-tuple-element.262), channel_id=1, source_target_pairs={{126,0},{127,1},{0,2},{1,3},{2,4},{3,5},{4,6},{5,7},{6,8},{7,9},{8... | collective-permute-start | bytes 32 | tf_op jit(solution)/shard_map/ppermute | solution.py:15
  30.0 16.3 %copy-start.1 = (s32[128,256]{1,0:T(8,128)S(1)}, s32[128,256]{1,0:T(8,128)}, u32[]{:S(2)}) copy-start(s32[128,256]{1,0:T(8,128)} %get-tuple-element.461) | copy-start | bytes 393220 | tf_op jit(solution)/shard_map/while
  30.1 18.4 %collective-permute-start = (bf16[64,1024]{1,0:T(8,128)(2,1)S(1)}, bf16[64,1024]{1,0:T(8,128)(2,1)}, u32[]{:S(2)}, u32[]{:S(2)}) collective-permute-start(bf16[64,1024]{1,0:T(8,128)(2,1)S(1)} %get-tuple-element.396), channel_id=1, source_target_pairs={{127,0},{0,1},{1,2},{2,3},{3,4},{4,5},{5,6},{6,7},{7,8},{8,9},{9,1... | collective-permute-start | bytes 393224 | tf_op jit(solution)/shard_map/while/body/eval_jaxpr/ppermute | solution.py:15
  32.0 18.2 %collective-permute-start.1 = (bf16[64,1024]{1,0:T(8,128)(2,1)S(1)}, bf16[64,1024]{1,0:T(8,128)(2,1)S(1)}, u32[]{:S(2)}, u32[]{:S(2)}) collective-permute-start(bf16[64,1024]{1,0:T(8,128)(2,1)S(1)} %get-tuple-element.398), channel_id=1, source_target_pairs={{1,0},{2,1},{3,2},{4,3},{5,4},{6,5},{7,6},{8,7},{9,8},{10,9},{11,1... | collective-permute-start | bytes 393224 | tf_op jit(solution)/shard_map/while/body/eval_jaxpr/ppermute | solution.py:15
  35.2 15.8 %collective-permute-start.2 = (bf16[64,1024]{1,0:T(8,128)(2,1)S(1)}, bf16[64,1024]{1,0:T(8,128)(2,1)S(1)}, u32[]{:S(2)}, u32[]{:S(2)}) collective-permute-start(bf16[64,1024]{1,0:T(8,128)(2,1)S(1)} %get-tuple-element.400), channel_id=1, source_target_pairs={{2,0},{3,1},{4,2},{5,3},{6,4},{7,5},{8,6},{9,7},{10,8},{11,9},{12,... | collective-permute-start | bytes 393224 | tf_op jit(solution)/shard_map/while/body/eval_jaxpr/ppermute | solution.py:15
  53.9 6.6 %collective-permute-start.3 = (bf16[64,1024]{1,0:T(8,128)(2,1)S(1)}, bf16[64,1024]{1,0:T(8,128)(2,1)S(1)}, u32[]{:S(2)}, u32[]{:S(2)}) collective-permute-start(bf16[64,1024]{1,0:T(8,128)(2,1)S(1)} %get-tuple-element.407), channel_id=1, source_target_pairs={{0,128},{128,256},{256,384},{1,129},{129,257},{257,385},{2,130},{1... | collective-permute-start | bytes 393224 | tf_op jit(solution)/shard_map/while/body/eval_jaxpr/ppermute | solution.py:21
  64.3 16.3 %copy-start.1 = (s32[128,256]{1,0:T(8,128)S(1)}, s32[128,256]{1,0:T(8,128)}, u32[]{:S(2)}) copy-start(s32[128,256]{1,0:T(8,128)} %get-tuple-element.461) | copy-start | bytes 393220 | tf_op jit(solution)/shard_map/while
  64.4 18.3 %collective-permute-start = (bf16[64,1024]{1,0:T(8,128)(2,1)S(1)}, bf16[64,1024]{1,0:T(8,128)(2,1)}, u32[]{:S(2)}, u32[]{:S(2)}) collective-permute-start(bf16[64,1024]{1,0:T(8,128)(2,1)S(1)} %get-tuple-element.396), channel_id=1, source_target_pairs={{127,0},{0,1},{1,2},{2,3},{3,4},{4,5},{5,6},{6,7},{7,8},{8,9},{9,1... | collective-permute-start | bytes 393224 | tf_op jit(solution)/shard_map/while/body/eval_jaxpr/ppermute | solution.py:15
  68.7 15.9 %collective-permute-start.1 = (bf16[64,1024]{1,0:T(8,128)(2,1)S(1)}, bf16[64,1024]{1,0:T(8,128)(2,1)S(1)}, u32[]{:S(2)}, u32[]{:S(2)}) collective-permute-start(bf16[64,1024]{1,0:T(8,128)(2,1)S(1)} %get-tuple-element.398), channel_id=1, source_target_pairs={{1,0},{2,1},{3,2},{4,3},{5,4},{6,5},{7,6},{8,7},{9,8},{10,9},{11,1... | collective-permute-start | bytes 393224 | tf_op jit(solution)/shard_map/while/body/eval_jaxpr/ppermute | solution.py:15
  70.6 14.8 %collective-permute-start.2 = (bf16[64,1024]{1,0:T(8,128)(2,1)S(1)}, bf16[64,1024]{1,0:T(8,128)(2,1)S(1)}, u32[]{:S(2)}, u32[]{:S(2)}) collective-permute-start(bf16[64,1024]{1,0:T(8,128)(2,1)S(1)} %get-tuple-element.400), channel_id=1, source_target_pairs={{2,0},{3,1},{4,2},{5,3},{6,4},{7,5},{8,6},{9,7},{10,8},{11,9},{12,... | collective-permute-start | bytes 393224 | tf_op jit(solution)/shard_map/while/body/eval_jaxpr/ppermute | solution.py:15
  78.4 7.0 %copy-start = (bf16[1024,1024]{1,0:T(8,128)(2,1)S(1)}, bf16[1024,1024]{1,0:T(8,128)(2,1)}, u32[]{:S(2)}) copy-start(bf16[1024,1024]{1,0:T(8,128)(2,1)} %get-tuple-element.466) | copy-start | bytes 6291460 | tf_op jit(solution)/shard_map/while
  88.2 6.6 %collective-permute-start.3 = (bf16[64,1024]{1,0:T(8,128)(2,1)S(1)}, bf16[64,1024]{1,0:T(8,128)(2,1)S(1)}, u32[]{:S(2)}, u32[]{:S(2)}) collective-permute-start(bf16[64,1024]{1,0:T(8,128)(2,1)S(1)} %get-tuple-element.407), channel_id=1, source_target_pairs={{0,128},{128,256},{256,384},{1,129},{129,257},{257,385},{2,130},{1... | collective-permute-start | bytes 393224 | tf_op jit(solution)/shard_map/while/body/eval_jaxpr/ppermute | solution.py:21
  98.7 16.3 %copy-start.1 = (s32[128,256]{1,0:T(8,128)S(1)}, s32[128,256]{1,0:T(8,128)}, u32[]{:S(2)}) copy-start(s32[128,256]{1,0:T(8,128)} %get-tuple-element.461) | copy-start | bytes 393220 | tf_op jit(solution)/shard_map/while
  98.8 18.3 %collective-permute-start = (bf16[64,1024]{1,0:T(8,128)(2,1)S(1)}, bf16[64,1024]{1,0:T(8,128)(2,1)}, u32[]{:S(2)}, u32[]{:S(2)}) collective-permute-start(bf16[64,1024]{1,0:T(8,128)(2,1)S(1)} %get-tuple-element.396), channel_id=1, source_target_pairs={{127,0},{0,1},{1,2},{2,3},{3,4},{4,5},{5,6},{6,7},{7,8},{8,9},{9,1... | collective-permute-start | bytes 393224 | tf_op jit(solution)/shard_map/while/body/eval_jaxpr/ppermute | solution.py:15
  103.0 15.9 %collective-permute-start.1 = (bf16[64,1024]{1,0:T(8,128)(2,1)S(1)}, bf16[64,1024]{1,0:T(8,128)(2,1)S(1)}, u32[]{:S(2)}, u32[]{:S(2)}) collective-permute-start(bf16[64,1024]{1,0:T(8,128)(2,1)S(1)} %get-tuple-element.398), channel_id=1, source_target_pairs={{1,0},{2,1},{3,2},{4,3},{5,4},{6,5},{7,6},{8,7},{9,8},{10,9},{11,1... | collective-permute-start | bytes 393224 | tf_op jit(solution)/shard_map/while/body/eval_jaxpr/ppermute | solution.py:15
  104.9 14.8 %collective-permute-start.2 = (bf16[64,1024]{1,0:T(8,128)(2,1)S(1)}, bf16[64,1024]{1,0:T(8,128)(2,1)S(1)}, u32[]{:S(2)}, u32[]{:S(2)}) collective-permute-start(bf16[64,1024]{1,0:T(8,128)(2,1)S(1)} %get-tuple-element.400), channel_id=1, source_target_pairs={{2,0},{3,1},{4,2},{5,3},{6,4},{7,5},{8,6},{9,7},{10,8},{11,9},{12,... | collective-permute-start | bytes 393224 | tf_op jit(solution)/shard_map/while/body/eval_jaxpr/ppermute | solution.py:15
  112.7 7.0 %copy-start = (bf16[1024,1024]{1,0:T(8,128)(2,1)S(1)}, bf16[1024,1024]{1,0:T(8,128)(2,1)}, u32[]{:S(2)}) copy-start(bf16[1024,1024]{1,0:T(8,128)(2,1)} %get-tuple-element.466) | copy-start | bytes 6291460 | tf_op jit(solution)/shard_map/while
  122.6 6.6 %collective-permute-start.3 = (bf16[64,1024]{1,0:T(8,128)(2,1)S(1)}, bf16[64,1024]{1,0:T(8,128)(2,1)S(1)}, u32[]{:S(2)}, u32[]{:S(2)}) collective-permute-start(bf16[64,1024]{1,0:T(8,128)(2,1)S(1)} %get-tuple-element.407), channel_id=1, source_target_pairs={{0,128},{128,256},{256,384},{1,129},{129,257},{257,385},{2,130},{1... | collective-permute-start | bytes 393224 | tf_op jit(solution)/shard_map/while/body/eval_jaxpr/ppermute | solution.py:21
  133.0 16.3 %copy-start.1 = (s32[128,256]{1,0:T(8,128)S(1)}, s32[128,256]{1,0:T(8,128)}, u32[]{:S(2)}) copy-start(s32[128,256]{1,0:T(8,128)} %get-tuple-element.461) | copy-start | bytes 393220 | tf_op jit(solution)/shard_map/while
  133.1 18.3 %collective-permute-start = (bf16[64,1024]{1,0:T(8,128)(2,1)S(1)}, bf16[64,1024]{1,0:T(8,128)(2,1)}, u32[]{:S(2)}, u32[]{:S(2)}) collective-permute-start(bf16[64,1024]{1,0:T(8,128)(2,1)S(1)} %get-tuple-element.396), channel_id=1, source_target_pairs={{127,0},{0,1},{1,2},{2,3},{3,4},{4,5},{5,6},{6,7},{7,8},{8,9},{9,1... | collective-permute-start | bytes 393224 | tf_op jit(solution)/shard_map/while/body/eval_jaxpr/ppermute | solution.py:15
  137.3 15.9 %collective-permute-start.1 = (bf16[64,1024]{1,0:T(8,128)(2,1)S(1)}, bf16[64,1024]{1,0:T(8,128)(2,1)S(1)}, u32[]{:S(2)}, u32[]{:S(2)}) collective-permute-start(bf16[64,1024]{1,0:T(8,128)(2,1)S(1)} %get-tuple-element.398), channel_id=1, source_target_pairs={{1,0},{2,1},{3,2},{4,3},{5,4},{6,5},{7,6},{8,7},{9,8},{10,9},{11,1... | collective-permute-start | bytes 393224 | tf_op jit(solution)/shard_map/while/body/eval_jaxpr/ppermute | solution.py:15
  139.2 14.8 %collective-permute-start.2 = (bf16[64,1024]{1,0:T(8,128)(2,1)S(1)}, bf16[64,1024]{1,0:T(8,128)(2,1)S(1)}, u32[]{:S(2)}, u32[]{:S(2)}) collective-permute-start(bf16[64,1024]{1,0:T(8,128)(2,1)S(1)} %get-tuple-element.400), channel_id=1, source_target_pairs={{2,0},{3,1},{4,2},{5,3},{6,4},{7,5},{8,6},{9,7},{10,8},{11,9},{12,... | collective-permute-start | bytes 393224 | tf_op jit(solution)/shard_map/while/body/eval_jaxpr/ppermute | solution.py:15
  147.0 7.0 %copy-start = (bf16[1024,1024]{1,0:T(8,128)(2,1)S(1)}, bf16[1024,1024]{1,0:T(8,128)(2,1)}, u32[]{:S(2)}) copy-start(bf16[1024,1024]{1,0:T(8,128)(2,1)} %get-tuple-element.466) | copy-start | bytes 6291460 | tf_op jit(solution)/shard_map/while
  156.9 6.6 %collective-permute-start.3 = (bf16[64,1024]{1,0:T(8,128)(2,1)S(1)}, bf16[64,1024]{1,0:T(8,128)(2,1)S(1)}, u32[]{:S(2)}, u32[]{:S(2)}) collective-permute-start(bf16[64,1024]{1,0:T(8,128)(2,1)S(1)} %get-tuple-element.407), channel_id=1, source_target_pairs={{0,128},{128,256},{256,384},{1,129},{129,257},{257,385},{2,130},{1... | collective-permute-start | bytes 393224 | tf_op jit(solution)/shard_map/while/body/eval_jaxpr/ppermute | solution.py:21
  167.3 16.3 %copy-start.1 = (s32[128,256]{1,0:T(8,128)S(1)}, s32[128,256]{1,0:T(8,128)}, u32[]{:S(2)}) copy-start(s32[128,256]{1,0:T(8,128)} %get-tuple-element.461) | copy-start | bytes 393220 | tf_op jit(solution)/shard_map/while
  167.4 18.3 %collective-permute-start = (bf16[64,1024]{1,0:T(8,128)(2,1)S(1)}, bf16[64,1024]{1,0:T(8,128)(2,1)}, u32[]{:S(2)}, u32[]{:S(2)}) collective-permute-start(bf16[64,1024]{1,0:T(8,128)(2,1)S(1)} %get-tuple-element.396), channel_id=1, source_target_pairs={{127,0},{0,1},{1,2},{2,3},{3,4},{4,5},{5,6},{6,7},{7,8},{8,9},{9,1... | collective-permute-start | bytes 393224 | tf_op jit(solution)/shard_map/while/body/eval_jaxpr/ppermute | solution.py:15
  171.7 15.9 %collective-permute-start.1 = (bf16[64,1024]{1,0:T(8,128)(2,1)S(1)}, bf16[64,1024]{1,0:T(8,128)(2,1)S(1)}, u32[]{:S(2)}, u32[]{:S(2)}) collective-permute-start(bf16[64,1024]{1,0:T(8,128)(2,1)S(1)} %get-tuple-element.398), channel_id=1, source_target_pairs={{1,0},{2,1},{3,2},{4,3},{5,4},{6,5},{7,6},{8,7},{9,8},{10,9},{11,1... | collective-permute-start | bytes 393224 | tf_op jit(solution)/shard_map/while/body/eval_jaxpr/ppermute | solution.py:15
  173.6 14.8 %collective-permute-start.2 = (bf16[64,1024]{1,0:T(8,128)(2,1)S(1)}, bf16[64,1024]{1,0:T(8,128)(2,1)S(1)}, u32[]{:S(2)}, u32[]{:S(2)}) collective-permute-start(bf16[64,1024]{1,0:T(8,128)(2,1)S(1)} %get-tuple-element.400), channel_id=1, source_target_pairs={{2,0},{3,1},{4,2},{5,3},{6,4},{7,5},{8,6},{9,7},{10,8},{11,9},{12,... | collective-permute-start | bytes 393224 | tf_op jit(solution)/shard_map/while/body/eval_jaxpr/ppermute | solution.py:15
  181.4 7.0 %copy-start = (bf16[1024,1024]{1,0:T(8,128)(2,1)S(1)}, bf16[1024,1024]{1,0:T(8,128)(2,1)}, u32[]{:S(2)}) copy-start(bf16[1024,1024]{1,0:T(8,128)(2,1)} %get-tuple-element.466) | copy-start | bytes 6291460 | tf_op jit(solution)/shard_map/while
  191.2 6.6 %collective-permute-start.3 = (bf16[64,1024]{1,0:T(8,128)(2,1)S(1)}, bf16[64,1024]{1,0:T(8,128)(2,1)S(1)}, u32[]{:S(2)}, u32[]{:S(2)}) collective-permute-start(bf16[64,1024]{1,0:T(8,128)(2,1)S(1)} %get-tuple-element.407), channel_id=1, source_target_pairs={{0,128},{128,256},{256,384},{1,129},{129,257},{257,385},{2,130},{1... | collective-permute-start | bytes 393224 | tf_op jit(solution)/shard_map/while/body/eval_jaxpr/ppermute | solution.py:21
  (1 other events, 7.0 us)
where the time goes:
time: 200 us; the launch traced here: 198 us
  starting transfers between devices  75.1 us (38%)
  matrix products  42.8 us (21%)
  waiting for transfers between devices  39.3 us (20%)
  local copies, waits for them, and re-layouts  15.8 us (8%)
  other arithmetic  14.3 us (7%)
  loops' own time  10.5 us (5%)
    ppermute x18, starting transfers between devices, passed_along(): return lax.ppermute(block, axis, route)  68.7 us
    ppermute x5, waiting for transfers between devices, from_behind(): lax.ppermute(value, axis, [(source, source + steps) for source in range(i...  26.4 us
    dot_general x15, matrix products, tile_term(): jnp.dot(tile_mask.astype(jnp.bfloat16), source_rows, preferred_element_ty...  17.4 us
    dot_general x5, matrix products, one_step(): jnp.dot(mean_rows, weight_neigh, preferred_element_type=jnp.float32)  14.4 us
    ppermute x18, waiting for transfers between devices, passed_along(): return lax.ppermute(block, axis, route)  12.9 us
    dot_general x5, matrix products, one_step(): jnp.dot(own_rows, weight_self, preferred_element_type=jnp.float32)  11.1 us
    another operation x1, loops' own time, per_device(): lax.fori_loop(0, slab_count + lax.axis_size('section') - 1, one_step, ini...  10.5 us
    dynamic_slice x15, local copies, waits for them, and re-layouts, chosen(): lax.dynamic_index_in_dim(asked[position], slab_now, 0, keepdims=False)  9.56 us
  transfers between devices with their start and end apart: 23, of which 7 were waited for; matrix products, arithmetic and copies ran while one was open for 23% of the time, Pallas kernels for 0%

commit v1 on v0

v1 whole, which is shorter than its diff:
```python
import functools

import jax
import jax.numpy as jnp
from jax import lax
from jax.experimental import pallas as pl
from jax.experimental.pallas import tpu as pltpu
from jax.sharding import PartitionSpec as P

BLOCK = 64
TILES = 4
VMEM = pl.BlockSpec(memory_space=pltpu.VMEM)
SMEM = pl.BlockSpec(memory_space=pltpu.SMEM)
ANY = pl.BlockSpec(memory_space=pl.ANY)


def params():
    return pltpu.CompilerParams(vmem_limit_bytes=32 * 1024 * 1024)


def mask_kernel(where_ref, picks_ref, edges_ref, mask_ref, degree_ref):
    odd = where_ref[1] == 1
    for slab in range(2):
        rows = pl.ds(slab * BLOCK, BLOCK)
        e = edges_ref[rows, :].astype(jnp.float32)
        tiles = [e[:, t * BLOCK : (t + 1) * BLOCK] for t in range(TILES)]
        pick = [picks_ref[slab, k] for k in range(3)]
        behind, ahead, ahead2 = tiles[1], tiles[2], tiles[3]
        swap = jnp.where(odd, behind, ahead)
        cross = jnp.where(odd, ahead, behind)
        swap_pick = jnp.where(odd, pick[0], pick[1])
        cross_pick = jnp.where(odd, pick[1], pick[0])
        peers = ((swap, swap_pick), (cross, cross_pick), (ahead2, pick[2]))
        columns = [tiles[0]]
        for wanted in range(2):
            for tile, p in peers:
                columns.append(tile * jnp.where(p == wanted, 1.0, 0.0))
        columns.append(jnp.zeros_like(tiles[0]))
        full = jnp.concatenate(columns, axis=1)
        mask_ref[rows, :] = full.astype(jnp.bfloat16)
        degree = 1.0 + jnp.sum(full, axis=1, keepdims=True)
        degree_ref[rows, :] = jnp.broadcast_to(degree, (BLOCK, 128))


def self_kernel(layer, row, where_ref, own_ref, weight_ref, out_ref):
    @pl.when(where_ref[0] == layer)
    def _():
        out_ref[...] = jnp.dot(
            own_ref[pl.ds(row, BLOCK), :], weight_ref[...], preferred_element_type=jnp.float32
        )


def layer_kernel(layer, slab, rows, first, *refs):
    where_ref, mask_ref, degree_ref, self_ref, weight_ref = refs[:5]
    sources = refs[5:12]
    if first:
        made_ref, result_ref, sem = refs[12:]
    else:
        made_ref, result_ref, sem = refs[13:]

    @pl.when(where_ref[0] == layer)
    def _():
        mine = pl.ds(slab * BLOCK, BLOCK)
        gathered = jnp.concatenate(
            [ref[pl.ds(row, BLOCK), :] for ref, row in zip(sources, rows)], axis=0
        )
        summed = jnp.dot(
            mask_ref[mine, : 7 * BLOCK], gathered, preferred_element_type=jnp.float32
        )
        mean_rows = (summed / degree_ref[mine, :1]).astype(jnp.bfloat16)
        hidden = self_ref[...] + jnp.dot(
            mean_rows, weight_ref[...], preferred_element_type=jnp.float32
        )
        made_ref[...] = jnp.maximum(hidden, 0.0).astype(jnp.bfloat16)
        copy = pltpu.make_async_copy(made_ref, result_ref.at[mine, :], sem)
        copy.start()
        copy.wait()


def per_device(stacked, edges, picks, self_w, neigh_w):
    layers, domains = lax.axis_size("section"), lax.axis_size("dom")
    width = stacked.shape[2]
    features = stacked[0]
    weight_self, weight_neigh = self_w[0], neigh_w[0]
    section = lax.axis_index("section")
    domain = lax.axis_index("dom")
    where = jnp.stack([section, domain % 2]).astype(jnp.int32)
    axes = ("section", "dom")
    everyone = range(domains)

    def route(value, jumps, sections, hop):
        pairs = [
            (s * domains + (d + jump) % domains, (s + hop) * domains + d)
            for s in sections
            for d in everyone
            for jump in jumps(d)
        ]
        return lax.ppermute(value, axes, pairs)

    def here(d):
        return (0,)

    def swapped(d):
        return (1,) if d % 2 == 0 else (-1,)

    def crossed(d):
        return (-1,) if d % 2 == 0 else (1,)

    def up2(d):
        return (2,)

    mask, degree = pl.pallas_call(
        mask_kernel,
        out_shape=(
            jax.ShapeDtypeStruct((2 * BLOCK, 8 * BLOCK), jnp.bfloat16),
            jax.ShapeDtypeStruct((2 * BLOCK, 128), jnp.float32),
        ),
        in_specs=[SMEM, SMEM, VMEM],
        out_specs=(VMEM, VMEM),
        compiler_params=params(),
        name="masks",
    )(where, picks, edges)

    def self_part(layer, own, row):
        return pl.pallas_call(
            functools.partial(self_kernel, layer, row),
            out_shape=jax.ShapeDtypeStruct((BLOCK, width), jnp.float32),
            in_specs=[SMEM, VMEM, VMEM],
            out_specs=VMEM,
            compiler_params=params(),
            cost_estimate=pl.CostEstimate(
                flops=2 * BLOCK * width * width, bytes_accessed=2 * width * width, transcendentals=0
            ),
            name="self_part",
        )(where, own, weight_self)

    def layer_part(layer, slab, sources, part, result):
        arrays, rows = zip(*sources)
        first = result is None
        extra = () if first else (result,)
        return pl.pallas_call(
            functools.partial(layer_kernel, layer, slab, rows, first),
            out_shape=(
                jax.ShapeDtypeStruct((BLOCK, width), jnp.bfloat16),
                jax.ShapeDtypeStruct((2 * BLOCK, width), jnp.bfloat16),
            ),
            in_specs=[SMEM] + [VMEM] * 11 + [ANY] * len(extra),
            out_specs=(VMEM, ANY),
            scratch_shapes=[pltpu.SemaphoreType.DMA],
            input_output_aliases={} if first else {12: 1},
            compiler_params=params(),
            cost_estimate=pl.CostEstimate(
                flops=4 * BLOCK * width * width, bytes_accessed=2 * width * width, transcendentals=0
            ),
            name="layer_part",
        )(where, mask, degree, part, weight_neigh, *arrays, *extra)

    staged = [route(features, jumps, range(layers), 0) for jumps in (up2, crossed, swapped)][::-1]
    old = [[(array, slab * BLOCK) for array in staged] for slab in range(2)]
    own = [(features, 0), (features, BLOCK)]
    fresh = old
    result = None
    for layer in range(layers):
        made = []
        incoming = []
        for slab in range(2):
            if layer:
                own_now, peers_now = arriving[slab]
                swap = route(own_now, swapped, [layer], 0)
                own[slab] = (own_now, 0)
                fresh[slab] = [(swap, 0)] + [(array, 0) for array in peers_now]
            part = self_part(layer, *own[slab])
            second = fresh[1] if slab == 1 else old[1]
            produced, result = layer_part(
                layer, slab, [own[slab]] + fresh[0] + second, part, result
            )
            if layer < layers - 1:
                sent = [route(produced, jumps, [layer], 1) for jumps in (here, crossed, up2)]
                incoming.append((sent[0], sent[1:]))
        arriving = incoming
        fresh = [None, None]
    return result[None]


def solution(mesh):
    in_specs = (
        P("section", "dom", None),
        P("dom", None),
        P("dom", None),
        P("section", None, None),
        P("section", None, None),
    )
    out_specs = P("section", "dom", None)
    return jax.shard_map(
        per_device, mesh=mesh, in_specs=in_specs, out_specs=out_specs, check_vma=False
    )
```

time: 200 us -> 102 us (0.51)
  matrix products: 42.8 us -> 0 us
  starting transfers between devices: 75.1 us -> 42.1 us
  Pallas kernels: 0 us -> 14.5 us
  other arithmetic: 14.3 us -> 0.08 us
  local copies, waits for them, and re-layouts: 15.8 us -> 4.49 us
  loops' own time: 10.5 us -> 0 us
    dot_general x25 -> x0, matrix products: 42.8 us -> none  [the longest x15 17.4 us: tile_term(): jnp.dot(tile_mask.astype(jnp.bfloat16), source_rows, preferred_element_ty...]
    ppermute x23 -> x27, starting transfers between devices: 75.1 us -> 42.1 us  [route(): return lax.ppermute(value, axes, pairs)]
    pallas_call x0 -> x17, Pallas kernels: none -> 14.5 us  [the longest x8 8.39 us: layer_part(): pl.pallas_call(functools.partial(layer_kernel, layer, slab, rows, first),...]
    another operation x1 -> x0, loops' own time: 10.5 us -> none  [per_device(): lax.fori_loop(0, slab_count + lax.axis_size('section') - 1, one_step, ini...]
    dynamic_slice x20 -> x0, local copies, waits for them, and re-layouts: 9.75 us -> none  [the longest x15 9.56 us: chosen(): lax.dynamic_index_in_dim(asked[position], slab_now, 0, keepdims=False)]
    add x5 -> x0, other arithmetic: 9.45 us -> none  [one_step(): degree = degree + jnp.where(live_row[position], counted, 0.0)]
    slice x6 -> x0, local copies, waits for them, and re-layouts: 4.27 us -> none  [the longest x5 3.27 us: one_step(): summed = summed + jnp.where(live_row[position], term, 0.0)]
    unnamed x1 -> x12, local copies, waits for them, and re-layouts: 0.95 us -> 4.49 us
  transfers between devices with their start and end apart: 23 -> 27, of which waited for: 7 -> 4; matrix products, arithmetic and copies ran while one was open for 23% -> 0% of each run, Pallas kernels for 0% -> 11%
where the time goes in v1:
time: 102 us; the launch traced here: 100 us
  starting transfers between devices  42.1 us (41%)
  waiting for transfers between devices  38.3 us (38%)
  Pallas kernels  14.5 us (14%)
  local copies, waits for them, and re-layouts  4.49 us (4%)
    ppermute x27, starting transfers between devices, route(): return lax.ppermute(value, axes, pairs)  42.1 us
    ppermute x27, waiting for transfers between devices, route(): return lax.ppermute(value, axes, pairs)  38.3 us
    pallas_call x8, Pallas kernels, layer_part(): pl.pallas_call(functools.partial(layer_kernel, layer, slab, rows, first),...  8.39 us
    pallas_call x8, Pallas kernels, self_part(): pl.pallas_call(functools.partial(self_kernel, layer, row), out_shape=jax....  5.33 us
    unnamed x12, local copies, waits for them, and re-layouts  4.49 us
  transfers between devices with their start and end apart: 27, of which 4 were waited for; matrix products, arithmetic and copies ran while one was open for 0% of the time, Pallas kernels for 11%

profile of v1, /device:TPU:7, one launch (start us, length us, event | category | flops | bytes accessed | tf_op | source)
XLA Modules:
  0.0 100.1 jit_solution(7129203470465616830)
XLA Ops:
  0.0 2.6 %collective-permute-start = (bf16[128,1024]{1,0:T(8,128)(2,1)}, bf16[128,1024]{1,0:T(8,128)(2,1)S(1)}, u32[]{:S(2)}, u32[]{:S(2)}) collective-permute-start(bf16[128,1024]{1,0:T(8,128)(2,1)} %bitcast.22), channel_id=1, source_target_pairs={{1,0},{0,1},{3,2},{2,3},{5,4},{4,5},{7,6},{6,7},{9,8},{8,9},{11,10... | collective-permute-start | bytes 786440 | tf_op jit(solution)/shard_map/ppermute | solution.py:98
  2.6 3.9 %collective-permute-start.1 = (bf16[128,1024]{1,0:T(8,128)(2,1)}, bf16[128,1024]{1,0:T(8,128)(2,1)S(1)}, u32[]{:S(2)}, u32[]{:S(2)}) collective-permute-start(bf16[128,1024]{1,0:T(8,128)(2,1)} %bitcast.23), channel_id=1, source_target_pairs={{127,0},{2,1},{1,2},{4,3},{3,4},{6,5},{5,6},{8,7},{7,8},{10,9},{9,... | collective-permute-start | bytes 786440 | tf_op jit(solution)/shard_map/ppermute | solution.py:98
  6.5 11.6 %collective-permute-start.2 = (bf16[128,1024]{1,0:T(8,128)(2,1)}, bf16[128,1024]{1,0:T(8,128)(2,1)S(1)}, u32[]{:S(2)}, u32[]{:S(2)}) collective-permute-start(bf16[128,1024]{1,0:T(8,128)(2,1)} %bitcast.24), channel_id=1, source_target_pairs={{2,0},{3,1},{4,2},{5,3},{6,4},{7,5},{8,6},{9,7},{10,8},{11,9},{12,... | collective-permute-start | bytes 786440 | tf_op jit(solution)/shard_map/ppermute | solution.py:98
  18.2 0.9 copy-done.4
  19.1 0.7 copy-done.5
  19.8 0.8 masks.1
  20.6 1.6 %copy-done = bf16[1,1024,1024]{2,1,0:T(8,128)(2,1)S(1)} copy-done((bf16[1,1024,1024]{2,1,0:T(8,128)(2,1)S(1)}, bf16[1,1024,1024]{2,1,0:T(8,128)(2,1)}, u32[]{:S(2)}) %copy-start) | copy-done | bytes 2097176
  22.2 0.9 copy-done.3
  23.7 0.9 collective-permute-done.2.refs_8_.refs_11_
  25.3 0.8 collective-permute-start.4
  27.4 0.7 collective-permute-start.3
  28.1 0.7 collective-permute-start.6
  28.8 0.7 collective-permute-start.7
  29.5 0.7 collective-permute-start.5
  30.2 0.7 collective-permute-start.9
  30.8 0.7 collective-permute-start.10
  33.9 0.7 collective-permute-start.12
  36.5 0.7 collective-permute-start.15
  38.6 0.7 collective-permute-start.18
  41.7 1.3 %collective-permute-start.20 = (bf16[64,1024]{1,0:T(8,128)(2,1)S(1)}, bf16[64,1024]{1,0:T(8,128)(2,1)S(1)}, u32[]{:S(2)}, u32[]{:S(2)}) collective-permute-start(bf16[64,1024]{1,0:T(8,128)(2,1)S(1)} %get-tuple-element.33), channel_id=1, source_target_pairs={{256,384},{257,385},{258,386},{259,387},{260,388},{261,389},{262,3... | collective-permute-start | bytes 393224 | tf_op jit(solution)/shard_map/ppermute | solution.py:98
  43.6 1.3 %collective-permute-start.19 = (bf16[64,1024]{1,0:T(8,128)(2,1)S(1)}, bf16[64,1024]{1,0:T(8,128)(2,1)S(1)}, u32[]{:S(2)}, u32[]{:S(2)}) collective-permute-start(bf16[64,1024]{1,0:T(8,128)(2,1)S(1)} %get-tuple-element.32), channel_id=1, source_target_pairs={{256,384},{257,385},{258,386},{259,387},{260,388},{261,389},{262,3... | collective-permute-start | bytes 393224 | tf_op jit(solution)/shard_map/ppermute | solution.py:98
  44.9 1.3 %collective-permute-start.22 = (bf16[64,1024]{1,0:T(8,128)(2,1)S(1)}, bf16[64,1024]{1,0:T(8,128)(2,1)S(1)}, u32[]{:S(2)}, u32[]{:S(2)}) collective-permute-start(bf16[64,1024]{1,0:T(8,128)(2,1)S(1)} %get-tuple-element.33), channel_id=1, source_target_pairs={{383,384},{258,385},{257,386},{260,387},{259,388},{262,389},{261,3... | collective-permute-start | bytes 393224 | tf_op jit(solution)/shard_map/ppermute | solution.py:98
  46.2 1.3 %collective-permute-start.23 = (bf16[64,1024]{1,0:T(8,128)(2,1)S(1)}, bf16[64,1024]{1,0:T(8,128)(2,1)S(1)}, u32[]{:S(2)}, u32[]{:S(2)}) collective-permute-start(bf16[64,1024]{1,0:T(8,128)(2,1)S(1)} %get-tuple-element.33), channel_id=1, source_target_pairs={{258,384},{259,385},{260,386},{261,387},{262,388},{263,389},{264,3... | collective-permute-start | bytes 393224 | tf_op jit(solution)/shard_map/ppermute | solution.py:98
  47.5 37.0 %collective-permute-done.20.own_ref.refs_5_ = bf16[64,1024]{1,0:T(8,128)(2,1)S(1)} collective-permute-done((bf16[64,1024]{1,0:T(8,128)(2,1)S(1)}, bf16[64,1024]{1,0:T(8,128)(2,1)S(1)}, u32[]{:S(2)}, u32[]{:S(2)}) %collective-permute-start.20) | collective-permute-done | bytes 131104 | tf_op jit(solution)/shard_map/ppermute | solution.py:98
  84.5 2.8 %collective-permute-start.21 = (bf16[64,1024]{1,0:T(8,128)(2,1)S(1)}, bf16[64,1024]{1,0:T(8,128)(2,1)S(1)}, u32[]{:S(2)}, u32[]{:S(2)}) collective-permute-start(bf16[64,1024]{1,0:T(8,128)(2,1)S(1)} %collective-permute-done.20.own_ref.refs_5_), channel_id=1, source_target_pairs={{385,384},{384,385},{387,386},{386,387},{389,388},{388,389},{391,3... | collective-permute-start | bytes 393224 | tf_op jit(solution)/shard_map/ppermute | solution.py:98
  87.3 1.3 %collective-permute-start.25 = (bf16[64,1024]{1,0:T(8,128)(2,1)S(1)}, bf16[64,1024]{1,0:T(8,128)(2,1)S(1)}, u32[]{:S(2)}, u32[]{:S(2)}) collective-permute-start(bf16[64,1024]{1,0:T(8,128)(2,1)S(1)} %get-tuple-element.32), channel_id=1, source_target_pairs={{383,384},{258,385},{257,386},{260,387},{259,388},{262,389},{261,3... | collective-permute-start | bytes 393224 | tf_op jit(solution)/shard_map/ppermute | solution.py:98
  88.7 1.3 %collective-permute-start.26 = (bf16[64,1024]{1,0:T(8,128)(2,1)S(1)}, bf16[64,1024]{1,0:T(8,128)(2,1)S(1)}, u32[]{:S(2)}, u32[]{:S(2)}) collective-permute-start(bf16[64,1024]{1,0:T(8,128)(2,1)S(1)} %get-tuple-element.32), channel_id=1, source_target_pairs={{258,384},{259,385},{260,386},{261,387},{262,388},{263,389},{264,3... | collective-permute-start | bytes 393224 | tf_op jit(solution)/shard_map/ppermute | solution.py:98
  90.0 2.6 %collective-permute-start.24 = (bf16[64,1024]{1,0:T(8,128)(2,1)S(1)}, bf16[64,1024]{1,0:T(8,128)(2,1)S(1)}, u32[]{:S(2)}, u32[]{:S(2)}) collective-permute-start(bf16[64,1024]{1,0:T(8,128)(2,1)S(1)} %collective-permute-done.19.own_ref.refs_5_), channel_id=1, source_target_pairs={{385,384},{384,385},{387,386},{386,387},{389,388},{388,389},{391,3... | collective-permute-start | bytes 393224 | tf_op jit(solution)/shard_map/ppermute | solution.py:98
  92.6 1.0 %self_part.14.refs_3_ = f32[64,1024]{1,0:T(8,128)S(1)} custom-call(s32[2]{0:T(128)S(1)} %pad_add_fusion.where_ref.refs_0_, bf16[64,1024]{1,0:T(8,128)(2,1)S(1)} %collective-permute-done.19.own_ref.refs_5_, bf16[1024,1024]{1,0:T(8,128)(2,1)S(1)} %bitcast.12), custom_call_target="tpu_custom_call" | custom-call | flops 134217728 | bytes 2097152 | tf_op jit(solution)/shard_map/self_part/pallas_call | solution.py:125
  93.6 1.0 %self_part.15.refs_3_ = f32[64,1024]{1,0:T(8,128)S(1)} custom-call(s32[2]{0:T(128)S(1)} %pad_add_fusion.where_ref.refs_0_, bf16[64,1024]{1,0:T(8,128)(2,1)S(1)} %collective-permute-done.20.own_ref.refs_5_, bf16[1024,1024]{1,0:T(8,128)(2,1)S(1)} %bitcast.13), custom_call_target="tpu_custom_call" | custom-call | flops 134217728 | bytes 2097152 | tf_op jit(solution)/shard_map/self_part/pallas_call | solution.py:125
  94.6 2.5 %layer_part.14 = (bf16[64,1024]{1,0:T(8,128)(2,1)}, bf16[128,1024]{1,0:T(8,128)(2,1)}) custom-call(s32[2]{0:T(128)S(1)} %pad_add_fusion.where_ref.refs_0_, bf16[128,512]{1,0:T(8,128)(2,1)S(1)} %get-tuple-element.21.refs_1_, f32[128,128]{1,0:T(8,128)S(1)} %get-tuple-element.22.refs_2_, ...), custom_call_target="tpu_custom_call", output_to_operand_aliasing={{1}: (12, {})} | custom-call | flops 268435456 | bytes 2097152 | tf_op jit(solution)/shard_map/layer_part/pallas_call | solution.py:141
  97.6 2.5 %layer_part.15 = (bf16[64,1024]{1,0:T(8,128)(2,1)}, bf16[128,1024]{1,0:T(8,128)(2,1)}) custom-call(s32[2]{0:T(128)S(1)} %pad_add_fusion.where_ref.refs_0_, bf16[128,512]{1,0:T(8,128)(2,1)S(1)} %get-tuple-element.21.refs_1_, f32[128,128]{1,0:T(8,128)S(1)} %get-tuple-element.22.refs_2_, ...), custom_call_target="tpu_custom_call", output_to_operand_aliasing={{1}: (12, {})} | custom-call | flops 268435456 | bytes 2097152 | tf_op jit(solution)/shard_map/layer_part/pallas_call | solution.py:141
  (52 shorter events, 11.6 us)
Async XLA Ops:
  0.0 23.7 %collective-permute-start = (bf16[128,1024]{1,0:T(8,128)(2,1)}, bf16[128,1024]{1,0:T(8,128)(2,1)S(1)}, u32[]{:S(2)}, u32[]{:S(2)}) collective-permute-start(bf16[128,1024]{1,0:T(8,128)(2,1)} %bitcast.22), channel_id=1, source_target_pairs={{1,0},{0,1},{3,2},{2,3},{5,4},{4,5},{7,6},{6,7},{9,8},{8,9},{11,10... | collective-permute-start | bytes 786440 | tf_op jit(solution)/shard_map/ppermute | solution.py:98
  2.6 21.1 %collective-permute-start.1 = (bf16[128,1024]{1,0:T(8,128)(2,1)}, bf16[128,1024]{1,0:T(8,128)(2,1)S(1)}, u32[]{:S(2)}, u32[]{:S(2)}) collective-permute-start(bf16[128,1024]{1,0:T(8,128)(2,1)} %bitcast.23), channel_id=1, source_target_pairs={{127,0},{2,1},{1,2},{4,3},{3,4},{6,5},{5,6},{8,7},{7,8},{10,9},{9,... | collective-permute-start | bytes 786440 | tf_op jit(solution)/shard_map/ppermute | solution.py:98
  6.5 18.1 %collective-permute-start.2 = (bf16[128,1024]{1,0:T(8,128)(2,1)}, bf16[128,1024]{1,0:T(8,128)(2,1)S(1)}, u32[]{:S(2)}, u32[]{:S(2)}) collective-permute-start(bf16[128,1024]{1,0:T(8,128)(2,1)} %bitcast.24), channel_id=1, source_target_pairs={{2,0},{3,1},{4,2},{5,3},{6,4},{7,5},{8,6},{9,7},{10,8},{11,9},{12,... | collective-permute-start | bytes 786440 | tf_op jit(solution)/shard_map/ppermute | solution.py:98
  18.2 0.9 copy-start.4
  20.6 1.6 %copy-start = (bf16[1,1024,1024]{2,1,0:T(8,128)(2,1)S(1)}, bf16[1,1024,1024]{2,1,0:T(8,128)(2,1)}, u32[]{:S(2)}) copy-start(bf16[1,1024,1024]{2,1,0:T(8,128)(2,1)} %param.8) | copy-start | bytes 6291460
  22.2 0.9 copy-start.3
  23.1 1.6 %copy-start.2 = (bf16[1,1024,1024]{2,1,0:T(8,128)(2,1)S(1)}, bf16[1,1024,1024]{2,1,0:T(8,128)(2,1)}, u32[]{:S(2)}) copy-start(bf16[1,1024,1024]{2,1,0:T(8,128)(2,1)} %param.9) | copy-start | bytes 6291460
  24.7 1.6 %copy-start.1 = (bf16[1,1024,1024]{2,1,0:T(8,128)(2,1)S(1)}, bf16[1,1024,1024]{2,1,0:T(8,128)(2,1)}, u32[]{:S(2)}) copy-start(bf16[1,1024,1024]{2,1,0:T(8,128)(2,1)} %param.8) | copy-start | bytes 6291460
  25.3 4.2 %collective-permute-start.4 = (bf16[64,1024]{1,0:T(8,128)(2,1)S(1)}, bf16[64,1024]{1,0:T(8,128)(2,1)S(1)}, u32[]{:S(2)}, u32[]{:S(2)}) collective-permute-start(bf16[64,1024]{1,0:T(8,128)(2,1)S(1)} %get-tuple-element.25), channel_id=1, source_target_pairs={{0,128},{1,129},{2,130},{3,131},{4,132},{5,133},{6,134},{7,135},{8... | collective-permute-start | bytes 393224 | tf_op jit(solution)/shard_map/ppermute | solution.py:98
  27.4 3.4 %collective-permute-start.3 = (bf16[64,1024]{1,0:T(8,128)(2,1)S(1)}, bf16[64,1024]{1,0:T(8,128)(2,1)S(1)}, u32[]{:S(2)}, u32[]{:S(2)}) collective-permute-start(bf16[64,1024]{1,0:T(8,128)(2,1)S(1)} %get-tuple-element.24), channel_id=1, source_target_pairs={{0,128},{1,129},{2,130},{3,131},{4,132},{5,133},{6,134},{7,135},{8... | collective-permute-start | bytes 393224 | tf_op jit(solution)/shard_map/ppermute | solution.py:98
  28.1 3.4 %collective-permute-start.6 = (bf16[64,1024]{1,0:T(8,128)(2,1)S(1)}, bf16[64,1024]{1,0:T(8,128)(2,1)S(1)}, u32[]{:S(2)}, u32[]{:S(2)}) collective-permute-start(bf16[64,1024]{1,0:T(8,128)(2,1)S(1)} %get-tuple-element.25), channel_id=1, source_target_pairs={{127,128},{2,129},{1,130},{4,131},{3,132},{6,133},{5,134},{8,135},... | collective-permute-start | bytes 393224 | tf_op jit(solution)/shard_map/ppermute | solution.py:98
  28.8 4.5 %collective-permute-start.7 = (bf16[64,1024]{1,0:T(8,128)(2,1)S(1)}, bf16[64,1024]{1,0:T(8,128)(2,1)S(1)}, u32[]{:S(2)}, u32[]{:S(2)}) collective-permute-start(bf16[64,1024]{1,0:T(8,128)(2,1)S(1)} %get-tuple-element.25), channel_id=1, source_target_pairs={{2,128},{3,129},{4,130},{5,131},{6,132},{7,133},{8,134},{9,135},{1... | collective-permute-start | bytes 393224 | tf_op jit(solution)/shard_map/ppermute | solution.py:98
  29.5 3.9 %collective-permute-start.5 = (bf16[64,1024]{1,0:T(8,128)(2,1)S(1)}, bf16[64,1024]{1,0:T(8,128)(2,1)S(1)}, u32[]{:S(2)}, u32[]{:S(2)}) collective-permute-start(bf16[64,1024]{1,0:T(8,128)(2,1)S(1)} %collective-permute-done.4.own_ref.refs_5_), channel_id=1, source_target_pairs={{129,128},{128,129},{131,130},{130,131},{133,132},{132,133},{135,1... | collective-permute-start | bytes 393224 | tf_op jit(solution)/shard_map/ppermute | solution.py:98
  30.2 4.4 %collective-permute-start.9 = (bf16[64,1024]{1,0:T(8,128)(2,1)S(1)}, bf16[64,1024]{1,0:T(8,128)(2,1)S(1)}, u32[]{:S(2)}, u32[]{:S(2)}) collective-permute-start(bf16[64,1024]{1,0:T(8,128)(2,1)S(1)} %get-tuple-element.24), channel_id=1, source_target_pairs={{127,128},{2,129},{1,130},{4,131},{3,132},{6,133},{5,134},{8,135},... | collective-permute-start | bytes 393224 | tf_op jit(solution)/shard_map/ppermute | solution.py:98
  30.8 3.8 %collective-permute-start.10 = (bf16[64,1024]{1,0:T(8,128)(2,1)S(1)}, bf16[64,1024]{1,0:T(8,128)(2,1)S(1)}, u32[]{:S(2)}, u32[]{:S(2)}) collective-permute-start(bf16[64,1024]{1,0:T(8,128)(2,1)S(1)} %get-tuple-element.24), channel_id=1, source_target_pairs={{2,128},{3,129},{4,130},{5,131},{6,132},{7,133},{8,134},{9,135},{1... | collective-permute-start | bytes 393224 | tf_op jit(solution)/shard_map/ppermute | solution.py:98
  31.5 3.1 %collective-permute-start.8 = (bf16[64,1024]{1,0:T(8,128)(2,1)S(1)}, bf16[64,1024]{1,0:T(8,128)(2,1)S(1)}, u32[]{:S(2)}, u32[]{:S(2)}) collective-permute-start(bf16[64,1024]{1,0:T(8,128)(2,1)S(1)} %collective-permute-done.3.own_ref.refs_5_), channel_id=1, source_target_pairs={{129,128},{128,129},{131,130},{130,131},{133,132},{132,133},{135,1... | collective-permute-start | bytes 393224 | tf_op jit(solution)/shard_map/ppermute | solution.py:98
  33.9 3.3 %collective-permute-start.12 = (bf16[64,1024]{1,0:T(8,128)(2,1)S(1)}, bf16[64,1024]{1,0:T(8,128)(2,1)S(1)}, u32[]{:S(2)}, u32[]{:S(2)}) collective-permute-start(bf16[64,1024]{1,0:T(8,128)(2,1)S(1)} %get-tuple-element.29), channel_id=1, source_target_pairs={{128,256},{129,257},{130,258},{131,259},{132,260},{133,261},{134,2... | collective-permute-start | bytes 393224 | tf_op jit(solution)/shard_map/ppermute | solution.py:98
  35.2 3.4 %collective-permute-start.11 = (bf16[64,1024]{1,0:T(8,128)(2,1)S(1)}, bf16[64,1024]{1,0:T(8,128)(2,1)S(1)}, u32[]{:S(2)}, u32[]{:S(2)}) collective-permute-start(bf16[64,1024]{1,0:T(8,128)(2,1)S(1)} %get-tuple-element.28), channel_id=1, source_target_pairs={{128,256},{129,257},{130,258},{131,259},{132,260},{133,261},{134,2... | collective-permute-start | bytes 393224 | tf_op jit(solution)/shard_map/ppermute | solution.py:98
  35.9 3.4 %collective-permute-start.14 = (bf16[64,1024]{1,0:T(8,128)(2,1)S(1)}, bf16[64,1024]{1,0:T(8,128)(2,1)S(1)}, u32[]{:S(2)}, u32[]{:S(2)}) collective-permute-start(bf16[64,1024]{1,0:T(8,128)(2,1)S(1)} %get-tuple-element.29), channel_id=1, source_target_pairs={{255,256},{130,257},{129,258},{132,259},{131,260},{134,261},{133,2... | collective-permute-start | bytes 393224 | tf_op jit(solution)/shard_map/ppermute | solution.py:98
  36.5 4.5 %collective-permute-start.15 = (bf16[64,1024]{1,0:T(8,128)(2,1)S(1)}, bf16[64,1024]{1,0:T(8,128)(2,1)S(1)}, u32[]{:S(2)}, u32[]{:S(2)}) collective-permute-start(bf16[64,1024]{1,0:T(8,128)(2,1)S(1)} %get-tuple-element.29), channel_id=1, source_target_pairs={{130,256},{131,257},{132,258},{133,259},{134,260},{135,261},{136,2... | collective-permute-start | bytes 393224 | tf_op jit(solution)/shard_map/ppermute | solution.py:98
  37.2 3.9 %collective-permute-start.13 = (bf16[64,1024]{1,0:T(8,128)(2,1)S(1)}, bf16[64,1024]{1,0:T(8,128)(2,1)S(1)}, u32[]{:S(2)}, u32[]{:S(2)}) collective-permute-start(bf16[64,1024]{1,0:T(8,128)(2,1)S(1)} %collective-permute-done.12.own_ref.refs_5_), channel_id=1, source_target_pairs={{257,256},{256,257},{259,258},{258,259},{261,260},{260,261},{263,2... | collective-permute-start | bytes 393224 | tf_op jit(solution)/shard_map/ppermute | solution.py:98
  37.9 5.1 %collective-permute-start.17 = (bf16[64,1024]{1,0:T(8,128)(2,1)S(1)}, bf16[64,1024]{1,0:T(8,128)(2,1)S(1)}, u32[]{:S(2)}, u32[]{:S(2)}) collective-permute-start(bf16[64,1024]{1,0:T(8,128)(2,1)S(1)} %get-tuple-element.28), channel_id=1, source_target_pairs={{255,256},{130,257},{129,258},{132,259},{131,260},{134,261},{133,2... | collective-permute-start | bytes 393224 | tf_op jit(solution)/shard_map/ppermute | solution.py:98
  38.6 4.4 %collective-permute-start.18 = (bf16[64,1024]{1,0:T(8,128)(2,1)S(1)}, bf16[64,1024]{1,0:T(8,128)(2,1)S(1)}, u32[]{:S(2)}, u32[]{:S(2)}) collective-permute-start(bf16[64,1024]{1,0:T(8,128)(2,1)S(1)} %get-tuple-element.28), channel_id=1, source_target_pairs={{130,256},{131,257},{132,258},{133,259},{134,260},{135,261},{136,2... | collective-permute-start | bytes 393224 | tf_op jit(solution)/shard_map/ppermute | solution.py:98
  39.3 3.7 %collective-permute-start.16 = (bf16[64,1024]{1,0:T(8,128)(2,1)S(1)}, bf16[64,1024]{1,0:T(8,128)(2,1)S(1)}, u32[]{:S(2)}, u32[]{:S(2)}) collective-permute-start(bf16[64,1024]{1,0:T(8,128)(2,1)S(1)} %collective-permute-done.11.own_ref.refs_5_), channel_id=1, source_target_pairs={{257,256},{256,257},{259,258},{258,259},{261,260},{260,261},{263,2... | collective-permute-start | bytes 393224 | tf_op jit(solution)/shard_map/ppermute | solution.py:98
  41.7 42.8 %collective-permute-start.20 = (bf16[64,1024]{1,0:T(8,128)(2,1)S(1)}, bf16[64,1024]{1,0:T(8,128)(2,1)S(1)}, u32[]{:S(2)}, u32[]{:S(2)}) collective-permute-start(bf16[64,1024]{1,0:T(8,128)(2,1)S(1)} %get-tuple-element.33), channel_id=1, source_target_pairs={{256,384},{257,385},{258,386},{259,387},{260,388},{261,389},{262,3... | collective-permute-start | bytes 393224 | tf_op jit(solution)/shard_map/ppermute | solution.py:98
  43.6 45.1 %collective-permute-start.19 = (bf16[64,1024]{1,0:T(8,128)(2,1)S(1)}, bf16[64,1024]{1,0:T(8,128)(2,1)S(1)}, u32[]{:S(2)}, u32[]{:S(2)}) collective-permute-start(bf16[64,1024]{1,0:T(8,128)(2,1)S(1)} %get-tuple-element.32), channel_id=1, source_target_pairs={{256,384},{257,385},{258,386},{259,387},{260,388},{261,389},{262,3... | collective-permute-start | bytes 393224 | tf_op jit(solution)/shard_map/ppermute | solution.py:98
  44.9 45.1 %collective-permute-start.22 = (bf16[64,1024]{1,0:T(8,128)(2,1)S(1)}, bf16[64,1024]{1,0:T(8,128)(2,1)S(1)}, u32[]{:S(2)}, u32[]{:S(2)}) collective-permute-start(bf16[64,1024]{1,0:T(8,128)(2,1)S(1)} %get-tuple-element.33), channel_id=1, source_target_pairs={{383,384},{258,385},{257,386},{260,387},{259,388},{262,389},{261,3... | collective-permute-start | bytes 393224 | tf_op jit(solution)/shard_map/ppermute | solution.py:98
  46.2 48.4 %collective-permute-start.23 = (bf16[64,1024]{1,0:T(8,128)(2,1)S(1)}, bf16[64,1024]{1,0:T(8,128)(2,1)S(1)}, u32[]{:S(2)}, u32[]{:S(2)}) collective-permute-start(bf16[64,1024]{1,0:T(8,128)(2,1)S(1)} %get-tuple-element.33), channel_id=1, source_target_pairs={{258,384},{259,385},{260,386},{261,387},{262,388},{263,389},{264,3... | collective-permute-start | bytes 393224 | tf_op jit(solution)/shard_map/ppermute | solution.py:98
  84.5 10.2 %collective-permute-start.21 = (bf16[64,1024]{1,0:T(8,128)(2,1)S(1)}, bf16[64,1024]{1,0:T(8,128)(2,1)S(1)}, u32[]{:S(2)}, u32[]{:S(2)}) collective-permute-start(bf16[64,1024]{1,0:T(8,128)(2,1)S(1)} %collective-permute-done.20.own_ref.refs_5_), channel_id=1, source_target_pairs={{385,384},{384,385},{387,386},{386,387},{389,388},{388,389},{391,3... | collective-permute-start | bytes 393224 | tf_op jit(solution)/shard_map/ppermute | solution.py:98
  87.3 9.8 %collective-permute-start.25 = (bf16[64,1024]{1,0:T(8,128)(2,1)S(1)}, bf16[64,1024]{1,0:T(8,128)(2,1)S(1)}, u32[]{:S(2)}, u32[]{:S(2)}) collective-permute-start(bf16[64,1024]{1,0:T(8,128)(2,1)S(1)} %get-tuple-element.32), channel_id=1, source_target_pairs={{383,384},{258,385},{257,386},{260,387},{259,388},{262,389},{261,3... | collective-permute-start | bytes 393224 | tf_op jit(solution)/shard_map/ppermute | solution.py:98
  88.7 8.9 %collective-permute-start.26 = (bf16[64,1024]{1,0:T(8,128)(2,1)S(1)}, bf16[64,1024]{1,0:T(8,128)(2,1)S(1)}, u32[]{:S(2)}, u32[]{:S(2)}) collective-permute-start(bf16[64,1024]{1,0:T(8,128)(2,1)S(1)} %get-tuple-element.32), channel_id=1, source_target_pairs={{258,384},{259,385},{260,386},{261,387},{262,388},{263,389},{264,3... | collective-permute-start | bytes 393224 | tf_op jit(solution)/shard_map/ppermute | solution.py:98
  90.0 7.6 %collective-permute-start.24 = (bf16[64,1024]{1,0:T(8,128)(2,1)S(1)}, bf16[64,1024]{1,0:T(8,128)(2,1)S(1)}, u32[]{:S(2)}, u32[]{:S(2)}) collective-permute-start(bf16[64,1024]{1,0:T(8,128)(2,1)S(1)} %collective-permute-done.19.own_ref.refs_5_), channel_id=1, source_target_pairs={{385,384},{384,385},{387,386},{386,387},{389,388},{388,389},{391,3... | collective-permute-start | bytes 393224 | tf_op jit(solution)/shard_map/ppermute | solution.py:98
  (1 other events, 0.7 us)

commit v2 on v1

v2 whole, which is shorter than its diff:
```python
import functools

import jax
import jax.numpy as jnp
from jax import lax
from jax.experimental import pallas as pl
from jax.experimental.pallas import tpu as pltpu
from jax.sharding import PartitionSpec as P

BLOCK = 64
TILES = 4
VMEM = pl.BlockSpec(memory_space=pltpu.VMEM)
SMEM = pl.BlockSpec(memory_space=pltpu.SMEM)
ANY = pl.BlockSpec(memory_space=pl.ANY)


def params():
    return pltpu.CompilerParams(vmem_limit_bytes=32 * 1024 * 1024)


def mask_kernel(where_ref, picks_ref, edges_ref, mask_ref, degree_ref):
    odd = where_ref[1] == 1
    for slab in range(2):
        rows = pl.ds(slab * BLOCK, BLOCK)
        e = edges_ref[rows, :].astype(jnp.float32)
        tiles = [e[:, t * BLOCK : (t + 1) * BLOCK] for t in range(TILES)]
        pick = [picks_ref[slab, k] for k in range(3)]
        behind, ahead, ahead2 = tiles[1], tiles[2], tiles[3]
        swap = jnp.where(odd, behind, ahead)
        cross = jnp.where(odd, ahead, behind)
        swap_pick = jnp.where(odd, pick[0], pick[1])
        cross_pick = jnp.where(odd, pick[1], pick[0])
        peers = ((ahead2, pick[2]), (cross, cross_pick), (swap, swap_pick))
        columns = [tiles[0]]
        for wanted in range(2):
            for tile, p in peers:
                columns.append(tile * jnp.where(p == wanted, 1.0, 0.0))
        columns.append(jnp.zeros_like(tiles[0]))
        full = jnp.concatenate(columns, axis=1)
        mask_ref[rows, :] = full.astype(jnp.bfloat16)
        degree = 1.0 + jnp.sum(full, axis=1, keepdims=True)
        degree_ref[rows, :] = jnp.broadcast_to(degree, (BLOCK, 128))


def self_kernel(layer, row, where_ref, own_ref, weight_ref, out_ref):
    @pl.when(where_ref[0] == layer)
    def _():
        out_ref[...] = jnp.dot(
            own_ref[pl.ds(row, BLOCK), :], weight_ref[...], preferred_element_type=jnp.float32
        )


def product(slab, rows, refs):
    mask_ref, degree_ref, self_ref, weight_ref = refs[:4]
    mine = pl.ds(slab * BLOCK, BLOCK)
    gathered = jnp.concatenate(
        [ref[pl.ds(row, BLOCK), :] for ref, row in zip(refs[4:], rows)], axis=0
    )
    summed = jnp.dot(
        mask_ref[mine, : 7 * BLOCK], gathered, preferred_element_type=jnp.float32
    )
    mean_rows = (summed / degree_ref[mine, :1]).astype(jnp.bfloat16)
    hidden = self_ref[...] + jnp.dot(
        mean_rows, weight_ref[...], preferred_element_type=jnp.float32
    )
    return jnp.maximum(hidden, 0.0).astype(jnp.bfloat16)


def layer_kernel(layer, slab, rows, where_ref, *refs):
    @pl.when(where_ref[0] == layer)
    def _():
        refs[-1][...] = product(slab, rows, refs[:11])


def last_kernel(layer, rows, where_ref, *refs):
    made = refs[11:-3]
    result_ref, block_ref, sems = refs[-3:]

    def leave(source, slab):
        return pltpu.make_async_copy(
            source, result_ref.at[pl.ds(slab * BLOCK, BLOCK), :], sems.at[slab]
        )

    for earlier in range(layer):

        @pl.when(where_ref[0] == earlier)
        def _():
            copies = [leave(made[2 * earlier + slab], slab) for slab in range(2)]
            for copy in copies:
                copy.start()
            for copy in copies:
                copy.wait()

    @pl.when(where_ref[0] == layer)
    def _():
        before = leave(made[2 * layer], 0)
        before.start()
        block_ref[...] = product(1, rows, refs[:11])
        after = leave(block_ref, 1)
        after.start()
        before.wait()
        after.wait()


def per_device(stacked, edges, picks, self_w, neigh_w):
    layers, domains = lax.axis_size("section"), lax.axis_size("dom")
    width = stacked.shape[2]
    features = stacked[0]
    weight_self, weight_neigh = self_w[0], neigh_w[0]
    section = lax.axis_index("section")
    domain = lax.axis_index("dom")
    where = jnp.stack([section, domain % 2]).astype(jnp.int32)
    axes = ("section", "dom")
    everyone = range(domains)

    def route(value, jumps, sections, hop, label):
        pairs = [
            (s * domains + (d + jump) % domains, (s + hop) * domains + d)
            for s in sections
            for d in everyone
            for jump in jumps(d)
        ]
        with jax.named_scope(label):
            return lax.ppermute(value, axes, pairs)

    def here(d):
        return (0,)

    def swapped(d):
        return (1,) if d % 2 == 0 else (-1,)

    def crossed(d):
        return (-1,) if d % 2 == 0 else (1,)

    def up2(d):
        return (2,)

    mask, degree = pl.pallas_call(
        mask_kernel,
        out_shape=(
            jax.ShapeDtypeStruct((2 * BLOCK, 8 * BLOCK), jnp.bfloat16),
            jax.ShapeDtypeStruct((2 * BLOCK, 128), jnp.float32),
        ),
        in_specs=[SMEM, SMEM, VMEM],
        out_specs=(VMEM, VMEM),
        compiler_params=params(),
        name="masks",
    )(where, picks, edges)

    cost = pl.CostEstimate(flops=1_000_000_000, bytes_accessed=0, transcendentals=0)

    def self_part(layer, own, row):
        return pl.pallas_call(
            functools.partial(self_kernel, layer, row),
            out_shape=jax.ShapeDtypeStruct((BLOCK, width), jnp.float32),
            in_specs=[SMEM, VMEM, VMEM],
            out_specs=VMEM,
            compiler_params=params(),
            cost_estimate=cost,
            name="self_part",
        )(where, own, weight_self)

    def layer_part(layer, slab, sources, part):
        arrays, rows = zip(*sources)
        return pl.pallas_call(
            functools.partial(layer_kernel, layer, slab, rows),
            out_shape=jax.ShapeDtypeStruct((BLOCK, width), jnp.bfloat16),
            in_specs=[SMEM] + [VMEM] * 11,
            out_specs=VMEM,
            compiler_params=params(),
            cost_estimate=cost,
            name="layer_part",
        )(where, mask, degree, part, weight_neigh, *arrays)

    def last_part(layer, sources, part, made):
        arrays, rows = zip(*sources)
        return pl.pallas_call(
            functools.partial(last_kernel, layer, rows),
            out_shape=jax.ShapeDtypeStruct((2 * BLOCK, width), jnp.bfloat16),
            in_specs=[SMEM] + [VMEM] * (11 + len(made)),
            out_specs=ANY,
            scratch_shapes=[
                pltpu.VMEM((BLOCK, width), jnp.bfloat16),
                pltpu.SemaphoreType.DMA((2,)),
            ],
            compiler_params=params(),
            cost_estimate=cost,
            name="last_part",
        )(where, mask, degree, part, weight_neigh, *arrays, *made)

    staged = [
        route(features, jumps, range(layers), 0, "init_" + jumps.__name__)
        for jumps in (up2, crossed, swapped)
    ]
    old = [[(array, slab * BLOCK) for array in staged] for slab in range(2)]
    made = []
    for layer in range(layers):
        incoming = []
        fresh = [old[0], None]
        for slab in range(2):
            if layer:
                own_now, peers_now = arriving[slab]
                if slab:
                    own_now, _ = lax.optimization_barrier((own_now, made[-1]))
                swap = route(own_now, swapped, [layer], 0, f"swap_l{layer}s{slab}")
                own = (own_now, 0)
                fresh[slab] = [(array, 0) for array in peers_now + [swap]]
            else:
                own = (features, slab * BLOCK)
                fresh[slab] = old[slab]
            with jax.named_scope(f"self_l{layer}s{slab}"):
                part = self_part(layer, *own)
            second = fresh[1] if slab == 1 else old[1]
            sources = [own] + fresh[0] + second
            with jax.named_scope(f"layer_l{layer}s{slab}"):
                if layer == layers - 1 and slab == 1:
                    result = last_part(layer, sources, part, made)
                else:
                    made.append(layer_part(layer, slab, sources, part))
            if layer < layers - 1:
                sent = [
                    route(made[-1], jumps, [layer], 1, f"{jumps.__name__}_l{layer}s{slab}")
                    for jumps in (here, up2, crossed)
                ]
                incoming.append((sent[0], sent[1:]))
        arriving = incoming
    return result[None]


def solution(mesh):
    in_specs = (
        P("section", "dom", None),
        P("dom", None),
        P("dom", None),
        P("section", None, None),
        P("section", None, None),
    )
    out_specs = P("section", "dom", None)
    return jax.shard_map(
        per_device, mesh=mesh, in_specs=in_specs, out_specs=out_specs, check_vma=False
    )
```

time: 102 us -> 92.8 us (0.910); the launches traced: 100 us -> 92.2 us
  waiting for transfers between devices: 38.3 us -> 32.7 us
  Pallas kernels: 14.5 us -> 12.5 us
    ppermute x27, waiting for transfers between devices: 38.3 us -> 32.7 us  [route(): return lax.ppermute(value, axes, pairs)]
    pallas_call x8, Pallas kernels: 8.39 us -> 6.41 us  [the longest x7 4.51 us: layer_part(): pl.pallas_call(functools.partial(layer_kernel, layer, slab, rows), out_sh...]
where the time goes in v2:
time: 92.8 us; the launch traced here: 92.2 us
  starting transfers between devices  42.2 us (45%)
  waiting for transfers between devices  32.7 us (35%)
  Pallas kernels  12.5 us (13%)
  local copies, waits for them, and re-layouts  4.13 us (4%)
    ppermute x27, starting transfers between devices, route(): return lax.ppermute(value, axes, pairs)  42.2 us
    ppermute x27, waiting for transfers between devices, route(): return lax.ppermute(value, axes, pairs)  32.7 us
    pallas_call x8, Pallas kernels, self_part(): pl.pallas_call(functools.partial(self_kernel, layer, row), out_shape=jax....  5.33 us
    pallas_call x7, Pallas kernels, layer_part(): pl.pallas_call(functools.partial(layer_kernel, layer, slab, rows), out_sh...  4.51 us
    unnamed x12, local copies, waits for them, and re-layouts  4.13 us
    pallas_call x1, Pallas kernels, last_part(): pl.pallas_call(functools.partial(last_kernel, layer, rows), out_shape=jax...  1.9 us
  transfers between devices with their start and end apart: 27, of which 4 were waited for; matrix products, arithmetic and copies ran while one was open for 0% of the time, Pallas kernels for 11%

profile of v2, /device:TPU:7, one launch (start us, length us, event | category | flops | bytes accessed | tf_op | source)
XLA Modules:
  0.0 92.2 jit_solution(9491515008802271113)
XLA Ops:
  0.0 13.7 %collective-permute-start = (bf16[128,1024]{1,0:T(8,128)(2,1)}, bf16[128,1024]{1,0:T(8,128)(2,1)S(1)}, u32[]{:S(2)}, u32[]{:S(2)}) collective-permute-start(bf16[128,1024]{1,0:T(8,128)(2,1)} %bitcast.14), channel_id=1, source_target_pairs={{2,0},{3,1},{4,2},{5,3},{6,4},{7,5},{8,6},{9,7},{10,8},{11,9},{12,... | collective-permute-start | bytes 786440 | tf_op jit(solution)/shard_map/init_up2/ppermute | solution.py:124
  13.7 1.9 %collective-permute-start.1 = (bf16[128,1024]{1,0:T(8,128)(2,1)}, bf16[128,1024]{1,0:T(8,128)(2,1)S(1)}, u32[]{:S(2)}, u32[]{:S(2)}) collective-permute-start(bf16[128,1024]{1,0:T(8,128)(2,1)} %bitcast.15), channel_id=1, source_target_pairs={{127,0},{2,1},{1,2},{4,3},{3,4},{6,5},{5,6},{8,7},{7,8},{10,9},{9,... | collective-permute-start | bytes 786440 | tf_op jit(solution)/shard_map/init_crossed/ppermute | solution.py:124
  15.6 2.9 %collective-permute-start.2 = (bf16[128,1024]{1,0:T(8,128)(2,1)}, bf16[128,1024]{1,0:T(8,128)(2,1)S(1)}, u32[]{:S(2)}, u32[]{:S(2)}) collective-permute-start(bf16[128,1024]{1,0:T(8,128)(2,1)} %bitcast.16), channel_id=1, source_target_pairs={{1,0},{0,1},{3,2},{2,3},{5,4},{4,5},{7,6},{6,7},{9,8},{8,9},{11,10... | collective-permute-start | bytes 786440 | tf_op jit(solution)/shard_map/init_swapped/ppermute | solution.py:124
  18.6 0.9 copy-done.2
  19.5 0.7 copy-done.3
  20.2 0.8 masks.1
  21.0 0.9 %copy-done.1 = bf16[1,128,1024]{2,1,0:T(8,128)(2,1)S(1)} copy-done((bf16[1,128,1024]{2,1,0:T(8,128)(2,1)S(1)}, bf16[1,128,1024]{2,1,0:T(8,128)(2,1)}, u32[]{:S(2)}) %copy-start.1) | copy-done | bytes 262168
  21.9 1.6 %copy-done.4 = bf16[1,1024,1024]{2,1,0:T(8,128)(2,1)S(1)} copy-done((bf16[1,1024,1024]{2,1,0:T(8,128)(2,1)S(1)}, bf16[1,1024,1024]{2,1,0:T(8,128)(2,1)}, u32[]{:S(2)}) %copy-start.4) | copy-done | bytes 2097176
  24.7 0.7 collective-permute-start.4
  25.9 0.7 collective-permute-start.5
  26.6 0.7 collective-permute-start.6
  27.3 0.7 collective-permute-start.7
  28.5 0.7 collective-permute-start.3
  29.2 0.7 collective-permute-start.8
  30.5 0.8 collective-permute-start.9
  31.9 0.7 collective-permute-start.12
  35.2 0.7 collective-permute-start.15
  39.6 1.3 %collective-permute-start.20 = (bf16[64,1024]{1,0:T(8,128)(2,1)S(1)}, bf16[64,1024]{1,0:T(8,128)(2,1)S(1)}, u32[]{:S(2)}, u32[]{:S(2)}) collective-permute-start(bf16[64,1024]{1,0:T(8,128)(2,1)S(1)} %layer_part.11.refs_15_), channel_id=1, source_target_pairs={{256,384},{257,385},{258,386},{259,387},{260,388},{261,389},{262,3... | collective-permute-start | bytes 393224 | tf_op jit(solution)/shard_map/here_l2s0/ppermute | solution.py:124
  41.6 1.3 %collective-permute-start.21 = (bf16[64,1024]{1,0:T(8,128)(2,1)S(1)}, bf16[64,1024]{1,0:T(8,128)(2,1)S(1)}, u32[]{:S(2)}, u32[]{:S(2)}) collective-permute-start(bf16[64,1024]{1,0:T(8,128)(2,1)S(1)} %layer_part.11.refs_15_), channel_id=1, source_target_pairs={{258,384},{259,385},{260,386},{261,387},{262,388},{263,389},{264,3... | collective-permute-start | bytes 393224 | tf_op jit(solution)/shard_map/up2_l2s0/ppermute | solution.py:124
  43.5 1.3 %collective-permute-start.22 = (bf16[64,1024]{1,0:T(8,128)(2,1)S(1)}, bf16[64,1024]{1,0:T(8,128)(2,1)S(1)}, u32[]{:S(2)}, u32[]{:S(2)}) collective-permute-start(bf16[64,1024]{1,0:T(8,128)(2,1)S(1)} %layer_part.11.refs_15_), channel_id=1, source_target_pairs={{383,384},{258,385},{257,386},{260,387},{259,388},{262,389},{261,3... | collective-permute-start | bytes 393224 | tf_op jit(solution)/shard_map/crossed_l2s0/ppermute | solution.py:124
  44.8 19.6 %collective-permute-done.20.own_ref.refs_4_ = bf16[64,1024]{1,0:T(8,128)(2,1)S(1)} collective-permute-done((bf16[64,1024]{1,0:T(8,128)(2,1)S(1)}, bf16[64,1024]{1,0:T(8,128)(2,1)S(1)}, u32[]{:S(2)}, u32[]{:S(2)}) %collective-permute-start.20) | collective-permute-done | bytes 131104 | tf_op jit(solution)/shard_map/here_l2s0/ppermute | solution.py:124
  64.4 2.6 %collective-permute-start.23 = (bf16[64,1024]{1,0:T(8,128)(2,1)S(1)}, bf16[64,1024]{1,0:T(8,128)(2,1)S(1)}, u32[]{:S(2)}, u32[]{:S(2)}) collective-permute-start(bf16[64,1024]{1,0:T(8,128)(2,1)S(1)} %collective-permute-done.20.own_ref.refs_4_), channel_id=1, source_target_pairs={{385,384},{384,385},{387,386},{386,387},{389,388},{388,389},{391,3... | collective-permute-start | bytes 393224 | tf_op jit(solution)/shard_map/swap_l3s0/ppermute | solution.py:124
  67.6 1.3 %collective-permute-start.19 = (bf16[64,1024]{1,0:T(8,128)(2,1)S(1)}, bf16[64,1024]{1,0:T(8,128)(2,1)S(1)}, u32[]{:S(2)}, u32[]{:S(2)}) collective-permute-start(bf16[64,1024]{1,0:T(8,128)(2,1)S(1)} %layer_part.12.refs_16_), channel_id=1, source_target_pairs={{256,384},{257,385},{258,386},{259,387},{260,388},{261,389},{262,3... | collective-permute-start | bytes 393224 | tf_op jit(solution)/shard_map/here_l2s1/ppermute | solution.py:124
  68.9 1.3 %collective-permute-start.24 = (bf16[64,1024]{1,0:T(8,128)(2,1)S(1)}, bf16[64,1024]{1,0:T(8,128)(2,1)S(1)}, u32[]{:S(2)}, u32[]{:S(2)}) collective-permute-start(bf16[64,1024]{1,0:T(8,128)(2,1)S(1)} %layer_part.12.refs_16_), channel_id=1, source_target_pairs={{258,384},{259,385},{260,386},{261,387},{262,388},{263,389},{264,3... | collective-permute-start | bytes 393224 | tf_op jit(solution)/shard_map/up2_l2s1/ppermute | solution.py:124
  70.2 1.0 %self_part.14.refs_2_ = f32[64,1024]{1,0:T(8,128)S(1)} custom-call(s32[2]{0:T(128)S(1)} %pad_add_fusion.where_ref, bf16[64,1024]{1,0:T(8,128)(2,1)S(1)} %collective-permute-done.20.own_ref.refs_4_, bf16[1024,1024]{1,0:T(8,128)(2,1)S(1)} %bitcast.27), custom_call_target="tpu_custom_call" | custom-call | flops 1000000000 | tf_op jit(solution)/shard_map/self_l3s0/self_part/pallas_call | solution.py:153
  71.2 3.7 %collective-permute-done.21.refs_5_ = bf16[64,1024]{1,0:T(8,128)(2,1)S(1)} collective-permute-done((bf16[64,1024]{1,0:T(8,128)(2,1)S(1)}, bf16[64,1024]{1,0:T(8,128)(2,1)S(1)}, u32[]{:S(2)}, u32[]{:S(2)}) %collective-permute-start.21) | collective-permute-done | bytes 131104 | tf_op jit(solution)/shard_map/up2_l2s0/ppermute | solution.py:124
  74.9 1.3 %collective-permute-start.25 = (bf16[64,1024]{1,0:T(8,128)(2,1)S(1)}, bf16[64,1024]{1,0:T(8,128)(2,1)S(1)}, u32[]{:S(2)}, u32[]{:S(2)}) collective-permute-start(bf16[64,1024]{1,0:T(8,128)(2,1)S(1)} %layer_part.12.refs_16_), channel_id=1, source_target_pairs={{383,384},{258,385},{257,386},{260,387},{259,388},{262,389},{261,3... | collective-permute-start | bytes 393224 | tf_op jit(solution)/shard_map/crossed_l2s1/ppermute | solution.py:124
  76.3 1.2 %layer_part.13.refs_17_ = bf16[64,1024]{1,0:T(8,128)(2,1)S(1)} custom-call(s32[2]{0:T(128)S(1)} %pad_add_fusion.where_ref, bf16[128,512]{1,0:T(8,128)(2,1)S(1)} %get-tuple-element.10.refs_0_, f32[128,128]{1,0:T(8,128)S(1)} %get-tuple-element.11.refs_1_, f32[64,1024]{1,0:T(8,128)S(1)} %self_part.14.refs_2_, bf16[1024,1024]{1,0:T(8,128)(2,1)S(1)} %bitcast.12, ...), custom_call_target="tpu_custom_call" | custom-call | flops 1000000000 | tf_op jit(solution)/shard_map/layer_l3s0/layer_part/pallas_call | solution.py:165
  77.5 9.2 %collective-permute-done.19.own_ref.refs_4_ = bf16[64,1024]{1,0:T(8,128)(2,1)S(1)} collective-permute-done((bf16[64,1024]{1,0:T(8,128)(2,1)S(1)}, bf16[64,1024]{1,0:T(8,128)(2,1)S(1)}, u32[]{:S(2)}, u32[]{:S(2)}) %collective-permute-start.19) | collective-permute-done | bytes 131104 | tf_op jit(solution)/shard_map/here_l2s1/ppermute | solution.py:124
  86.7 2.6 %collective-permute-start.26 = (bf16[64,1024]{1,0:T(8,128)(2,1)S(1)}, bf16[64,1024]{1,0:T(8,128)(2,1)S(1)}, u32[]{:S(2)}, u32[]{:S(2)}) collective-permute-start(bf16[64,1024]{1,0:T(8,128)(2,1)S(1)} %collective-permute-done.19.own_ref.refs_4_), channel_id=1, source_target_pairs={{385,384},{384,385},{387,386},{386,387},{389,388},{388,389},{391,3... | collective-permute-start | bytes 393224 | tf_op jit(solution)/shard_map/swap_l3s1/ppermute | solution.py:124
  89.3 1.0 %self_part.15.refs_2_ = f32[64,1024]{1,0:T(8,128)S(1)} custom-call(s32[2]{0:T(128)S(1)} %pad_add_fusion.where_ref, bf16[64,1024]{1,0:T(8,128)(2,1)S(1)} %collective-permute-done.19.own_ref.refs_4_, bf16[1024,1024]{1,0:T(8,128)(2,1)S(1)} %bitcast.28), custom_call_target="tpu_custom_call" | custom-call | flops 1000000000 | tf_op jit(solution)/shard_map/self_l3s1/self_part/pallas_call | solution.py:153
  90.3 1.9 %last_part.1 = bf16[128,1024]{1,0:T(8,128)(2,1)} custom-call(s32[2]{0:T(128)S(1)} %pad_add_fusion.where_ref, bf16[128,512]{1,0:T(8,128)(2,1)S(1)} %get-tuple-element.10.refs_0_, f32[128,128]{1,0:T(8,128)S(1)} %get-tuple-element.11.refs_1_, f32[64,1024]{1,0:T(8,128)S(1)} %self_part.15.refs_2_, bf16[1024,1024]{1,0:T(8,128)(2,1)S(1)} %bitcast.13, ...), custom_call_target="tpu_custom_call" | custom-call | flops 1000000000 | tf_op jit(solution)/shard_map/layer_l3s1/last_part/pallas_call | solution.py:177
  (52 shorter events, 11.5 us)
Async XLA Ops:
  0.0 24.1 %copy-start = (bf16[1,1024,1024]{2,1,0:T(8,128)(2,1)S(1)}, bf16[1,1024,1024]{2,1,0:T(8,128)(2,1)}, u32[]{:S(2)}) copy-start(bf16[1,1024,1024]{2,1,0:T(8,128)(2,1)} %param.9) | copy-start | bytes 6291460
  0.0 24.1 %collective-permute-start = (bf16[128,1024]{1,0:T(8,128)(2,1)}, bf16[128,1024]{1,0:T(8,128)(2,1)S(1)}, u32[]{:S(2)}, u32[]{:S(2)}) collective-permute-start(bf16[128,1024]{1,0:T(8,128)(2,1)} %bitcast.14), channel_id=1, source_target_pairs={{2,0},{3,1},{4,2},{5,3},{6,4},{7,5},{8,6},{9,7},{10,8},{11,9},{12,... | collective-permute-start | bytes 786440 | tf_op jit(solution)/shard_map/init_up2/ppermute | solution.py:124
  13.7 10.4 %collective-permute-start.1 = (bf16[128,1024]{1,0:T(8,128)(2,1)}, bf16[128,1024]{1,0:T(8,128)(2,1)S(1)}, u32[]{:S(2)}, u32[]{:S(2)}) collective-permute-start(bf16[128,1024]{1,0:T(8,128)(2,1)} %bitcast.15), channel_id=1, source_target_pairs={{127,0},{2,1},{1,2},{4,3},{3,4},{6,5},{5,6},{8,7},{7,8},{10,9},{9,... | collective-permute-start | bytes 786440 | tf_op jit(solution)/shard_map/init_crossed/ppermute | solution.py:124
  15.6 8.5 %collective-permute-start.2 = (bf16[128,1024]{1,0:T(8,128)(2,1)}, bf16[128,1024]{1,0:T(8,128)(2,1)S(1)}, u32[]{:S(2)}, u32[]{:S(2)}) collective-permute-start(bf16[128,1024]{1,0:T(8,128)(2,1)} %bitcast.16), channel_id=1, source_target_pairs={{1,0},{0,1},{3,2},{2,3},{5,4},{4,5},{7,6},{6,7},{9,8},{8,9},{11,10... | collective-permute-start | bytes 786440 | tf_op jit(solution)/shard_map/init_swapped/ppermute | solution.py:124
  18.6 0.9 copy-start.2
  21.0 1.0 %copy-start.1 = (bf16[1,128,1024]{2,1,0:T(8,128)(2,1)S(1)}, bf16[1,128,1024]{2,1,0:T(8,128)(2,1)}, u32[]{:S(2)}) copy-start(bf16[1,128,1024]{2,1,0:T(8,128)(2,1)} %param.5) | copy-start | bytes 786436
  21.9 1.6 %copy-start.4 = (bf16[1,1024,1024]{2,1,0:T(8,128)(2,1)S(1)}, bf16[1,1024,1024]{2,1,0:T(8,128)(2,1)}, u32[]{:S(2)}) copy-start(bf16[1,1024,1024]{2,1,0:T(8,128)(2,1)} %param.8) | copy-start | bytes 6291460
  24.7 2.6 %collective-permute-start.4 = (bf16[64,1024]{1,0:T(8,128)(2,1)S(1)}, bf16[64,1024]{1,0:T(8,128)(2,1)S(1)}, u32[]{:S(2)}, u32[]{:S(2)}) collective-permute-start(bf16[64,1024]{1,0:T(8,128)(2,1)S(1)} %layer_part.8.refs_11_), channel_id=1, source_target_pairs={{0,128},{1,129},{2,130},{3,131},{4,132},{5,133},{6,134},{7,135},{8... | collective-permute-start | bytes 393224 | tf_op jit(solution)/shard_map/here_l0s0/ppermute | solution.py:124
  25.9 4.5 %collective-permute-start.5 = (bf16[64,1024]{1,0:T(8,128)(2,1)S(1)}, bf16[64,1024]{1,0:T(8,128)(2,1)S(1)}, u32[]{:S(2)}, u32[]{:S(2)}) collective-permute-start(bf16[64,1024]{1,0:T(8,128)(2,1)S(1)} %layer_part.8.refs_11_), channel_id=1, source_target_pairs={{2,128},{3,129},{4,130},{5,131},{6,132},{7,133},{8,134},{9,135},{1... | collective-permute-start | bytes 393224 | tf_op jit(solution)/shard_map/up2_l0s0/ppermute | solution.py:124
  26.6 4.7 %collective-permute-start.6 = (bf16[64,1024]{1,0:T(8,128)(2,1)S(1)}, bf16[64,1024]{1,0:T(8,128)(2,1)S(1)}, u32[]{:S(2)}, u32[]{:S(2)}) collective-permute-start(bf16[64,1024]{1,0:T(8,128)(2,1)S(1)} %layer_part.8.refs_11_), channel_id=1, source_target_pairs={{127,128},{2,129},{1,130},{4,131},{3,132},{6,133},{5,134},{8,135},... | collective-permute-start | bytes 393224 | tf_op jit(solution)/shard_map/crossed_l0s0/ppermute | solution.py:124
  27.3 4.0 %collective-permute-start.7 = (bf16[64,1024]{1,0:T(8,128)(2,1)S(1)}, bf16[64,1024]{1,0:T(8,128)(2,1)S(1)}, u32[]{:S(2)}, u32[]{:S(2)}) collective-permute-start(bf16[64,1024]{1,0:T(8,128)(2,1)S(1)} %collective-permute-done.4.own_ref.refs_4_), channel_id=1, source_target_pairs={{129,128},{128,129},{131,130},{130,131},{133,132},{132,133},{135,1... | collective-permute-start | bytes 393224 | tf_op jit(solution)/shard_map/swap_l1s0/ppermute | solution.py:124
  28.5 4.0 %collective-permute-start.3 = (bf16[64,1024]{1,0:T(8,128)(2,1)S(1)}, bf16[64,1024]{1,0:T(8,128)(2,1)S(1)}, u32[]{:S(2)}, u32[]{:S(2)}) collective-permute-start(bf16[64,1024]{1,0:T(8,128)(2,1)S(1)} %layer_part.7.refs_12_), channel_id=1, source_target_pairs={{0,128},{1,129},{2,130},{3,131},{4,132},{5,133},{6,134},{7,135},{8... | collective-permute-start | bytes 393224 | tf_op jit(solution)/shard_map/here_l0s1/ppermute | solution.py:124
  29.2 5.3 %collective-permute-start.8 = (bf16[64,1024]{1,0:T(8,128)(2,1)S(1)}, bf16[64,1024]{1,0:T(8,128)(2,1)S(1)}, u32[]{:S(2)}, u32[]{:S(2)}) collective-permute-start(bf16[64,1024]{1,0:T(8,128)(2,1)S(1)} %layer_part.7.refs_12_), channel_id=1, source_target_pairs={{2,128},{3,129},{4,130},{5,131},{6,132},{7,133},{8,134},{9,135},{1... | collective-permute-start | bytes 393224 | tf_op jit(solution)/shard_map/up2_l0s1/ppermute | solution.py:124
  30.4 3.5 %copy-start.5 = (bf16[1,1024,1024]{2,1,0:T(8,128)(2,1)S(1)}, bf16[1,1024,1024]{2,1,0:T(8,128)(2,1)}, u32[]{:S(2)}) copy-start(bf16[1,1024,1024]{2,1,0:T(8,128)(2,1)} %param.8) | copy-start | bytes 6291460
  30.5 5.4 %collective-permute-start.9 = (bf16[64,1024]{1,0:T(8,128)(2,1)S(1)}, bf16[64,1024]{1,0:T(8,128)(2,1)S(1)}, u32[]{:S(2)}, u32[]{:S(2)}) collective-permute-start(bf16[64,1024]{1,0:T(8,128)(2,1)S(1)} %layer_part.7.refs_12_), channel_id=1, source_target_pairs={{127,128},{2,129},{1,130},{4,131},{3,132},{6,133},{5,134},{8,135},... | collective-permute-start | bytes 393224 | tf_op jit(solution)/shard_map/crossed_l0s1/ppermute | solution.py:124
  31.9 3.3 %collective-permute-start.12 = (bf16[64,1024]{1,0:T(8,128)(2,1)S(1)}, bf16[64,1024]{1,0:T(8,128)(2,1)S(1)}, u32[]{:S(2)}, u32[]{:S(2)}) collective-permute-start(bf16[64,1024]{1,0:T(8,128)(2,1)S(1)} %layer_part.9.refs_13_), channel_id=1, source_target_pairs={{128,256},{129,257},{130,258},{131,259},{132,260},{133,261},{134,2... | collective-permute-start | bytes 393224 | tf_op jit(solution)/shard_map/here_l1s0/ppermute | solution.py:124
  32.5 3.3 %collective-permute-start.10 = (bf16[64,1024]{1,0:T(8,128)(2,1)S(1)}, bf16[64,1024]{1,0:T(8,128)(2,1)S(1)}, u32[]{:S(2)}, u32[]{:S(2)}) collective-permute-start(bf16[64,1024]{1,0:T(8,128)(2,1)S(1)} %collective-permute-done.3.own_ref.refs_4_), channel_id=1, source_target_pairs={{129,128},{128,129},{131,130},{130,131},{133,132},{132,133},{135,1... | collective-permute-start | bytes 393224 | tf_op jit(solution)/shard_map/swap_l1s1/ppermute | solution.py:124
  33.2 5.1 %collective-permute-start.13 = (bf16[64,1024]{1,0:T(8,128)(2,1)S(1)}, bf16[64,1024]{1,0:T(8,128)(2,1)S(1)}, u32[]{:S(2)}, u32[]{:S(2)}) collective-permute-start(bf16[64,1024]{1,0:T(8,128)(2,1)S(1)} %layer_part.9.refs_13_), channel_id=1, source_target_pairs={{130,256},{131,257},{132,258},{133,259},{134,260},{135,261},{136,2... | collective-permute-start | bytes 393224 | tf_op jit(solution)/shard_map/up2_l1s0/ppermute | solution.py:124
  34.5 4.5 %collective-permute-start.14 = (bf16[64,1024]{1,0:T(8,128)(2,1)S(1)}, bf16[64,1024]{1,0:T(8,128)(2,1)S(1)}, u32[]{:S(2)}, u32[]{:S(2)}) collective-permute-start(bf16[64,1024]{1,0:T(8,128)(2,1)S(1)} %layer_part.9.refs_13_), channel_id=1, source_target_pairs={{255,256},{130,257},{129,258},{132,259},{131,260},{134,261},{133,2... | collective-permute-start | bytes 393224 | tf_op jit(solution)/shard_map/crossed_l1s0/ppermute | solution.py:124
  35.2 3.9 %collective-permute-start.15 = (bf16[64,1024]{1,0:T(8,128)(2,1)S(1)}, bf16[64,1024]{1,0:T(8,128)(2,1)S(1)}, u32[]{:S(2)}, u32[]{:S(2)}) collective-permute-start(bf16[64,1024]{1,0:T(8,128)(2,1)S(1)} %collective-permute-done.12.own_ref.refs_4_), channel_id=1, source_target_pairs={{257,256},{256,257},{259,258},{258,259},{261,260},{260,261},{263,2... | collective-permute-start | bytes 393224 | tf_op jit(solution)/shard_map/swap_l2s0/ppermute | solution.py:124
  36.4 4.5 %collective-permute-start.11 = (bf16[64,1024]{1,0:T(8,128)(2,1)S(1)}, bf16[64,1024]{1,0:T(8,128)(2,1)S(1)}, u32[]{:S(2)}, u32[]{:S(2)}) collective-permute-start(bf16[64,1024]{1,0:T(8,128)(2,1)S(1)} %layer_part.10.refs_14_), channel_id=1, source_target_pairs={{128,256},{129,257},{130,258},{131,259},{132,260},{133,261},{134,2... | collective-permute-start | bytes 393224 | tf_op jit(solution)/shard_map/here_l1s1/ppermute | solution.py:124
  37.1 6.3 %collective-permute-start.16 = (bf16[64,1024]{1,0:T(8,128)(2,1)S(1)}, bf16[64,1024]{1,0:T(8,128)(2,1)S(1)}, u32[]{:S(2)}, u32[]{:S(2)}) collective-permute-start(bf16[64,1024]{1,0:T(8,128)(2,1)S(1)} %layer_part.10.refs_14_), channel_id=1, source_target_pairs={{130,256},{131,257},{132,258},{133,259},{134,260},{135,261},{136,2... | collective-permute-start | bytes 393224 | tf_op jit(solution)/shard_map/up2_l1s1/ppermute | solution.py:124
  38.3 28.7 %collective-permute-start.17 = (bf16[64,1024]{1,0:T(8,128)(2,1)S(1)}, bf16[64,1024]{1,0:T(8,128)(2,1)S(1)}, u32[]{:S(2)}, u32[]{:S(2)}) collective-permute-start(bf16[64,1024]{1,0:T(8,128)(2,1)S(1)} %layer_part.10.refs_14_), channel_id=1, source_target_pairs={{255,256},{130,257},{129,258},{132,259},{131,260},{134,261},{133,2... | collective-permute-start | bytes 393224 | tf_op jit(solution)/shard_map/crossed_l1s1/ppermute | solution.py:124
  39.6 24.8 %collective-permute-start.20 = (bf16[64,1024]{1,0:T(8,128)(2,1)S(1)}, bf16[64,1024]{1,0:T(8,128)(2,1)S(1)}, u32[]{:S(2)}, u32[]{:S(2)}) collective-permute-start(bf16[64,1024]{1,0:T(8,128)(2,1)S(1)} %layer_part.11.refs_15_), channel_id=1, source_target_pairs={{256,384},{257,385},{258,386},{259,387},{260,388},{261,389},{262,3... | collective-permute-start | bytes 393224 | tf_op jit(solution)/shard_map/here_l2s0/ppermute | solution.py:124
  40.9 26.1 %collective-permute-start.18 = (bf16[64,1024]{1,0:T(8,128)(2,1)S(1)}, bf16[64,1024]{1,0:T(8,128)(2,1)S(1)}, u32[]{:S(2)}, u32[]{:S(2)}) collective-permute-start(bf16[64,1024]{1,0:T(8,128)(2,1)S(1)} %collective-permute-done.11.own_ref.refs_4_), channel_id=1, source_target_pairs={{257,256},{256,257},{259,258},{258,259},{261,260},{260,261},{263,2... | collective-permute-start | bytes 393224 | tf_op jit(solution)/shard_map/swap_l2s1/ppermute | solution.py:124
  41.6 33.3 %collective-permute-start.21 = (bf16[64,1024]{1,0:T(8,128)(2,1)S(1)}, bf16[64,1024]{1,0:T(8,128)(2,1)S(1)}, u32[]{:S(2)}, u32[]{:S(2)}) collective-permute-start(bf16[64,1024]{1,0:T(8,128)(2,1)S(1)} %layer_part.11.refs_15_), channel_id=1, source_target_pairs={{258,384},{259,385},{260,386},{261,387},{262,388},{263,389},{264,3... | collective-permute-start | bytes 393224 | tf_op jit(solution)/shard_map/up2_l2s0/ppermute | solution.py:124
  43.5 32.8 %collective-permute-start.22 = (bf16[64,1024]{1,0:T(8,128)(2,1)S(1)}, bf16[64,1024]{1,0:T(8,128)(2,1)S(1)}, u32[]{:S(2)}, u32[]{:S(2)}) collective-permute-start(bf16[64,1024]{1,0:T(8,128)(2,1)S(1)} %layer_part.11.refs_15_), channel_id=1, source_target_pairs={{383,384},{258,385},{257,386},{260,387},{259,388},{262,389},{261,3... | collective-permute-start | bytes 393224 | tf_op jit(solution)/shard_map/crossed_l2s0/ppermute | solution.py:124
  64.4 11.9 %collective-permute-start.23 = (bf16[64,1024]{1,0:T(8,128)(2,1)S(1)}, bf16[64,1024]{1,0:T(8,128)(2,1)S(1)}, u32[]{:S(2)}, u32[]{:S(2)}) collective-permute-start(bf16[64,1024]{1,0:T(8,128)(2,1)S(1)} %collective-permute-done.20.own_ref.refs_4_), channel_id=1, source_target_pairs={{385,384},{384,385},{387,386},{386,387},{389,388},{388,389},{391,3... | collective-permute-start | bytes 393224 | tf_op jit(solution)/shard_map/swap_l3s0/ppermute | solution.py:124
  67.6 19.1 %collective-permute-start.19 = (bf16[64,1024]{1,0:T(8,128)(2,1)S(1)}, bf16[64,1024]{1,0:T(8,128)(2,1)S(1)}, u32[]{:S(2)}, u32[]{:S(2)}) collective-permute-start(bf16[64,1024]{1,0:T(8,128)(2,1)S(1)} %layer_part.12.refs_16_), channel_id=1, source_target_pairs={{256,384},{257,385},{258,386},{259,387},{260,388},{261,389},{262,3... | collective-permute-start | bytes 393224 | tf_op jit(solution)/shard_map/here_l2s1/ppermute | solution.py:124
  68.9 21.4 %collective-permute-start.24 = (bf16[64,1024]{1,0:T(8,128)(2,1)S(1)}, bf16[64,1024]{1,0:T(8,128)(2,1)S(1)}, u32[]{:S(2)}, u32[]{:S(2)}) collective-permute-start(bf16[64,1024]{1,0:T(8,128)(2,1)S(1)} %layer_part.12.refs_16_), channel_id=1, source_target_pairs={{258,384},{259,385},{260,386},{261,387},{262,388},{263,389},{264,3... | collective-permute-start | bytes 393224 | tf_op jit(solution)/shard_map/up2_l2s1/ppermute | solution.py:124
  74.9 15.4 %collective-permute-start.25 = (bf16[64,1024]{1,0:T(8,128)(2,1)S(1)}, bf16[64,1024]{1,0:T(8,128)(2,1)S(1)}, u32[]{:S(2)}, u32[]{:S(2)}) collective-permute-start(bf16[64,1024]{1,0:T(8,128)(2,1)S(1)} %layer_part.12.refs_16_), channel_id=1, source_target_pairs={{383,384},{258,385},{257,386},{260,387},{259,388},{262,389},{261,3... | collective-permute-start | bytes 393224 | tf_op jit(solution)/shard_map/crossed_l2s1/ppermute | solution.py:124
  86.7 3.6 %collective-permute-start.26 = (bf16[64,1024]{1,0:T(8,128)(2,1)S(1)}, bf16[64,1024]{1,0:T(8,128)(2,1)S(1)}, u32[]{:S(2)}, u32[]{:S(2)}) collective-permute-start(bf16[64,1024]{1,0:T(8,128)(2,1)S(1)} %collective-permute-done.19.own_ref.refs_4_), channel_id=1, source_target_pairs={{385,384},{384,385},{387,386},{386,387},{389,388},{388,389},{391,3... | collective-permute-start | bytes 393224 | tf_op jit(solution)/shard_map/swap_l3s1/ppermute | solution.py:124
  (1 other events, 0.7 us)

commit v3 on v0

v3 whole, which is shorter than its diff:
```python
import functools

import jax
import jax.numpy as jnp
from jax import lax
from jax.experimental import pallas as pl
from jax.experimental.pallas import tpu as pltpu
from jax.sharding import PartitionSpec as P

BLOCK = 64
ROWS = 2 * BLOCK
SPAN = 6 * BLOCK
VMEM = pl.BlockSpec(memory_space=pltpu.VMEM)
SMEM = pl.BlockSpec(memory_space=pltpu.SMEM)
ANY = pl.BlockSpec(memory_space=pl.ANY)
COST = pl.CostEstimate(flops=1_000_000_000, bytes_accessed=0, transcendentals=0)


def params():
    return pltpu.CompilerParams(vmem_limit_bytes=32 * 1024 * 1024)


def at(where_ref, section, core):
    return (where_ref[0] == section) & (where_ref[1] == core)


def dot(a, b):
    return jnp.dot(a, b, preferred_element_type=jnp.float32)


def tiles_kernel(picks_ref, edges_ref, tiles_ref):
    for slab in range(2):
        rows = pl.ds(slab * BLOCK, BLOCK)
        e = edges_ref[rows, :].astype(jnp.float32)
        columns = [e[:, :BLOCK]]
        for wanted in range(2):
            for k in range(3):
                live = jnp.where(picks_ref[slab, k] == wanted, 1.0, 0.0)
                columns.append(e[:, (k + 1) * BLOCK : (k + 2) * BLOCK] * live)
        columns.append(jnp.zeros_like(columns[0]))
        tiles_ref[rows, :] = jnp.concatenate(columns, axis=1).astype(jnp.bfloat16)


def weave_kernel(where_ref, mine_ref, other_ref, near_ref, far_ref, lend_ref, degree_ref):
    for core in range(2):
        even_ref, odd_ref = (mine_ref, other_ref) if core == 0 else (other_ref, mine_ref)

        @pl.when(where_ref[1] == core)
        def _():
            def put(out_ref, to_slab, from_slab):
                for r, ref in enumerate((even_ref, odd_ref)):
                    t = ref[pl.ds(to_slab * BLOCK, BLOCK), :].astype(jnp.float32)
                    part = [t[:, i * BLOCK : (i + 1) * BLOCK] for i in range(7)]
                    none = jnp.zeros_like(part[0])
                    behind, ahead, ahead2 = part[1 + 3 * from_slab : 4 + 3 * from_slab]
                    own = part[0] if to_slab == from_slab else none
                    five = [behind, own, ahead, ahead2, none]
                    columns = five + [none] if r == 0 else [none] + five
                    out_ref[pl.ds(r * BLOCK, BLOCK), :] = jnp.concatenate(columns, axis=1).astype(
                        jnp.bfloat16
                    )

            put(near_ref, core, core)
            put(far_ref, core, 1 - core)
            put(lend_ref, 1, 0)
            for r, ref in enumerate((even_ref, odd_ref)):
                t = ref[pl.ds(core * BLOCK, BLOCK), :].astype(jnp.float32)
                degree = 1.0 + jnp.sum(t, axis=1, keepdims=True)
                degree_ref[pl.ds(r * BLOCK, BLOCK), :] = jnp.broadcast_to(degree, (BLOCK, 128))


def staged_rows(core, slab, refs):
    down, mine, other, up_mine, up_other = refs
    if core == 0:
        order = (down, mine, other, up_mine, up_other, down)
    else:
        order = (down, other, mine, up_other, up_mine, down)
    return jnp.concatenate([ref[pl.ds(slab * BLOCK, BLOCK), :] for ref in order], axis=0)


def finish(summed, degree_ref, self_ref, weight_ref):
    mean_rows = (summed / degree_ref[:, :1]).astype(jnp.bfloat16)
    hidden = self_ref[...] + dot(mean_rows, weight_ref[...])
    return jnp.maximum(hidden, 0.0).astype(jnp.bfloat16)


def first_self_kernel(where_ref, weight_ref, mine_ref, other_ref, out_ref):
    for core in range(2):
        even_ref, odd_ref = (mine_ref, other_ref) if core == 0 else (other_ref, mine_ref)

        @pl.when(at(where_ref, 0, core))
        def _():
            rows = pl.ds(core * BLOCK, BLOCK)
            own = jnp.concatenate([even_ref[rows, :], odd_ref[rows, :]], axis=0)
            out_ref[...] = dot(own, weight_ref[...])


def first_kernel(
    core, where_ref, near_ref, far_ref, degree_ref, self_ref, weight_ref, down_ref, mine_ref,
    other_ref, up_mine_ref, up_other_ref, made_ref, tail_ref,
):
    refs = (down_ref, mine_ref, other_ref, up_mine_ref, up_other_ref)

    @pl.when(at(where_ref, 0, core))
    def _():
        summed = dot(near_ref[...], staged_rows(core, core, refs))
        summed = summed + dot(far_ref[...], staged_rows(core, 1 - core, refs))
        made = finish(summed, degree_ref, self_ref, weight_ref)
        made_ref[...] = made
        tail_ref[...] = made[BLOCK:]


def history_kernel(
    where_ref, far_ref, down_ref, mine_ref, other_ref, up_mine_ref, up_other_ref, out_ref
):
    refs = (down_ref, mine_ref, other_ref, up_mine_ref, up_other_ref)

    @pl.when((where_ref[0] > 0) & (where_ref[1] == 0))
    def _():
        out_ref[...] = dot(far_ref[...], staged_rows(0, 1, refs))


def self_kernel(layer, core, where_ref, weight_ref, own_ref, out_ref):
    @pl.when(at(where_ref, layer, core))
    def _():
        out_ref[...] = dot(own_ref[...], weight_ref[...])


def fresh_rows(down_ref, own_ref, up_ref):
    return jnp.concatenate([down_ref[...], own_ref[...], up_ref[...], down_ref[...]], axis=0)


def slab0_kernel(
    layer, where_ref, near_ref, lend_ref, degree_ref, self_ref, base_ref, weight_ref, down_ref,
    own_ref, up_ref, made_ref, tail_ref, lent_ref,
):
    @pl.when(at(where_ref, layer, 0))
    def _():
        rows = fresh_rows(down_ref, own_ref, up_ref)
        summed = dot(near_ref[...], rows) + base_ref[...]
        made = finish(summed, degree_ref, self_ref, weight_ref)
        made_ref[...] = made
        tail_ref[...] = made[BLOCK:]
        lent_ref[...] = dot(lend_ref[...], rows)


def slab1_kernel(
    layer, where_ref, near_ref, degree_ref, self_ref, base_ref, weight_ref, down_ref, own_ref,
    up_ref, made_ref, tail_ref,
):
    @pl.when(at(where_ref, layer, 1))
    def _():
        rows = fresh_rows(down_ref, own_ref, up_ref)
        summed = dot(near_ref[...], rows) + base_ref[...]
        made = finish(summed, degree_ref, self_ref, weight_ref)
        made_ref[...] = made
        tail_ref[...] = made[BLOCK:]


def last_kernel(
    layer, where_ref, near_ref, degree_ref, self_ref, base_ref, weight_ref, down_ref, own_ref,
    up_ref, *refs,
):
    done, (home_ref, away_ref) = refs[:-2], refs[-2:]
    for earlier in range(layer + 1):
        for core in range(2):
            if (earlier, core) == (layer, 1):
                continue
            ref = done[2 * earlier + core]

            @pl.when(at(where_ref, earlier, core))
            def _():
                home_ref[...] = ref[pl.ds(core * BLOCK, BLOCK), :]
                away_ref[...] = ref[pl.ds((1 - core) * BLOCK, BLOCK), :]

    @pl.when(at(where_ref, layer, 1))
    def _():
        rows = fresh_rows(down_ref, own_ref, up_ref)
        summed = dot(near_ref[...], rows) + base_ref[...]
        made = finish(summed, degree_ref, self_ref, weight_ref)
        home_ref[...] = made[BLOCK:]
        away_ref[...] = made[:BLOCK]


def leave_kernel(where_ref, home_ref, arrived_ref, result_ref, sems):
    for core in range(2):

        @pl.when(where_ref[1] == core)
        def _():
            copies = [
                pltpu.make_async_copy(
                    ref, result_ref.at[pl.ds(slab * BLOCK, BLOCK), :], sems.at[slab]
                )
                for slab, ref in ((core, home_ref), (1 - core, arrived_ref))
            ]
            for copy in copies:
                copy.start()
            for copy in copies:
                copy.wait()


def call(kernel, outs, *args, label, **extra):
    options = dict(compiler_params=params(), cost_estimate=COST, name=label)
    options.update(extra)
    specs = [SMEM if a.dtype == jnp.int32 and a.size < 128 else VMEM for a in args]
    options.setdefault("out_specs", [VMEM] * len(outs))
    return pl.pallas_call(kernel, out_shape=outs, in_specs=specs, **options)(*args)


def per_device(stacked, edges, picks, self_w, neigh_w):
    layers, domains = lax.axis_size("section"), lax.axis_size("dom")
    width = stacked.shape[2]
    mine = stacked[0]
    weight_self, weight_neigh = self_w[0], neigh_w[0]
    where = jnp.stack([lax.axis_index("section"), lax.axis_index("dom") % 2]).astype(jnp.int32)

    def bf16(rows, columns=width):
        return jax.ShapeDtypeStruct((rows, columns), jnp.bfloat16)

    def f32(rows, columns=width):
        return jax.ShapeDtypeStruct((rows, columns), jnp.float32)

    def route(value, jump, cores, sections, hop, label):
        pairs = [
            (s * domains + (d + jump(d)) % domains, (s + hop) * domains + d)
            for s in sections
            for d in range(domains)
            if d % 2 in cores
        ]
        with jax.named_scope(label):
            return lax.ppermute(value, ("section", "dom"), pairs)

    def steady(jump):
        return lambda d: jump

    def partner(d):
        return 1 if d % 2 == 0 else -1

    every = range(layers)
    both = (0, 1)
    up_mine = route(mine, steady(2), both, every, 0, "init_up")
    down_even = route(mine, steady(-1), (0,), every, 0, "init_down")
    other = route(mine, partner, both, every, 0, "init_other")
    (tiles,) = call(tiles_kernel, [bf16(ROWS, 8 * BLOCK)], picks, edges, label="tiles")
    tiles_other = route(tiles, partner, both, every, 0, "init_tiles")
    near, far, lend, degree = call(
        weave_kernel,
        [bf16(ROWS, SPAN)] * 3 + [f32(ROWS, 128)],
        where, tiles, tiles_other,
        label="weave",
    )
    (part,) = call(first_self_kernel, [f32(ROWS)], where, weight_self, mine, other, label="self0")
    up_other = route(up_mine, partner, both, every, 0, "init_up_other")
    down_odd = route(down_even, partner, (1,), [0], 0, "init_down_odd")
    made, tail = [], []
    for core in range(2):
        m, t = call(
            functools.partial(first_kernel, core),
            [bf16(ROWS), bf16(BLOCK)],
            where, near, far, degree, part, weight_neigh,
            down_odd if core else down_even, mine, other, up_mine, up_other,
            label="first",
        )
        made.append(m)
        tail.append(t)
    (base,) = call(
        history_kernel, [f32(ROWS)], where, far, down_even, mine, other, up_mine, up_other,
        label="history",
    )
    done = list(made)
    for layer in range(1, layers):
        fresh = []
        for core in range(2):
            cores, ends = (core,), [layer - 1]
            own = route(made[core], steady(0), cores, ends, 1, f"own_l{layer}c{core}")
            up = route(made[core], steady(2), cores, ends, 1, f"up_l{layer}c{core}")
            down = route(tail[core], steady(-2), cores, ends, 1, f"down_l{layer}c{core}")
            with jax.named_scope(f"self_l{layer}c{core}"):
                (part,) = call(
                    functools.partial(self_kernel, layer, core), [f32(ROWS)],
                    where, weight_self, own, label="self",
                )
            fresh.append((part, down, own, up))
        part, down, own, up = fresh[0]
        with jax.named_scope(f"slab0_l{layer}"):
            m0, t0, lent = call(
                functools.partial(slab0_kernel, layer),
                [bf16(ROWS), bf16(BLOCK), f32(ROWS)],
                where, near, lend, degree, part, base, weight_neigh, down, own, up,
                label="slab0",
            )
        lent = route(lent, partner, (1,), [layer], 0, f"lent_l{layer}")
        part, down, own, up = fresh[1]
        inputs = (where, near, degree, part, lent, weight_neigh, down, own, up)
        done.append(m0)
        with jax.named_scope(f"slab1_l{layer}"):
            if layer < layers - 1:
                m1, t1 = call(
                    functools.partial(slab1_kernel, layer), [bf16(ROWS), bf16(BLOCK)], *inputs,
                    label="slab1",
                )
                done.append(m1)
                made, tail = [m0, m1], [t0, t1]
            else:
                home, away = call(
                    functools.partial(last_kernel, layer), [bf16(BLOCK)] * 2, *inputs, *done,
                    label="last",
                )
    arrived = route(away, partner, both, every, 0, "last_swap")
    (result,) = call(
        leave_kernel,
        [bf16(ROWS)],
        where, home, arrived,
        label="leave",
        out_specs=[ANY],
        scratch_shapes=[pltpu.SemaphoreType.DMA((2,))],
    )
    return result[None]


def solution(mesh):
    in_specs = (
        P("section", "dom", None),
        P("dom", None),
        P("dom", None),
        P("section", None, None),
        P("section", None, None),
    )
    out_specs = P("section", "dom", None)
    return jax.shard_map(
        per_device, mesh=mesh, in_specs=in_specs, out_specs=out_specs, check_vma=False
    )
```

time: 200 us -> 98.5 us (0.49)
  matrix products: 42.8 us -> 0 us
  starting transfers between devices: 75.1 us -> 43.4 us
  other arithmetic: 14.3 us -> 0.08 us
  local copies, waits for them, and re-layouts: 15.8 us -> 2.56 us
  Pallas kernels: 0 us -> 13.2 us
  loops' own time: 10.5 us -> 0 us
    dot_general x25 -> x0, matrix products: 42.8 us -> none  [the longest x15 17.4 us: tile_term(): jnp.dot(tile_mask.astype(jnp.bfloat16), source_rows, preferred_element_ty...]
    ppermute x23 -> x28, starting transfers between devices: 75.1 us -> 43.4 us  [route(): return lax.ppermute(value, ('section', 'dom'), pairs)]
    pallas_call x0 -> x19, Pallas kernels: none -> 13.2 us  [call(): pl.pallas_call(kernel, out_shape=outs, in_specs=specs, **options)(*args)]
    another operation x1 -> x0, loops' own time: 10.5 us -> none  [per_device(): lax.fori_loop(0, slab_count + lax.axis_size('section') - 1, one_step, ini...]
    dynamic_slice x20 -> x0, local copies, waits for them, and re-layouts: 9.75 us -> none  [the longest x15 9.56 us: chosen(): lax.dynamic_index_in_dim(asked[position], slab_now, 0, keepdims=False)]
    add x5 -> x0, other arithmetic: 9.45 us -> none  [one_step(): degree = degree + jnp.where(live_row[position], counted, 0.0)]
    slice x6 -> x0, local copies, waits for them, and re-layouts: 4.27 us -> none  [the longest x5 3.27 us: one_step(): summed = summed + jnp.where(live_row[position], term, 0.0)]
    lt x5 -> x0, other arithmetic: 3.47 us -> none  [one_step(): lax.dynamic_index_in_dim(picks, slab_now, 0, keepdims=False) < slab_count]
  transfers between devices with their start and end apart: 23 -> 28, of which waited for: 7 -> 3; matrix products, arithmetic and copies ran while one was open for 23% -> 0% of each run, Pallas kernels for 0% -> 10%
where the time goes in v3:
time: 98.5 us; the launch traced here: 97.9 us
  starting transfers between devices  43.4 us (44%)
  waiting for transfers between devices  38.1 us (39%)
  Pallas kernels  13.2 us (13%)
  local copies, waits for them, and re-layouts  2.56 us (3%)
    ppermute x28, starting transfers between devices, route(): return lax.ppermute(value, ('section', 'dom'), pairs)  43.4 us
    ppermute x28, waiting for transfers between devices, route(): return lax.ppermute(value, ('section', 'dom'), pairs)  38.1 us
    pallas_call x19, Pallas kernels, call(): pl.pallas_call(kernel, out_shape=outs, in_specs=specs, **options)(*args)  13.2 us
    unnamed x10, local copies, waits for them, and re-layouts  2.56 us
  transfers between devices with their start and end apart: 28, of which 3 were waited for; matrix products, arithmetic and copies ran while one was open for 0% of the time, Pallas kernels for 10%

profile of v3, /device:TPU:7, one launch (start us, length us, event | category | flops | bytes accessed | tf_op | source)
XLA Modules:
  0.0 97.9 jit_solution(2591686050006265036)
XLA Ops:
  0.0 13.7 %collective-permute-start.4 = (bf16[128,1024]{1,0:T(8,128)(2,1)}, bf16[128,1024]{1,0:T(8,128)(2,1)S(1)}, u32[]{:S(2)}, u32[]{:S(2)}) collective-permute-start(bf16[128,1024]{1,0:T(8,128)(2,1)} %bitcast.14), channel_id=1, source_target_pairs={{2,0},{3,1},{4,2},{5,3},{6,4},{7,5},{8,6},{9,7},{10,8},{11,9},{12,... | collective-permute-start | bytes 786440 | tf_op jit(solution)/shard_map/init_up/ppermute | solution.py:231
  13.7 2.9 %collective-permute-start.1 = (bf16[128,1024]{1,0:T(8,128)(2,1)}, bf16[128,1024]{1,0:T(8,128)(2,1)S(1)}, u32[]{:S(2)}, u32[]{:S(2)}) collective-permute-start(bf16[128,1024]{1,0:T(8,128)(2,1)} %bitcast.15), channel_id=1, source_target_pairs={{1,0},{0,1},{3,2},{2,3},{5,4},{4,5},{7,6},{6,7},{9,8},{8,9},{11,10... | collective-permute-start | bytes 786440 | tf_op jit(solution)/shard_map/init_other/ppermute | solution.py:231
  16.6 0.9 copy-done.3
  18.8 2.1 %collective-permute-start = (bf16[128,512]{1,0:T(8,128)(2,1)S(1)}, bf16[128,512]{1,0:T(8,128)(2,1)S(1)}, u32[]{:S(2)}, u32[]{:S(2)}) collective-permute-start(bf16[128,512]{1,0:T(8,128)(2,1)S(1)} %tiles.1.mine_ref), channel_id=1, source_target_pairs={{1,0},{0,1},{3,2},{2,3},{5,4},{4,5},{7,6},{6,7},{9,8},{8,9},{11,10... | collective-permute-start | bytes 393224 | tf_op jit(solution)/shard_map/init_tiles/ppermute | solution.py:231
  20.9 1.3 %collective-permute-start.2 = (bf16[128,1024]{1,0:T(8,128)(2,1)S(1)}, bf16[128,1024]{1,0:T(8,128)(2,1)S(1)}, u32[]{:S(2)}, u32[]{:S(2)}) collective-permute-start(bf16[128,1024]{1,0:T(8,128)(2,1)S(1)} %bitcast.16), channel_id=1, source_target_pairs={{127,0},{1,2},{3,4},{5,6},{7,8},{9,10},{11,12},{13,14},{15,16},{17... | collective-permute-start | bytes 786440 | tf_op jit(solution)/shard_map/init_down/ppermute | solution.py:231
  22.2 2.4 %collective-permute-start.5 = (bf16[128,1024]{1,0:T(8,128)(2,1)S(1)}, bf16[128,1024]{1,0:T(8,128)(2,1)S(1)}, u32[]{:S(2)}, u32[]{:S(2)}) collective-permute-start(bf16[128,1024]{1,0:T(8,128)(2,1)S(1)} %collective-permute-done.4.up_mine_ref), channel_id=1, source_target_pairs={{1,0},{0,1},{3,2},{2,3},{5,4},{4,5},{7,6},{6,7},{9,8},{8,9},{11,10... | collective-permute-start | bytes 786440 | tf_op jit(solution)/shard_map/init_up_other/ppermute | solution.py:231
  24.7 0.7 weave.1
  26.0 1.0 copy-done
  27.6 0.7 collective-permute-start.7
  28.3 0.7 collective-permute-start.9
  28.9 0.7 collective-permute-start.3
  32.0 0.7 collective-permute-start.14
  32.7 0.7 collective-permute-start.10
  33.4 0.7 collective-permute-start.16
  34.7 0.7 collective-permute-start.6
  36.0 0.7 collective-permute-start.12
  38.5 0.7 collective-permute-start.21
  39.2 0.7 collective-permute-start.17
  40.5 0.7 collective-permute-start.23
  41.8 0.7 collective-permute-start.13
  45.1 1.2 %slab0.5 = (bf16[128,1024]{1,0:T(8,128)(2,1)S(1)}, bf16[64,1024]{1,0:T(8,128)(2,1)}, f32[128,1024]{1,0:T(8,128)S(1)}) custom-call(s32[2]{0:T(128)S(1)} %pad_add_fusion.where_ref, bf16[128,384]{1,0:T(8,128)(2,1)S(1)} %get-tuple-element.27.near_ref, bf16[128,384]{1,0:T(8,128)(2,1)S(1)} %get-tuple-element.31.lend_ref, ...), custom_call_target="tpu_custom_call" | custom-call | flops 1000000000 | tf_op jit(solution)/shard_map/slab0_l3/slab0/pallas_call | solution.py:207
  46.3 1.3 %collective-permute-start.24 = (f32[128,1024]{1,0:T(8,128)S(1)}, f32[128,1024]{1,0:T(8,128)S(1)}, u32[]{:S(2)}, u32[]{:S(2)}) collective-permute-start(f32[128,1024]{1,0:T(8,128)S(1)} %get-tuple-element.44), channel_id=1, source_target_pairs={{384,385},{386,387},{388,389},{390,391},{392,393},{394,395},{396,3... | collective-permute-start | bytes 1572872 | tf_op jit(solution)/shard_map/lent_l3/ppermute | solution.py:231
  48.7 1.3 %collective-permute-start.20 = (bf16[128,1024]{1,0:T(8,128)(2,1)S(1)}, bf16[128,1024]{1,0:T(8,128)(2,1)S(1)}, u32[]{:S(2)}, u32[]{:S(2)}) collective-permute-start(bf16[128,1024]{1,0:T(8,128)(2,1)S(1)} %get-tuple-element.41.refs_5_), channel_id=1, source_target_pairs={{257,385},{259,387},{261,389},{263,391},{265,393},{267,395},{269,3... | collective-permute-start | bytes 786440 | tf_op jit(solution)/shard_map/own_l3c1/ppermute | solution.py:231
  50.0 1.3 %collective-permute-start.26 = (bf16[128,1024]{1,0:T(8,128)(2,1)S(1)}, bf16[128,1024]{1,0:T(8,128)(2,1)S(1)}, u32[]{:S(2)}, u32[]{:S(2)}) collective-permute-start(bf16[128,1024]{1,0:T(8,128)(2,1)S(1)} %get-tuple-element.41.refs_5_), channel_id=1, source_target_pairs={{259,385},{261,387},{263,389},{265,391},{267,393},{269,395},{271,3... | collective-permute-start | bytes 786440 | tf_op jit(solution)/shard_map/up_l3c1/ppermute | solution.py:231
  51.3 1.3 %collective-permute-start.25 = (bf16[64,1024]{1,0:T(8,128)(2,1)S(1)}, bf16[64,1024]{1,0:T(8,128)(2,1)S(1)}, u32[]{:S(2)}, u32[]{:S(2)}) collective-permute-start(bf16[64,1024]{1,0:T(8,128)(2,1)S(1)} %get-tuple-element.45), channel_id=1, source_target_pairs={{383,385},{257,387},{259,389},{261,391},{263,393},{265,395},{267,3... | collective-permute-start | bytes 393224 | tf_op jit(solution)/shard_map/down_l3c1/ppermute | solution.py:231
  52.6 30.7 %collective-permute-done.20.own_ref = bf16[128,1024]{1,0:T(8,128)(2,1)S(1)} collective-permute-done((bf16[128,1024]{1,0:T(8,128)(2,1)S(1)}, bf16[128,1024]{1,0:T(8,128)(2,1)S(1)}, u32[]{:S(2)}, u32[]{:S(2)}) %collective-permute-start.20) | collective-permute-done | bytes 262176 | tf_op jit(solution)/shard_map/own_l3c1/ppermute | solution.py:231
  83.3 1.0 %self.10.self_ref = f32[128,1024]{1,0:T(8,128)S(1)} custom-call(s32[2]{0:T(128)S(1)} %pad_add_fusion.where_ref, bf16[1024,1024]{1,0:T(8,128)(2,1)S(1)} %bitcast.27, bf16[128,1024]{1,0:T(8,128)(2,1)S(1)} %collective-permute-done.20.own_ref), custom_call_target="tpu_custom_call" | custom-call | flops 1000000000 | tf_op jit(solution)/shard_map/self_l3c1/self/pallas_call | solution.py:207
  84.3 6.3 %collective-permute-done.24.base_ref = f32[128,1024]{1,0:T(8,128)S(1)} collective-permute-done((f32[128,1024]{1,0:T(8,128)S(1)}, f32[128,1024]{1,0:T(8,128)S(1)}, u32[]{:S(2)}, u32[]{:S(2)}) %collective-permute-start.24) | collective-permute-done | bytes 524320 | tf_op jit(solution)/shard_map/lent_l3/ppermute | solution.py:231
  90.7 1.2 %last.1 = (bf16[64,1024]{1,0:T(8,128)(2,1)S(1)}, bf16[64,1024]{1,0:T(8,128)(2,1)S(1)}) custom-call(s32[2]{0:T(128)S(1)} %pad_add_fusion.where_ref, bf16[128,384]{1,0:T(8,128)(2,1)S(1)} %get-tuple-element.27.near_ref, f32[128,128]{1,0:T(8,128)S(1)} %get-tuple-element.28.degree_ref, f32[128,1024]{1,0:T(8,128)S(1)} %self.10.self_ref, ...), custom_call_target="tpu_custom_call" | custom-call | flops 1000000000 | tf_op jit(solution)/shard_map/slab1_l3/last/pallas_call | solution.py:207
  91.9 3.8 %collective-permute-start.27 = (bf16[64,1024]{1,0:T(8,128)(2,1)S(1)}, bf16[64,1024]{1,0:T(8,128)(2,1)S(1)}, u32[]{:S(2)}, u32[]{:S(2)}) collective-permute-start(bf16[64,1024]{1,0:T(8,128)(2,1)S(1)} %get-tuple-element.48), channel_id=1, source_target_pairs={{1,0},{0,1},{3,2},{2,3},{5,4},{4,5},{7,6},{6,7},{9,8},{8,9},{11,10... | collective-permute-start | bytes 393224 | tf_op jit(solution)/shard_map/last_swap/ppermute | solution.py:231
  95.7 1.0 collective-permute-done.27.arrived_ref
  96.7 1.3 %leave.1 = bf16[128,1024]{1,0:T(8,128)(2,1)} custom-call(s32[2]{0:T(128)S(1)} %pad_add_fusion.where_ref, bf16[64,1024]{1,0:T(8,128)(2,1)S(1)} %get-tuple-element.47.home_ref, bf16[64,1024]{1,0:T(8,128)(2,1)S(1)} %collective-permute-done.27.arrived_ref), custom_call_target="tpu_custom_call" | custom-call | flops 1000000000 | tf_op jit(solution)/shard_map/leave/pallas_call | solution.py:207
  (54 shorter events, 12.7 us)
Async XLA Ops:
  0.0 20.9 %copy-start.1 = (bf16[1,128,1024]{2,1,0:T(8,128)(2,1)S(1)}, bf16[1,128,1024]{2,1,0:T(8,128)(2,1)}, u32[]{:S(2)}) copy-start(bf16[1,128,1024]{2,1,0:T(8,128)(2,1)} %param.5) | copy-start | bytes 786436
  0.0 22.2 %collective-permute-start.4 = (bf16[128,1024]{1,0:T(8,128)(2,1)}, bf16[128,1024]{1,0:T(8,128)(2,1)S(1)}, u32[]{:S(2)}, u32[]{:S(2)}) collective-permute-start(bf16[128,1024]{1,0:T(8,128)(2,1)} %bitcast.14), channel_id=1, source_target_pairs={{2,0},{3,1},{4,2},{5,3},{6,4},{7,5},{8,6},{9,7},{10,8},{11,9},{12,... | collective-permute-start | bytes 786440 | tf_op jit(solution)/shard_map/init_up/ppermute | solution.py:231
  13.7 11.7 %collective-permute-start.1 = (bf16[128,1024]{1,0:T(8,128)(2,1)}, bf16[128,1024]{1,0:T(8,128)(2,1)S(1)}, u32[]{:S(2)}, u32[]{:S(2)}) collective-permute-start(bf16[128,1024]{1,0:T(8,128)(2,1)} %bitcast.15), channel_id=1, source_target_pairs={{1,0},{0,1},{3,2},{2,3},{5,4},{4,5},{7,6},{6,7},{9,8},{8,9},{11,10... | collective-permute-start | bytes 786440 | tf_op jit(solution)/shard_map/init_other/ppermute | solution.py:231
  16.6 0.9 copy-start.3
  18.8 6.6 %copy-start.2 = (bf16[1,1024,1024]{2,1,0:T(8,128)(2,1)S(1)}, bf16[1,1024,1024]{2,1,0:T(8,128)(2,1)}, u32[]{:S(2)}) copy-start(bf16[1,1024,1024]{2,1,0:T(8,128)(2,1)} %param.8) | copy-start | bytes 6291460
  18.8 5.9 %collective-permute-start = (bf16[128,512]{1,0:T(8,128)(2,1)S(1)}, bf16[128,512]{1,0:T(8,128)(2,1)S(1)}, u32[]{:S(2)}, u32[]{:S(2)}) collective-permute-start(bf16[128,512]{1,0:T(8,128)(2,1)S(1)} %tiles.1.mine_ref), channel_id=1, source_target_pairs={{1,0},{0,1},{3,2},{2,3},{5,4},{4,5},{7,6},{6,7},{9,8},{8,9},{11,10... | collective-permute-start | bytes 393224 | tf_op jit(solution)/shard_map/init_tiles/ppermute | solution.py:231
  20.9 5.1 %collective-permute-start.2 = (bf16[128,1024]{1,0:T(8,128)(2,1)S(1)}, bf16[128,1024]{1,0:T(8,128)(2,1)S(1)}, u32[]{:S(2)}, u32[]{:S(2)}) collective-permute-start(bf16[128,1024]{1,0:T(8,128)(2,1)S(1)} %bitcast.16), channel_id=1, source_target_pairs={{127,0},{1,2},{3,4},{5,6},{7,8},{9,10},{11,12},{13,14},{15,16},{17... | collective-permute-start | bytes 786440 | tf_op jit(solution)/shard_map/init_down/ppermute | solution.py:231
  22.2 3.8 %collective-permute-start.5 = (bf16[128,1024]{1,0:T(8,128)(2,1)S(1)}, bf16[128,1024]{1,0:T(8,128)(2,1)S(1)}, u32[]{:S(2)}, u32[]{:S(2)}) collective-permute-start(bf16[128,1024]{1,0:T(8,128)(2,1)S(1)} %collective-permute-done.4.up_mine_ref), channel_id=1, source_target_pairs={{1,0},{0,1},{3,2},{2,3},{5,4},{4,5},{7,6},{6,7},{9,8},{8,9},{11,10... | collective-permute-start | bytes 786440 | tf_op jit(solution)/shard_map/init_up_other/ppermute | solution.py:231
  25.4 1.6 %copy-start = (bf16[1,1024,1024]{2,1,0:T(8,128)(2,1)S(1)}, bf16[1,1024,1024]{2,1,0:T(8,128)(2,1)}, u32[]{:S(2)}) copy-start(bf16[1,1024,1024]{2,1,0:T(8,128)(2,1)} %param.9) | copy-start | bytes 6291460
  27.6 3.3 %collective-permute-start.7 = (bf16[128,1024]{1,0:T(8,128)(2,1)S(1)}, bf16[128,1024]{1,0:T(8,128)(2,1)S(1)}, u32[]{:S(2)}, u32[]{:S(2)}) collective-permute-start(bf16[128,1024]{1,0:T(8,128)(2,1)S(1)} %get-tuple-element.32.refs_0_), channel_id=1, source_target_pairs={{0,128},{2,130},{4,132},{6,134},{8,136},{10,138},{12,140},{14,142}... | collective-permute-start | bytes 786440 | tf_op jit(solution)/shard_map/own_l1c0/ppermute | solution.py:231
  28.3 3.2 %collective-permute-start.9 = (bf16[128,1024]{1,0:T(8,128)(2,1)S(1)}, bf16[128,1024]{1,0:T(8,128)(2,1)S(1)}, u32[]{:S(2)}, u32[]{:S(2)}) collective-permute-start(bf16[128,1024]{1,0:T(8,128)(2,1)S(1)} %get-tuple-element.32.refs_0_), channel_id=1, source_target_pairs={{2,128},{4,130},{6,132},{8,134},{10,136},{12,138},{14,140},{16,142... | collective-permute-start | bytes 786440 | tf_op jit(solution)/shard_map/up_l1c0/ppermute | solution.py:231
  28.9 5.1 %collective-permute-start.3 = (bf16[128,1024]{1,0:T(8,128)(2,1)S(1)}, bf16[128,1024]{1,0:T(8,128)(2,1)S(1)}, u32[]{:S(2)}, u32[]{:S(2)}) collective-permute-start(bf16[128,1024]{1,0:T(8,128)(2,1)S(1)} %collective-permute-done.2.down_ref), channel_id=1, source_target_pairs={{0,1},{2,3},{4,5},{6,7},{8,9},{10,11},{12,13},{14,15},{16,17},{18,... | collective-permute-start | bytes 786440 | tf_op jit(solution)/shard_map/init_down_odd/ppermute | solution.py:231
  29.6 1.8 %collective-permute-start.8 = (bf16[64,1024]{1,0:T(8,128)(2,1)S(1)}, bf16[64,1024]{1,0:T(8,128)(2,1)S(1)}, u32[]{:S(2)}, u32[]{:S(2)}) collective-permute-start(bf16[64,1024]{1,0:T(8,128)(2,1)S(1)} %get-tuple-element.33), channel_id=1, source_target_pairs={{126,128},{0,130},{2,132},{4,134},{6,136},{8,138},{10,140},{12,142... | collective-permute-start | bytes 393224 | tf_op jit(solution)/shard_map/down_l1c0/ppermute | solution.py:231
  32.0 4.0 %collective-permute-start.14 = (bf16[128,1024]{1,0:T(8,128)(2,1)S(1)}, bf16[128,1024]{1,0:T(8,128)(2,1)S(1)}, u32[]{:S(2)}, u32[]{:S(2)}) collective-permute-start(bf16[128,1024]{1,0:T(8,128)(2,1)S(1)} %get-tuple-element.37.refs_2_), channel_id=1, source_target_pairs={{128,256},{130,258},{132,260},{134,262},{136,264},{138,266},{140,2... | collective-permute-start | bytes 786440 | tf_op jit(solution)/shard_map/own_l2c0/ppermute | solution.py:231
  32.7 8.5 %collective-permute-start.10 = (f32[128,1024]{1,0:T(8,128)S(1)}, f32[128,1024]{1,0:T(8,128)S(1)}, u32[]{:S(2)}, u32[]{:S(2)}) collective-permute-start(f32[128,1024]{1,0:T(8,128)S(1)} %get-tuple-element.34), channel_id=1, source_target_pairs={{128,129},{130,131},{132,133},{134,135},{136,137},{138,139},{140,1... | collective-permute-start | bytes 1572872 | tf_op jit(solution)/shard_map/lent_l1/ppermute | solution.py:231
  33.4 4.6 %collective-permute-start.16 = (bf16[128,1024]{1,0:T(8,128)(2,1)S(1)}, bf16[128,1024]{1,0:T(8,128)(2,1)S(1)}, u32[]{:S(2)}, u32[]{:S(2)}) collective-permute-start(bf16[128,1024]{1,0:T(8,128)(2,1)S(1)} %get-tuple-element.37.refs_2_), channel_id=1, source_target_pairs={{130,256},{132,258},{134,260},{136,262},{138,264},{140,266},{142,2... | collective-permute-start | bytes 786440 | tf_op jit(solution)/shard_map/up_l2c0/ppermute | solution.py:231
  34.7 4.6 %collective-permute-start.6 = (bf16[128,1024]{1,0:T(8,128)(2,1)S(1)}, bf16[128,1024]{1,0:T(8,128)(2,1)S(1)}, u32[]{:S(2)}, u32[]{:S(2)}) collective-permute-start(bf16[128,1024]{1,0:T(8,128)(2,1)S(1)} %get-tuple-element.30.refs_1_), channel_id=1, source_target_pairs={{1,129},{3,131},{5,133},{7,135},{9,137},{11,139},{13,141},{15,143}... | collective-permute-start | bytes 786440 | tf_op jit(solution)/shard_map/own_l1c1/ppermute | solution.py:231
  35.3 1.9 %collective-permute-start.15 = (bf16[64,1024]{1,0:T(8,128)(2,1)S(1)}, bf16[64,1024]{1,0:T(8,128)(2,1)S(1)}, u32[]{:S(2)}, u32[]{:S(2)}) collective-permute-start(bf16[64,1024]{1,0:T(8,128)(2,1)S(1)} %get-tuple-element.38), channel_id=1, source_target_pairs={{254,256},{128,258},{130,260},{132,262},{134,264},{136,266},{138,2... | collective-permute-start | bytes 393224 | tf_op jit(solution)/shard_map/down_l2c0/ppermute | solution.py:231
  36.0 5.2 %collective-permute-start.12 = (bf16[128,1024]{1,0:T(8,128)(2,1)S(1)}, bf16[128,1024]{1,0:T(8,128)(2,1)S(1)}, u32[]{:S(2)}, u32[]{:S(2)}) collective-permute-start(bf16[128,1024]{1,0:T(8,128)(2,1)S(1)} %get-tuple-element.30.refs_1_), channel_id=1, source_target_pairs={{3,129},{5,131},{7,133},{9,135},{11,137},{13,139},{15,141},{17,143... | collective-permute-start | bytes 786440 | tf_op jit(solution)/shard_map/up_l1c1/ppermute | solution.py:231
  37.3 3.2 %collective-permute-start.11 = (bf16[64,1024]{1,0:T(8,128)(2,1)S(1)}, bf16[64,1024]{1,0:T(8,128)(2,1)S(1)}, u32[]{:S(2)}, u32[]{:S(2)}) collective-permute-start(bf16[64,1024]{1,0:T(8,128)(2,1)S(1)} %get-tuple-element.35), channel_id=1, source_target_pairs={{127,129},{1,131},{3,133},{5,135},{7,137},{9,139},{11,141},{13,143... | collective-permute-start | bytes 393224 | tf_op jit(solution)/shard_map/down_l1c1/ppermute | solution.py:231
  38.5 4.6 %collective-permute-start.21 = (bf16[128,1024]{1,0:T(8,128)(2,1)S(1)}, bf16[128,1024]{1,0:T(8,128)(2,1)S(1)}, u32[]{:S(2)}, u32[]{:S(2)}) collective-permute-start(bf16[128,1024]{1,0:T(8,128)(2,1)S(1)} %get-tuple-element.42.refs_4_), channel_id=1, source_target_pairs={{256,384},{258,386},{260,388},{262,390},{264,392},{266,394},{268,3... | collective-permute-start | bytes 786440 | tf_op jit(solution)/shard_map/own_l3c0/ppermute | solution.py:231
  39.2 8.9 %collective-permute-start.17 = (f32[128,1024]{1,0:T(8,128)S(1)}, f32[128,1024]{1,0:T(8,128)S(1)}, u32[]{:S(2)}, u32[]{:S(2)}) collective-permute-start(f32[128,1024]{1,0:T(8,128)S(1)} %get-tuple-element.39), channel_id=1, source_target_pairs={{256,257},{258,259},{260,261},{262,263},{264,265},{266,267},{268,2... | collective-permute-start | bytes 1572872 | tf_op jit(solution)/shard_map/lent_l2/ppermute | solution.py:231
  40.5 4.6 %collective-permute-start.23 = (bf16[128,1024]{1,0:T(8,128)(2,1)S(1)}, bf16[128,1024]{1,0:T(8,128)(2,1)S(1)}, u32[]{:S(2)}, u32[]{:S(2)}) collective-permute-start(bf16[128,1024]{1,0:T(8,128)(2,1)S(1)} %get-tuple-element.42.refs_4_), channel_id=1, source_target_pairs={{258,384},{260,386},{262,388},{264,390},{266,392},{268,394},{270,3... | collective-permute-start | bytes 786440 | tf_op jit(solution)/shard_map/up_l3c0/ppermute | solution.py:231
  41.8 5.8 %collective-permute-start.13 = (bf16[128,1024]{1,0:T(8,128)(2,1)S(1)}, bf16[128,1024]{1,0:T(8,128)(2,1)S(1)}, u32[]{:S(2)}, u32[]{:S(2)}) collective-permute-start(bf16[128,1024]{1,0:T(8,128)(2,1)S(1)} %get-tuple-element.36.refs_3_), channel_id=1, source_target_pairs={{129,257},{131,259},{133,261},{135,263},{137,265},{139,267},{141,2... | collective-permute-start | bytes 786440 | tf_op jit(solution)/shard_map/own_l2c1/ppermute | solution.py:231
  42.4 1.9 %collective-permute-start.22 = (bf16[64,1024]{1,0:T(8,128)(2,1)S(1)}, bf16[64,1024]{1,0:T(8,128)(2,1)S(1)}, u32[]{:S(2)}, u32[]{:S(2)}) collective-permute-start(bf16[64,1024]{1,0:T(8,128)(2,1)S(1)} %get-tuple-element.43), channel_id=1, source_target_pairs={{382,384},{256,386},{258,388},{260,390},{262,392},{264,394},{266,3... | collective-permute-start | bytes 393224 | tf_op jit(solution)/shard_map/down_l3c0/ppermute | solution.py:231
  43.1 5.0 %collective-permute-start.19 = (bf16[128,1024]{1,0:T(8,128)(2,1)S(1)}, bf16[128,1024]{1,0:T(8,128)(2,1)S(1)}, u32[]{:S(2)}, u32[]{:S(2)}) collective-permute-start(bf16[128,1024]{1,0:T(8,128)(2,1)S(1)} %get-tuple-element.36.refs_3_), channel_id=1, source_target_pairs={{131,257},{133,259},{135,261},{137,263},{139,265},{141,267},{143,2... | collective-permute-start | bytes 786440 | tf_op jit(solution)/shard_map/up_l2c1/ppermute | solution.py:231
  44.4 3.8 %collective-permute-start.18 = (bf16[64,1024]{1,0:T(8,128)(2,1)S(1)}, bf16[64,1024]{1,0:T(8,128)(2,1)S(1)}, u32[]{:S(2)}, u32[]{:S(2)}) collective-permute-start(bf16[64,1024]{1,0:T(8,128)(2,1)S(1)} %get-tuple-element.40), channel_id=1, source_target_pairs={{255,257},{129,259},{131,261},{133,263},{135,265},{137,267},{139,2... | collective-permute-start | bytes 393224 | tf_op jit(solution)/shard_map/down_l2c1/ppermute | solution.py:231
  46.3 44.4 %collective-permute-start.24 = (f32[128,1024]{1,0:T(8,128)S(1)}, f32[128,1024]{1,0:T(8,128)S(1)}, u32[]{:S(2)}, u32[]{:S(2)}) collective-permute-start(f32[128,1024]{1,0:T(8,128)S(1)} %get-tuple-element.44), channel_id=1, source_target_pairs={{384,385},{386,387},{388,389},{390,391},{392,393},{394,395},{396,3... | collective-permute-start | bytes 1572872 | tf_op jit(solution)/shard_map/lent_l3/ppermute | solution.py:231
  48.7 34.6 %collective-permute-start.20 = (bf16[128,1024]{1,0:T(8,128)(2,1)S(1)}, bf16[128,1024]{1,0:T(8,128)(2,1)S(1)}, u32[]{:S(2)}, u32[]{:S(2)}) collective-permute-start(bf16[128,1024]{1,0:T(8,128)(2,1)S(1)} %get-tuple-element.41.refs_5_), channel_id=1, source_target_pairs={{257,385},{259,387},{261,389},{263,391},{265,393},{267,395},{269,3... | collective-permute-start | bytes 786440 | tf_op jit(solution)/shard_map/own_l3c1/ppermute | solution.py:231
  50.0 40.6 %collective-permute-start.26 = (bf16[128,1024]{1,0:T(8,128)(2,1)S(1)}, bf16[128,1024]{1,0:T(8,128)(2,1)S(1)}, u32[]{:S(2)}, u32[]{:S(2)}) collective-permute-start(bf16[128,1024]{1,0:T(8,128)(2,1)S(1)} %get-tuple-element.41.refs_5_), channel_id=1, source_target_pairs={{259,385},{261,387},{263,389},{265,391},{267,393},{269,395},{271,3... | collective-permute-start | bytes 786440 | tf_op jit(solution)/shard_map/up_l3c1/ppermute | solution.py:231
  51.3 33.0 %collective-permute-start.25 = (bf16[64,1024]{1,0:T(8,128)(2,1)S(1)}, bf16[64,1024]{1,0:T(8,128)(2,1)S(1)}, u32[]{:S(2)}, u32[]{:S(2)}) collective-permute-start(bf16[64,1024]{1,0:T(8,128)(2,1)S(1)} %get-tuple-element.45), channel_id=1, source_target_pairs={{383,385},{257,387},{259,389},{261,391},{263,393},{265,395},{267,3... | collective-permute-start | bytes 393224 | tf_op jit(solution)/shard_map/down_l3c1/ppermute | solution.py:231
  91.9 4.7 %collective-permute-start.27 = (bf16[64,1024]{1,0:T(8,128)(2,1)S(1)}, bf16[64,1024]{1,0:T(8,128)(2,1)S(1)}, u32[]{:S(2)}, u32[]{:S(2)}) collective-permute-start(bf16[64,1024]{1,0:T(8,128)(2,1)S(1)} %get-tuple-element.48), channel_id=1, source_target_pairs={{1,0},{0,1},{3,2},{2,3},{5,4},{4,5},{7,6},{6,7},{9,8},{8,9},{11,10... | collective-permute-start | bytes 393224 | tf_op jit(solution)/shard_map/last_swap/ppermute | solution.py:231
  (1 other events, 0.7 us)

commit v4 on v3

--- a/solution.py
+++ b/solution.py
@@ -267,21 +267,23 @@
         history_kernel, [f32(ROWS)], where, far, down_even, mine, other, up_mine, up_other,
         label="history",
     )
+    def send(rows, last_block, layer, core):
+        cores, ends = (core,), [layer - 1]
+        own = route(rows, steady(0), cores, ends, 1, f"own_l{layer}c{core}")
+        up = route(rows, steady(2), cores, ends, 1, f"up_l{layer}c{core}")
+        down = route(last_block, steady(-2), cores, ends, 1, f"down_l{layer}c{core}")
+        return own, up, down
+
     done = list(made)
+    tail[0], _ = lax.optimization_barrier((tail[0], down_odd))
+    moving = [send(made[core], tail[core], 1, core) for core in range(2)]
     for layer in range(1, layers):
-        fresh = []
-        for core in range(2):
-            cores, ends = (core,), [layer - 1]
-            own = route(made[core], steady(0), cores, ends, 1, f"own_l{layer}c{core}")
-            up = route(made[core], steady(2), cores, ends, 1, f"up_l{layer}c{core}")
-            down = route(tail[core], steady(-2), cores, ends, 1, f"down_l{layer}c{core}")
-            with jax.named_scope(f"self_l{layer}c{core}"):
-                (part,) = call(
-                    functools.partial(self_kernel, layer, core), [f32(ROWS)],
-                    where, weight_self, own, label="self",
-                )
-            fresh.append((part, down, own, up))
-        part, down, own, up = fresh[0]
+        (own, up, down), (own1, up1, down1) = moving
+        with jax.named_scope(f"self_l{layer}c0"):
+            (part,) = call(
+                functools.partial(self_kernel, layer, 0), [f32(ROWS)], where, weight_self, own,
+                label="self",
+            )
         with jax.named_scope(f"slab0_l{layer}"):
             m0, t0, lent = call(
                 functools.partial(slab0_kernel, layer),
@@ -289,10 +291,17 @@
                 where, near, lend, degree, part, base, weight_neigh, down, own, up,
                 label="slab0",
             )
+        done.append(m0)
+        if layer < layers - 1:
+            ahead = send(m0, t0, layer + 1, 0)
+            lent, *ahead = lax.optimization_barrier((lent, *ahead))
         lent = route(lent, partner, (1,), [layer], 0, f"lent_l{layer}")
-        part, down, own, up = fresh[1]
-        inputs = (where, near, degree, part, lent, weight_neigh, down, own, up)
-        done.append(m0)
+        with jax.named_scope(f"self_l{layer}c1"):
+            (part,) = call(
+                functools.partial(self_kernel, layer, 1), [f32(ROWS)], where, weight_self, own1,
+                label="self",
+            )
+        inputs = (where, near, degree, part, lent, weight_neigh, down1, own1, up1)
         with jax.named_scope(f"slab1_l{layer}"):
             if layer < layers - 1:
                 m1, t1 = call(
@@ -300,7 +309,7 @@
                     label="slab1",
                 )
                 done.append(m1)
-                made, tail = [m0, m1], [t0, t1]
+                moving = [ahead, send(m1, t1, layer + 1, 1)]
             else:
                 home, away = call(
                     functools.partial(last_kernel, layer), [bf16(BLOCK)] * 2, *inputs, *done,

time: 98.5 us -> 87.9 us (0.89)
  waiting for transfers between devices: 38.1 us -> 30.2 us
  starting transfers between devices: 43.4 us -> 41.6 us
    ppermute x28, waiting for transfers between devices: 38.1 us -> 30.2 us  [route(): return lax.ppermute(value, ('section', 'dom'), pairs)]
    ppermute x28, starting transfers between devices: 43.4 us -> 41.6 us  [route(): return lax.ppermute(value, ('section', 'dom'), pairs)]
  transfers between devices with their start and end apart: 28 -> 28, of which waited for: 3 -> 3; matrix products, arithmetic and copies ran while one was open for 0% -> 0% of each run, Pallas kernels for 10% -> 12%
where the time goes in v4:
time: 87.9 us; the launch traced here: 87.4 us
  starting transfers between devices  41.6 us (47%)
  waiting for transfers between devices  30.2 us (34%)
  Pallas kernels  13.2 us (15%)
  local copies, waits for them, and re-layouts  1.74 us (2%)
    ppermute x28, starting transfers between devices, route(): return lax.ppermute(value, ('section', 'dom'), pairs)  41.6 us
    ppermute x28, waiting for transfers between devices, route(): return lax.ppermute(value, ('section', 'dom'), pairs)  30.2 us
    pallas_call x19, Pallas kernels, call(): pl.pallas_call(kernel, out_shape=outs, in_specs=specs, **options)(*args)  13.2 us
  transfers between devices with their start and end apart: 28, of which 3 were waited for; matrix products, arithmetic and copies ran while one was open for 0% of the time, Pallas kernels for 12%

profile of v4, /device:TPU:7, one launch (start us, length us, event | category | flops | bytes accessed | tf_op | source)
XLA Modules:
  0.0 87.4 jit_solution(7381679261173271607)
XLA Ops:
  0.0 13.6 %collective-permute-start.4 = (bf16[128,1024]{1,0:T(8,128)(2,1)}, bf16[128,1024]{1,0:T(8,128)(2,1)S(1)}, u32[]{:S(2)}, u32[]{:S(2)}) collective-permute-start(bf16[128,1024]{1,0:T(8,128)(2,1)} %bitcast.14), channel_id=1, source_target_pairs={{2,0},{3,1},{4,2},{5,3},{6,4},{7,5},{8,6},{9,7},{10,8},{11,9},{12,... | collective-permute-start | bytes 786440 | tf_op jit(solution)/shard_map/init_up/ppermute | solution.py:231
  13.6 2.9 %collective-permute-start.1 = (bf16[128,1024]{1,0:T(8,128)(2,1)}, bf16[128,1024]{1,0:T(8,128)(2,1)S(1)}, u32[]{:S(2)}, u32[]{:S(2)}) collective-permute-start(bf16[128,1024]{1,0:T(8,128)(2,1)} %bitcast.15), channel_id=1, source_target_pairs={{1,0},{0,1},{3,2},{2,3},{5,4},{4,5},{7,6},{6,7},{9,8},{8,9},{11,10... | collective-permute-start | bytes 786440 | tf_op jit(solution)/shard_map/init_other/ppermute | solution.py:231
  16.4 1.3 %collective-permute-start.2 = (bf16[128,1024]{1,0:T(8,128)(2,1)}, bf16[128,1024]{1,0:T(8,128)(2,1)S(1)}, u32[]{:S(2)}, u32[]{:S(2)}) collective-permute-start(bf16[128,1024]{1,0:T(8,128)(2,1)} %bitcast.16), channel_id=1, source_target_pairs={{127,0},{1,2},{3,4},{5,6},{7,8},{9,10},{11,12},{13,14},{15,16},{17... | collective-permute-start | bytes 786440 | tf_op jit(solution)/shard_map/init_down/ppermute | solution.py:231
  17.8 0.9 %copy-done.3 = s32[128,256]{1,0:T(8,128)S(1)} copy-done((s32[128,256]{1,0:T(8,128)S(1)}, s32[128,256]{1,0:T(8,128)}, u32[]{:S(2)}) %copy-start.3) | copy-done | bytes 131096
  20.0 2.1 %collective-permute-start = (bf16[128,512]{1,0:T(8,128)(2,1)S(1)}, bf16[128,512]{1,0:T(8,128)(2,1)S(1)}, u32[]{:S(2)}, u32[]{:S(2)}) collective-permute-start(bf16[128,512]{1,0:T(8,128)(2,1)S(1)} %tiles.1.mine_ref), channel_id=1, source_target_pairs={{1,0},{0,1},{3,2},{2,3},{5,4},{4,5},{7,6},{6,7},{9,8},{8,9},{11,10... | collective-permute-start | bytes 393224 | tf_op jit(solution)/shard_map/init_tiles/ppermute | solution.py:231
  22.1 2.4 %collective-permute-start.5 = (bf16[128,1024]{1,0:T(8,128)(2,1)S(1)}, bf16[128,1024]{1,0:T(8,128)(2,1)S(1)}, u32[]{:S(2)}, u32[]{:S(2)}) collective-permute-start(bf16[128,1024]{1,0:T(8,128)(2,1)S(1)} %collective-permute-done.4.up_mine_ref), channel_id=1, source_target_pairs={{1,0},{0,1},{3,2},{2,3},{5,4},{4,5},{7,6},{6,7},{9,8},{8,9},{11,10... | collective-permute-start | bytes 786440 | tf_op jit(solution)/shard_map/init_up_other/ppermute | solution.py:231
  24.6 0.7 weave.1
  25.3 0.8 collective-permute-start.3
  27.5 0.7 collective-permute-start.7
  28.1 0.7 collective-permute-start.9
  31.2 0.7 collective-permute-start.10
  31.9 0.7 collective-permute-start.11
  33.3 0.7 collective-permute-start.13
  35.1 0.7 collective-permute-start.17
  35.8 0.7 collective-permute-start.18
  37.7 0.7 collective-permute-start.6
  38.4 0.7 collective-permute-start.15
  39.8 0.7 collective-permute-start.20
  41.7 0.7 collective-permute-start.16
  42.4 0.7 collective-permute-start.22
  44.3 1.2 %slab0.5 = (bf16[128,1024]{1,0:T(8,128)(2,1)S(1)}, bf16[64,1024]{1,0:T(8,128)(2,1)}, f32[128,1024]{1,0:T(8,128)S(1)}) custom-call(s32[2]{0:T(128)S(1)} %pad_add_fusion.where_ref, bf16[128,384]{1,0:T(8,128)(2,1)S(1)} %get-tuple-element.36.near_ref, bf16[128,384]{1,0:T(8,128)(2,1)S(1)} %get-tuple-element.40.lend_ref, ...), custom_call_target="tpu_custom_call" | custom-call | flops 1000000000 | tf_op jit(solution)/shard_map/slab0_l3/slab0/pallas_call | solution.py:207
  45.5 1.3 %collective-permute-start.24 = (f32[128,1024]{1,0:T(8,128)S(1)}, f32[128,1024]{1,0:T(8,128)S(1)}, u32[]{:S(2)}, u32[]{:S(2)}) collective-permute-start(f32[128,1024]{1,0:T(8,128)S(1)} %get-tuple-element.62), channel_id=1, source_target_pairs={{384,385},{386,387},{388,389},{390,391},{392,393},{394,395},{396,3... | collective-permute-start | bytes 1572872 | tf_op jit(solution)/shard_map/lent_l3/ppermute | solution.py:231
  47.9 1.3 %collective-permute-start.23 = (bf16[128,1024]{1,0:T(8,128)(2,1)S(1)}, bf16[128,1024]{1,0:T(8,128)(2,1)S(1)}, u32[]{:S(2)}, u32[]{:S(2)}) collective-permute-start(bf16[128,1024]{1,0:T(8,128)(2,1)S(1)} %get-tuple-element.58.refs_5_), channel_id=1, source_target_pairs={{257,385},{259,387},{261,389},{263,391},{265,393},{267,395},{269,3... | collective-permute-start | bytes 786440 | tf_op jit(solution)/shard_map/slab1_l2/own_l3c1/ppermute | solution.py:231
  49.2 1.3 %collective-permute-start.26 = (bf16[128,1024]{1,0:T(8,128)(2,1)S(1)}, bf16[128,1024]{1,0:T(8,128)(2,1)S(1)}, u32[]{:S(2)}, u32[]{:S(2)}) collective-permute-start(bf16[128,1024]{1,0:T(8,128)(2,1)S(1)} %get-tuple-element.58.refs_5_), channel_id=1, source_target_pairs={{259,385},{261,387},{263,389},{265,391},{267,393},{269,395},{271,3... | collective-permute-start | bytes 786440 | tf_op jit(solution)/shard_map/slab1_l2/up_l3c1/ppermute | solution.py:231
  50.5 1.3 %collective-permute-start.25 = (bf16[64,1024]{1,0:T(8,128)(2,1)S(1)}, bf16[64,1024]{1,0:T(8,128)(2,1)S(1)}, u32[]{:S(2)}, u32[]{:S(2)}) collective-permute-start(bf16[64,1024]{1,0:T(8,128)(2,1)S(1)} %get-tuple-element.63), channel_id=1, source_target_pairs={{383,385},{257,387},{259,389},{261,391},{263,393},{265,395},{267,3... | collective-permute-start | bytes 393224 | tf_op jit(solution)/shard_map/slab1_l2/down_l3c1/ppermute | solution.py:231
  51.8 27.0 %collective-permute-done.23.own_ref = bf16[128,1024]{1,0:T(8,128)(2,1)S(1)} collective-permute-done((bf16[128,1024]{1,0:T(8,128)(2,1)S(1)}, bf16[128,1024]{1,0:T(8,128)(2,1)S(1)}, u32[]{:S(2)}, u32[]{:S(2)}) %collective-permute-start.23) | collective-permute-done | bytes 262176 | tf_op jit(solution)/shard_map/slab1_l2/own_l3c1/ppermute | solution.py:231
  78.9 1.0 %self.10.self_ref = f32[128,1024]{1,0:T(8,128)S(1)} custom-call(s32[2]{0:T(128)S(1)} %pad_add_fusion.where_ref, bf16[1024,1024]{1,0:T(8,128)(2,1)S(1)} %bitcast.27, bf16[128,1024]{1,0:T(8,128)(2,1)S(1)} %collective-permute-done.23.own_ref), custom_call_target="tpu_custom_call" | custom-call | flops 1000000000 | tf_op jit(solution)/shard_map/self_l3c1/self/pallas_call | solution.py:207
  79.9 1.8 %collective-permute-done.25.down_ref = bf16[64,1024]{1,0:T(8,128)(2,1)S(1)} collective-permute-done((bf16[64,1024]{1,0:T(8,128)(2,1)S(1)}, bf16[64,1024]{1,0:T(8,128)(2,1)S(1)}, u32[]{:S(2)}, u32[]{:S(2)}) %collective-permute-start.25) | collective-permute-done | bytes 131104 | tf_op jit(solution)/shard_map/slab1_l2/down_l3c1/ppermute | solution.py:231
  81.7 1.2 %last.1 = (bf16[64,1024]{1,0:T(8,128)(2,1)S(1)}, bf16[64,1024]{1,0:T(8,128)(2,1)S(1)}) custom-call(s32[2]{0:T(128)S(1)} %pad_add_fusion.where_ref, bf16[128,384]{1,0:T(8,128)(2,1)S(1)} %get-tuple-element.36.near_ref, f32[128,128]{1,0:T(8,128)S(1)} %get-tuple-element.37.degree_ref, f32[128,1024]{1,0:T(8,128)S(1)} %self.10.self_ref, ...), custom_call_target="tpu_custom_call" | custom-call | flops 1000000000 | tf_op jit(solution)/shard_map/slab1_l3/last/pallas_call | solution.py:207
  82.9 1.9 %collective-permute-start.27 = (bf16[64,1024]{1,0:T(8,128)(2,1)S(1)}, bf16[64,1024]{1,0:T(8,128)(2,1)S(1)}, u32[]{:S(2)}, u32[]{:S(2)}) collective-permute-start(bf16[64,1024]{1,0:T(8,128)(2,1)S(1)} %get-tuple-element.66), channel_id=1, source_target_pairs={{1,0},{0,1},{3,2},{2,3},{5,4},{4,5},{7,6},{6,7},{9,8},{8,9},{11,10... | collective-permute-start | bytes 393224 | tf_op jit(solution)/shard_map/last_swap/ppermute | solution.py:231
  84.8 1.3 %collective-permute-done.27.arrived_ref = bf16[64,1024]{1,0:T(8,128)(2,1)S(1)} collective-permute-done((bf16[64,1024]{1,0:T(8,128)(2,1)S(1)}, bf16[64,1024]{1,0:T(8,128)(2,1)S(1)}, u32[]{:S(2)}, u32[]{:S(2)}) %collective-permute-start.27) | collective-permute-done | bytes 131104 | tf_op jit(solution)/shard_map/last_swap/ppermute | solution.py:231
  86.1 1.3 %leave.1 = bf16[128,1024]{1,0:T(8,128)(2,1)} custom-call(s32[2]{0:T(128)S(1)} %pad_add_fusion.where_ref, bf16[64,1024]{1,0:T(8,128)(2,1)S(1)} %get-tuple-element.65.home_ref, bf16[64,1024]{1,0:T(8,128)(2,1)S(1)} %collective-permute-done.27.arrived_ref), custom_call_target="tpu_custom_call" | custom-call | flops 1000000000 | tf_op jit(solution)/shard_map/leave/pallas_call | solution.py:207
  (54 shorter events, 12.2 us)
Async XLA Ops:
  0.0 22.1 %collective-permute-start.4 = (bf16[128,1024]{1,0:T(8,128)(2,1)}, bf16[128,1024]{1,0:T(8,128)(2,1)S(1)}, u32[]{:S(2)}, u32[]{:S(2)}) collective-permute-start(bf16[128,1024]{1,0:T(8,128)(2,1)} %bitcast.14), channel_id=1, source_target_pairs={{2,0},{3,1},{4,2},{5,3},{6,4},{7,5},{8,6},{9,7},{10,8},{11,9},{12,... | collective-permute-start | bytes 786440 | tf_op jit(solution)/shard_map/init_up/ppermute | solution.py:231
  13.6 12.6 %collective-permute-start.1 = (bf16[128,1024]{1,0:T(8,128)(2,1)}, bf16[128,1024]{1,0:T(8,128)(2,1)S(1)}, u32[]{:S(2)}, u32[]{:S(2)}) collective-permute-start(bf16[128,1024]{1,0:T(8,128)(2,1)} %bitcast.15), channel_id=1, source_target_pairs={{1,0},{0,1},{3,2},{2,3},{5,4},{4,5},{7,6},{6,7},{9,8},{8,9},{11,10... | collective-permute-start | bytes 786440 | tf_op jit(solution)/shard_map/init_other/ppermute | solution.py:231
  16.4 8.9 %collective-permute-start.2 = (bf16[128,1024]{1,0:T(8,128)(2,1)}, bf16[128,1024]{1,0:T(8,128)(2,1)S(1)}, u32[]{:S(2)}, u32[]{:S(2)}) collective-permute-start(bf16[128,1024]{1,0:T(8,128)(2,1)} %bitcast.16), channel_id=1, source_target_pairs={{127,0},{1,2},{3,4},{5,6},{7,8},{9,10},{11,12},{13,14},{15,16},{17... | collective-permute-start | bytes 786440 | tf_op jit(solution)/shard_map/init_down/ppermute | solution.py:231
  17.8 0.9 %copy-start.3 = (s32[128,256]{1,0:T(8,128)S(1)}, s32[128,256]{1,0:T(8,128)}, u32[]{:S(2)}) copy-start(s32[128,256]{1,0:T(8,128)} %edges_ref.1) | copy-start | bytes 393220
  20.0 6.2 %copy-start.1 = (bf16[1,128,1024]{2,1,0:T(8,128)(2,1)S(1)}, bf16[1,128,1024]{2,1,0:T(8,128)(2,1)}, u32[]{:S(2)}) copy-start(bf16[1,128,1024]{2,1,0:T(8,128)(2,1)} %param.5) | copy-start | bytes 786436
  20.0 6.2 %copy-start.2 = (bf16[1,1024,1024]{2,1,0:T(8,128)(2,1)S(1)}, bf16[1,1024,1024]{2,1,0:T(8,128)(2,1)}, u32[]{:S(2)}) copy-start(bf16[1,1024,1024]{2,1,0:T(8,128)(2,1)} %param.8) | copy-start | bytes 6291460
  20.0 4.6 %collective-permute-start = (bf16[128,512]{1,0:T(8,128)(2,1)S(1)}, bf16[128,512]{1,0:T(8,128)(2,1)S(1)}, u32[]{:S(2)}, u32[]{:S(2)}) collective-permute-start(bf16[128,512]{1,0:T(8,128)(2,1)S(1)} %tiles.1.mine_ref), channel_id=1, source_target_pairs={{1,0},{0,1},{3,2},{2,3},{5,4},{4,5},{7,6},{6,7},{9,8},{8,9},{11,10... | collective-permute-start | bytes 393224 | tf_op jit(solution)/shard_map/init_tiles/ppermute | solution.py:231
  22.1 4.6 %collective-permute-start.5 = (bf16[128,1024]{1,0:T(8,128)(2,1)S(1)}, bf16[128,1024]{1,0:T(8,128)(2,1)S(1)}, u32[]{:S(2)}, u32[]{:S(2)}) collective-permute-start(bf16[128,1024]{1,0:T(8,128)(2,1)S(1)} %collective-permute-done.4.up_mine_ref), channel_id=1, source_target_pairs={{1,0},{0,1},{3,2},{2,3},{5,4},{4,5},{7,6},{6,7},{9,8},{8,9},{11,10... | collective-permute-start | bytes 786440 | tf_op jit(solution)/shard_map/init_up_other/ppermute | solution.py:231
  25.3 1.6 %copy-start = (bf16[1,1024,1024]{2,1,0:T(8,128)(2,1)S(1)}, bf16[1,1024,1024]{2,1,0:T(8,128)(2,1)}, u32[]{:S(2)}) copy-start(bf16[1,1024,1024]{2,1,0:T(8,128)(2,1)} %param.9) | copy-start | bytes 6291460
  25.3 3.5 %collective-permute-start.3 = (bf16[128,1024]{1,0:T(8,128)(2,1)S(1)}, bf16[128,1024]{1,0:T(8,128)(2,1)S(1)}, u32[]{:S(2)}, u32[]{:S(2)}) collective-permute-start(bf16[128,1024]{1,0:T(8,128)(2,1)S(1)} %collective-permute-done.2.down_ref), channel_id=1, source_target_pairs={{0,1},{2,3},{4,5},{6,7},{8,9},{10,11},{12,13},{14,15},{16,17},{18,... | collective-permute-start | bytes 786440 | tf_op jit(solution)/shard_map/init_down_odd/ppermute | solution.py:231
  27.5 2.6 %collective-permute-start.7 = (bf16[128,1024]{1,0:T(8,128)(2,1)S(1)}, bf16[128,1024]{1,0:T(8,128)(2,1)S(1)}, u32[]{:S(2)}, u32[]{:S(2)}) collective-permute-start(bf16[128,1024]{1,0:T(8,128)(2,1)S(1)} %get-tuple-element.41.refs_0_), channel_id=1, source_target_pairs={{0,128},{2,130},{4,132},{6,134},{8,136},{10,138},{12,140},{14,142}... | collective-permute-start | bytes 786440 | tf_op jit(solution)/shard_map/own_l1c0/ppermute | solution.py:231
  28.1 2.5 %collective-permute-start.9 = (bf16[128,1024]{1,0:T(8,128)(2,1)S(1)}, bf16[128,1024]{1,0:T(8,128)(2,1)S(1)}, u32[]{:S(2)}, u32[]{:S(2)}) collective-permute-start(bf16[128,1024]{1,0:T(8,128)(2,1)S(1)} %get-tuple-element.41.refs_0_), channel_id=1, source_target_pairs={{2,128},{4,130},{6,132},{8,134},{10,136},{12,138},{14,140},{16,142... | collective-permute-start | bytes 786440 | tf_op jit(solution)/shard_map/up_l1c0/ppermute | solution.py:231
  28.8 1.8 %collective-permute-start.8 = (bf16[64,1024]{1,0:T(8,128)(2,1)S(1)}, bf16[64,1024]{1,0:T(8,128)(2,1)S(1)}, u32[]{:S(2)}, u32[]{:S(2)}) collective-permute-start(bf16[64,1024]{1,0:T(8,128)(2,1)S(1)} %get-tuple-element.43), channel_id=1, source_target_pairs={{126,128},{0,130},{2,132},{4,134},{6,136},{8,138},{10,140},{12,142... | collective-permute-start | bytes 393224 | tf_op jit(solution)/shard_map/down_l1c0/ppermute | solution.py:231
  31.2 2.1 %collective-permute-start.10 = (bf16[128,1024]{1,0:T(8,128)(2,1)S(1)}, bf16[128,1024]{1,0:T(8,128)(2,1)S(1)}, u32[]{:S(2)}, u32[]{:S(2)}) collective-permute-start(bf16[128,1024]{1,0:T(8,128)(2,1)S(1)} %get-tuple-element.45.refs_2_), channel_id=1, source_target_pairs={{128,256},{130,258},{132,260},{134,262},{136,264},{138,266},{140,2... | collective-permute-start | bytes 786440 | tf_op jit(solution)/shard_map/own_l2c0/ppermute | solution.py:231
  31.9 1.4 %collective-permute-start.11 = (bf16[128,1024]{1,0:T(8,128)(2,1)S(1)}, bf16[128,1024]{1,0:T(8,128)(2,1)S(1)}, u32[]{:S(2)}, u32[]{:S(2)}) collective-permute-start(bf16[128,1024]{1,0:T(8,128)(2,1)S(1)} %get-tuple-element.45.refs_2_), channel_id=1, source_target_pairs={{130,256},{132,258},{134,260},{136,262},{138,264},{140,266},{142,2... | collective-permute-start | bytes 786440 | tf_op jit(solution)/shard_map/up_l2c0/ppermute | solution.py:231
  32.6 0.7 collective-permute-start.12
  33.3 7.8 %collective-permute-start.13 = (f32[128,1024]{1,0:T(8,128)S(1)}, f32[128,1024]{1,0:T(8,128)S(1)}, u32[]{:S(2)}, u32[]{:S(2)}) collective-permute-start(f32[128,1024]{1,0:T(8,128)S(1)} %get-tuple-element.47), channel_id=1, source_target_pairs={{128,129},{130,131},{132,133},{134,135},{136,137},{138,139},{140,1... | collective-permute-start | bytes 1572872 | tf_op jit(solution)/shard_map/lent_l1/ppermute | solution.py:231
  35.1 4.0 %collective-permute-start.17 = (bf16[128,1024]{1,0:T(8,128)(2,1)S(1)}, bf16[128,1024]{1,0:T(8,128)(2,1)S(1)}, u32[]{:S(2)}, u32[]{:S(2)}) collective-permute-start(bf16[128,1024]{1,0:T(8,128)(2,1)S(1)} %get-tuple-element.54.refs_4_), channel_id=1, source_target_pairs={{256,384},{258,386},{260,388},{262,390},{264,392},{266,394},{268,3... | collective-permute-start | bytes 786440 | tf_op jit(solution)/shard_map/own_l3c0/ppermute | solution.py:231
  35.8 4.0 %collective-permute-start.18 = (bf16[128,1024]{1,0:T(8,128)(2,1)S(1)}, bf16[128,1024]{1,0:T(8,128)(2,1)S(1)}, u32[]{:S(2)}, u32[]{:S(2)}) collective-permute-start(bf16[128,1024]{1,0:T(8,128)(2,1)S(1)} %get-tuple-element.54.refs_4_), channel_id=1, source_target_pairs={{258,384},{260,386},{262,388},{264,390},{266,392},{268,394},{270,3... | collective-permute-start | bytes 786440 | tf_op jit(solution)/shard_map/up_l3c0/ppermute | solution.py:231
  36.5 1.9 %collective-permute-start.19 = (bf16[64,1024]{1,0:T(8,128)(2,1)S(1)}, bf16[64,1024]{1,0:T(8,128)(2,1)S(1)}, u32[]{:S(2)}, u32[]{:S(2)}) collective-permute-start(bf16[64,1024]{1,0:T(8,128)(2,1)S(1)} %get-tuple-element.55), channel_id=1, source_target_pairs={{382,384},{256,386},{258,388},{260,390},{262,392},{264,394},{266,3... | collective-permute-start | bytes 393224 | tf_op jit(solution)/shard_map/down_l3c0/ppermute | solution.py:231
  37.7 2.8 %collective-permute-start.6 = (bf16[128,1024]{1,0:T(8,128)(2,1)S(1)}, bf16[128,1024]{1,0:T(8,128)(2,1)S(1)}, u32[]{:S(2)}, u32[]{:S(2)}) collective-permute-start(bf16[128,1024]{1,0:T(8,128)(2,1)S(1)} %get-tuple-element.39.refs_1_), channel_id=1, source_target_pairs={{1,129},{3,131},{5,133},{7,135},{9,137},{11,139},{13,141},{15,143}... | collective-permute-start | bytes 786440 | tf_op jit(solution)/shard_map/own_l1c1/ppermute | solution.py:231
  38.4 2.7 %collective-permute-start.15 = (bf16[128,1024]{1,0:T(8,128)(2,1)S(1)}, bf16[128,1024]{1,0:T(8,128)(2,1)S(1)}, u32[]{:S(2)}, u32[]{:S(2)}) collective-permute-start(bf16[128,1024]{1,0:T(8,128)(2,1)S(1)} %get-tuple-element.39.refs_1_), channel_id=1, source_target_pairs={{3,129},{5,131},{7,133},{9,135},{11,137},{13,139},{15,141},{17,143... | collective-permute-start | bytes 786440 | tf_op jit(solution)/shard_map/up_l1c1/ppermute | solution.py:231
  39.1 2.0 %collective-permute-start.14 = (bf16[64,1024]{1,0:T(8,128)(2,1)S(1)}, bf16[64,1024]{1,0:T(8,128)(2,1)S(1)}, u32[]{:S(2)}, u32[]{:S(2)}) collective-permute-start(bf16[64,1024]{1,0:T(8,128)(2,1)S(1)} %get-tuple-element.48), channel_id=1, source_target_pairs={{127,129},{1,131},{3,133},{5,135},{7,137},{9,139},{11,141},{13,143... | collective-permute-start | bytes 393224 | tf_op jit(solution)/shard_map/down_l1c1/ppermute | solution.py:231
  39.8 7.6 %collective-permute-start.20 = (f32[128,1024]{1,0:T(8,128)S(1)}, f32[128,1024]{1,0:T(8,128)S(1)}, u32[]{:S(2)}, u32[]{:S(2)}) collective-permute-start(f32[128,1024]{1,0:T(8,128)S(1)} %get-tuple-element.56), channel_id=1, source_target_pairs={{256,257},{258,259},{260,261},{262,263},{264,265},{266,267},{268,2... | collective-permute-start | bytes 1572872 | tf_op jit(solution)/shard_map/lent_l2/ppermute | solution.py:231
  41.7 5.1 %collective-permute-start.16 = (bf16[128,1024]{1,0:T(8,128)(2,1)S(1)}, bf16[128,1024]{1,0:T(8,128)(2,1)S(1)}, u32[]{:S(2)}, u32[]{:S(2)}) collective-permute-start(bf16[128,1024]{1,0:T(8,128)(2,1)S(1)} %get-tuple-element.49.refs_3_), channel_id=1, source_target_pairs={{129,257},{131,259},{133,261},{135,263},{137,265},{139,267},{141,2... | collective-permute-start | bytes 786440 | tf_op jit(solution)/shard_map/slab1_l1/own_l2c1/ppermute | solution.py:231
  42.4 5.0 %collective-permute-start.22 = (bf16[128,1024]{1,0:T(8,128)(2,1)S(1)}, bf16[128,1024]{1,0:T(8,128)(2,1)S(1)}, u32[]{:S(2)}, u32[]{:S(2)}) collective-permute-start(bf16[128,1024]{1,0:T(8,128)(2,1)S(1)} %get-tuple-element.49.refs_3_), channel_id=1, source_target_pairs={{131,257},{133,259},{135,261},{137,263},{139,265},{141,267},{143,2... | collective-permute-start | bytes 786440 | tf_op jit(solution)/shard_map/slab1_l1/up_l2c1/ppermute | solution.py:231
  43.6 3.7 %collective-permute-start.21 = (bf16[64,1024]{1,0:T(8,128)(2,1)S(1)}, bf16[64,1024]{1,0:T(8,128)(2,1)S(1)}, u32[]{:S(2)}, u32[]{:S(2)}) collective-permute-start(bf16[64,1024]{1,0:T(8,128)(2,1)S(1)} %get-tuple-element.57), channel_id=1, source_target_pairs={{255,257},{129,259},{131,261},{133,263},{135,265},{137,267},{139,2... | collective-permute-start | bytes 393224 | tf_op jit(solution)/shard_map/slab1_l1/down_l2c1/ppermute | solution.py:231
  45.5 34.4 %collective-permute-start.24 = (f32[128,1024]{1,0:T(8,128)S(1)}, f32[128,1024]{1,0:T(8,128)S(1)}, u32[]{:S(2)}, u32[]{:S(2)}) collective-permute-start(f32[128,1024]{1,0:T(8,128)S(1)} %get-tuple-element.62), channel_id=1, source_target_pairs={{384,385},{386,387},{388,389},{390,391},{392,393},{394,395},{396,3... | collective-permute-start | bytes 1572872 | tf_op jit(solution)/shard_map/lent_l3/ppermute | solution.py:231
  47.9 30.9 %collective-permute-start.23 = (bf16[128,1024]{1,0:T(8,128)(2,1)S(1)}, bf16[128,1024]{1,0:T(8,128)(2,1)S(1)}, u32[]{:S(2)}, u32[]{:S(2)}) collective-permute-start(bf16[128,1024]{1,0:T(8,128)(2,1)S(1)} %get-tuple-element.58.refs_5_), channel_id=1, source_target_pairs={{257,385},{259,387},{261,389},{263,391},{265,393},{267,395},{269,3... | collective-permute-start | bytes 786440 | tf_op jit(solution)/shard_map/slab1_l2/own_l3c1/ppermute | solution.py:231
  49.2 32.4 %collective-permute-start.26 = (bf16[128,1024]{1,0:T(8,128)(2,1)S(1)}, bf16[128,1024]{1,0:T(8,128)(2,1)S(1)}, u32[]{:S(2)}, u32[]{:S(2)}) collective-permute-start(bf16[128,1024]{1,0:T(8,128)(2,1)S(1)} %get-tuple-element.58.refs_5_), channel_id=1, source_target_pairs={{259,385},{261,387},{263,389},{265,391},{267,393},{269,395},{271,3... | collective-permute-start | bytes 786440 | tf_op jit(solution)/shard_map/slab1_l2/up_l3c1/ppermute | solution.py:231
  50.5 31.1 %collective-permute-start.25 = (bf16[64,1024]{1,0:T(8,128)(2,1)S(1)}, bf16[64,1024]{1,0:T(8,128)(2,1)S(1)}, u32[]{:S(2)}, u32[]{:S(2)}) collective-permute-start(bf16[64,1024]{1,0:T(8,128)(2,1)S(1)} %get-tuple-element.63), channel_id=1, source_target_pairs={{383,385},{257,387},{259,389},{261,391},{263,393},{265,395},{267,3... | collective-permute-start | bytes 393224 | tf_op jit(solution)/shard_map/slab1_l2/down_l3c1/ppermute | solution.py:231
  82.9 3.2 %collective-permute-start.27 = (bf16[64,1024]{1,0:T(8,128)(2,1)S(1)}, bf16[64,1024]{1,0:T(8,128)(2,1)S(1)}, u32[]{:S(2)}, u32[]{:S(2)}) collective-permute-start(bf16[64,1024]{1,0:T(8,128)(2,1)S(1)} %get-tuple-element.66), channel_id=1, source_target_pairs={{1,0},{0,1},{3,2},{2,3},{5,4},{4,5},{7,6},{6,7},{9,8},{8,9},{11,10... | collective-permute-start | bytes 393224 | tf_op jit(solution)/shard_map/last_swap/ppermute | solution.py:231
  (1 other events, 0.7 us)

commit v5 on v4

--- a/solution.py
+++ b/solution.py
@@ -12,7 +12,6 @@
 SPAN = 6 * BLOCK
 VMEM = pl.BlockSpec(memory_space=pltpu.VMEM)
 SMEM = pl.BlockSpec(memory_space=pltpu.SMEM)
-ANY = pl.BlockSpec(memory_space=pl.ANY)
 COST = pl.CostEstimate(flops=1_000_000_000, bytes_accessed=0, transcendentals=0)
 
 
@@ -182,23 +181,6 @@
         away_ref[...] = made[:BLOCK]
 
 
-def leave_kernel(where_ref, home_ref, arrived_ref, result_ref, sems):
-    for core in range(2):
-
-        @pl.when(where_ref[1] == core)
-        def _():
-            copies = [
-                pltpu.make_async_copy(
-                    ref, result_ref.at[pl.ds(slab * BLOCK, BLOCK), :], sems.at[slab]
-                )
-                for slab, ref in ((core, home_ref), (1 - core, arrived_ref))
-            ]
-            for copy in copies:
-                copy.start()
-            for copy in copies:
-                copy.wait()
-
-
 def call(kernel, outs, *args, label, **extra):
     options = dict(compiler_params=params(), cost_estimate=COST, name=label)
     options.update(extra)
@@ -240,8 +222,9 @@
     both = (0, 1)
     up_mine = route(mine, steady(2), both, every, 0, "init_up")
     down_even = route(mine, steady(-1), (0,), every, 0, "init_down")
-    other = route(mine, partner, both, every, 0, "init_other")
     (tiles,) = call(tiles_kernel, [bf16(ROWS, 8 * BLOCK)], picks, edges, label="tiles")
+    held, tiles = lax.optimization_barrier((mine, tiles))
+    other = route(held, partner, both, every, 0, "init_other")
     tiles_other = route(tiles, partner, both, every, 0, "init_tiles")
     near, far, lend, degree = call(
         weave_kernel,
@@ -294,7 +277,8 @@
         done.append(m0)
         if layer < layers - 1:
             ahead = send(m0, t0, layer + 1, 0)
-            lent, *ahead = lax.optimization_barrier((lent, *ahead))
+            if layer > 1:
+                lent, *ahead = lax.optimization_barrier((lent, *ahead))
         lent = route(lent, partner, (1,), [layer], 0, f"lent_l{layer}")
         with jax.named_scope(f"self_l{layer}c1"):
             (part,) = call(
@@ -316,14 +300,9 @@
                     label="last",
                 )
     arrived = route(away, partner, both, every, 0, "last_swap")
-    (result,) = call(
-        leave_kernel,
-        [bf16(ROWS)],
-        where, home, arrived,
-        label="leave",
-        out_specs=[ANY],
-        scratch_shapes=[pltpu.SemaphoreType.DMA((2,))],
-    )
+    even = where[1] == 0
+    rows = [jnp.where(even, home, arrived), jnp.where(even, arrived, home)]
+    result = jnp.concatenate(rows, axis=0)
     return result[None]
 
 

time: 87.9 us -> 86.9 us (0.989)
  Pallas kernels: 13.2 us -> 11.9 us
    pallas_call x19 -> x18, Pallas kernels: 13.2 us -> 11.9 us  [call(): pl.pallas_call(kernel, out_shape=outs, in_specs=specs, **options)(*args)]
  transfers between devices with their start and end apart: 28 -> 28, of which waited for: 3 -> 4; matrix products, arithmetic and copies ran while one was open for 0% -> 0% of each run, Pallas kernels for 12% -> 12%
where the time goes in v5:
time: 86.9 us; the launch traced here: 86.3 us
  starting transfers between devices  41.7 us (48%)
  waiting for transfers between devices  29.5 us (34%)
  Pallas kernels  11.9 us (14%)
  local copies, waits for them, and re-layouts  1.75 us (2%)
    ppermute x28, starting transfers between devices, route(): return lax.ppermute(value, ('section', 'dom'), pairs)  41.7 us
    ppermute x28, waiting for transfers between devices, route(): return lax.ppermute(value, ('section', 'dom'), pairs)  29.5 us
    pallas_call x18, Pallas kernels, call(): pl.pallas_call(kernel, out_shape=outs, in_specs=specs, **options)(*args)  11.9 us
    unnamed x10, local copies, waits for them, and re-layouts  1.75 us
  transfers between devices with their start and end apart: 28, of which 4 were waited for; matrix products, arithmetic and copies ran while one was open for 0% of the time, Pallas kernels for 12%

profile of v5, /device:TPU:7, one launch (start us, length us, event | category | flops | bytes accessed | tf_op | source)
XLA Modules:
  0.0 86.3 jit_solution(9487333368417962896)
XLA Ops:
  0.0 13.7 %collective-permute-start.4 = (bf16[128,1024]{1,0:T(8,128)(2,1)}, bf16[128,1024]{1,0:T(8,128)(2,1)S(1)}, u32[]{:S(2)}, u32[]{:S(2)}) collective-permute-start(bf16[128,1024]{1,0:T(8,128)(2,1)} %bitcast.15), channel_id=1, source_target_pairs={{2,0},{3,1},{4,2},{5,3},{6,4},{7,5},{8,6},{9,7},{10,8},{11,9},{12,... | collective-permute-start | bytes 786440 | tf_op jit(solution)/shard_map/init_up/ppermute | solution.py:213
  13.7 1.3 %collective-permute-start.2 = (bf16[128,1024]{1,0:T(8,128)(2,1)}, bf16[128,1024]{1,0:T(8,128)(2,1)S(1)}, u32[]{:S(2)}, u32[]{:S(2)}) collective-permute-start(bf16[128,1024]{1,0:T(8,128)(2,1)} %bitcast.16), channel_id=1, source_target_pairs={{127,0},{1,2},{3,4},{5,6},{7,8},{9,10},{11,12},{13,14},{15,16},{17... | collective-permute-start | bytes 786440 | tf_op jit(solution)/shard_map/init_down/ppermute | solution.py:213
  15.0 0.9 %copy-done.3 = s32[128,256]{1,0:T(8,128)S(1)} copy-done((s32[128,256]{1,0:T(8,128)S(1)}, s32[128,256]{1,0:T(8,128)}, u32[]{:S(2)}) %copy-start.3) | copy-done | bytes 131096
  17.3 3.0 %collective-permute-start.1 = (bf16[128,1024]{1,0:T(8,128)(2,1)S(1)}, bf16[128,1024]{1,0:T(8,128)(2,1)S(1)}, u32[]{:S(2)}, u32[]{:S(2)}) collective-permute-start(bf16[128,1024]{1,0:T(8,128)(2,1)S(1)} %bitcast.17), channel_id=1, source_target_pairs={{1,0},{0,1},{3,2},{2,3},{5,4},{4,5},{7,6},{6,7},{9,8},{8,9},{11,10... | collective-permute-start | bytes 786440 | tf_op jit(solution)/shard_map/init_other/ppermute | solution.py:213
  20.3 1.9 %collective-permute-start = (bf16[128,512]{1,0:T(8,128)(2,1)S(1)}, bf16[128,512]{1,0:T(8,128)(2,1)S(1)}, u32[]{:S(2)}, u32[]{:S(2)}) collective-permute-start(bf16[128,512]{1,0:T(8,128)(2,1)S(1)} %tiles.1.mine_ref), channel_id=1, source_target_pairs={{1,0},{0,1},{3,2},{2,3},{5,4},{4,5},{7,6},{6,7},{9,8},{8,9},{11,10... | collective-permute-start | bytes 393224 | tf_op jit(solution)/shard_map/init_tiles/ppermute | solution.py:213
  22.2 2.4 %collective-permute-start.5 = (bf16[128,1024]{1,0:T(8,128)(2,1)S(1)}, bf16[128,1024]{1,0:T(8,128)(2,1)S(1)}, u32[]{:S(2)}, u32[]{:S(2)}) collective-permute-start(bf16[128,1024]{1,0:T(8,128)(2,1)S(1)} %collective-permute-done.4.up_mine_ref), channel_id=1, source_target_pairs={{1,0},{0,1},{3,2},{2,3},{5,4},{4,5},{7,6},{6,7},{9,8},{8,9},{11,10... | collective-permute-start | bytes 786440 | tf_op jit(solution)/shard_map/init_up_other/ppermute | solution.py:213
  24.7 0.7 weave.1
  25.4 0.8 collective-permute-start.3
  27.6 0.7 collective-permute-start.7
  28.3 0.7 collective-permute-start.9
  31.3 0.7 collective-permute-start.14
  32.0 0.7 collective-permute-start.16
  33.4 0.7 collective-permute-start.10
  35.2 0.7 collective-permute-start.17
  35.9 0.7 collective-permute-start.18
  37.8 0.7 collective-permute-start.6
  38.5 0.7 collective-permute-start.12
  39.9 0.7 collective-permute-start.20
  41.8 0.7 collective-permute-start.13
  44.4 1.2 %slab0.5 = (bf16[128,1024]{1,0:T(8,128)(2,1)S(1)}, bf16[64,1024]{1,0:T(8,128)(2,1)}, f32[128,1024]{1,0:T(8,128)S(1)}) custom-call(s32[2]{0:T(128)S(1)} %pad_add_fusion.where_ref, bf16[128,384]{1,0:T(8,128)(2,1)S(1)} %get-tuple-element.35.near_ref, bf16[128,384]{1,0:T(8,128)(2,1)S(1)} %get-tuple-element.40.lend_ref, ...), custom_call_target="tpu_custom_call" | custom-call | flops 1000000000 | tf_op jit(solution)/shard_map/slab0_l3/slab0/pallas_call | solution.py:189
  45.6 1.3 %collective-permute-start.24 = (f32[128,1024]{1,0:T(8,128)S(1)}, f32[128,1024]{1,0:T(8,128)S(1)}, u32[]{:S(2)}, u32[]{:S(2)}) collective-permute-start(f32[128,1024]{1,0:T(8,128)S(1)} %get-tuple-element.58), channel_id=1, source_target_pairs={{384,385},{386,387},{388,389},{390,391},{392,393},{394,395},{396,3... | collective-permute-start | bytes 1572872 | tf_op jit(solution)/shard_map/lent_l3/ppermute | solution.py:213
  48.0 1.3 %collective-permute-start.23 = (bf16[128,1024]{1,0:T(8,128)(2,1)S(1)}, bf16[128,1024]{1,0:T(8,128)(2,1)S(1)}, u32[]{:S(2)}, u32[]{:S(2)}) collective-permute-start(bf16[128,1024]{1,0:T(8,128)(2,1)S(1)} %get-tuple-element.54.refs_5_), channel_id=1, source_target_pairs={{257,385},{259,387},{261,389},{263,391},{265,393},{267,395},{269,3... | collective-permute-start | bytes 786440 | tf_op jit(solution)/shard_map/slab1_l2/own_l3c1/ppermute | solution.py:213
  49.4 1.3 %collective-permute-start.26 = (bf16[128,1024]{1,0:T(8,128)(2,1)S(1)}, bf16[128,1024]{1,0:T(8,128)(2,1)S(1)}, u32[]{:S(2)}, u32[]{:S(2)}) collective-permute-start(bf16[128,1024]{1,0:T(8,128)(2,1)S(1)} %get-tuple-element.54.refs_5_), channel_id=1, source_target_pairs={{259,385},{261,387},{263,389},{265,391},{267,393},{269,395},{271,3... | collective-permute-start | bytes 786440 | tf_op jit(solution)/shard_map/slab1_l2/up_l3c1/ppermute | solution.py:213
  50.6 1.3 %collective-permute-start.25 = (bf16[64,1024]{1,0:T(8,128)(2,1)S(1)}, bf16[64,1024]{1,0:T(8,128)(2,1)S(1)}, u32[]{:S(2)}, u32[]{:S(2)}) collective-permute-start(bf16[64,1024]{1,0:T(8,128)(2,1)S(1)} %get-tuple-element.59), channel_id=1, source_target_pairs={{383,385},{257,387},{259,389},{261,391},{263,393},{265,395},{267,3... | collective-permute-start | bytes 393224 | tf_op jit(solution)/shard_map/slab1_l2/down_l3c1/ppermute | solution.py:213
  52.0 24.0 %collective-permute-done.23.own_ref = bf16[128,1024]{1,0:T(8,128)(2,1)S(1)} collective-permute-done((bf16[128,1024]{1,0:T(8,128)(2,1)S(1)}, bf16[128,1024]{1,0:T(8,128)(2,1)S(1)}, u32[]{:S(2)}, u32[]{:S(2)}) %collective-permute-start.23) | collective-permute-done | bytes 262176 | tf_op jit(solution)/shard_map/slab1_l2/own_l3c1/ppermute | solution.py:213
  75.9 1.0 %self.10.self_ref = f32[128,1024]{1,0:T(8,128)S(1)} custom-call(s32[2]{0:T(128)S(1)} %pad_add_fusion.where_ref, bf16[1024,1024]{1,0:T(8,128)(2,1)S(1)} %bitcast.28, bf16[128,1024]{1,0:T(8,128)(2,1)S(1)} %collective-permute-done.23.own_ref), custom_call_target="tpu_custom_call" | custom-call | flops 1000000000 | tf_op jit(solution)/shard_map/self_l3c1/self/pallas_call | solution.py:189
  76.9 2.1 %collective-permute-done.24.base_ref = f32[128,1024]{1,0:T(8,128)S(1)} collective-permute-done((f32[128,1024]{1,0:T(8,128)S(1)}, f32[128,1024]{1,0:T(8,128)S(1)}, u32[]{:S(2)}, u32[]{:S(2)}) %collective-permute-start.24) | collective-permute-done | bytes 524320 | tf_op jit(solution)/shard_map/lent_l3/ppermute | solution.py:213
  79.0 2.1 %collective-permute-done.25.down_ref = bf16[64,1024]{1,0:T(8,128)(2,1)S(1)} collective-permute-done((bf16[64,1024]{1,0:T(8,128)(2,1)S(1)}, bf16[64,1024]{1,0:T(8,128)(2,1)S(1)}, u32[]{:S(2)}, u32[]{:S(2)}) %collective-permute-start.25) | collective-permute-done | bytes 131104 | tf_op jit(solution)/shard_map/slab1_l2/down_l3c1/ppermute | solution.py:213
  81.1 1.2 %last.1 = (bf16[64,1024]{1,0:T(8,128)(2,1)S(1)}, bf16[64,1024]{1,0:T(8,128)(2,1)S(1)}) custom-call(s32[2]{0:T(128)S(1)} %pad_add_fusion.where_ref, bf16[128,384]{1,0:T(8,128)(2,1)S(1)} %get-tuple-element.35.near_ref, f32[128,128]{1,0:T(8,128)S(1)} %get-tuple-element.36.degree_ref, f32[128,1024]{1,0:T(8,128)S(1)} %self.10.self_ref, ...), custom_call_target="tpu_custom_call" | custom-call | flops 1000000000 | tf_op jit(solution)/shard_map/slab1_l3/last/pallas_call | solution.py:189
  82.4 1.9 %collective-permute-start.27 = (bf16[64,1024]{1,0:T(8,128)(2,1)S(1)}, bf16[64,1024]{1,0:T(8,128)(2,1)S(1)}, u32[]{:S(2)}, u32[]{:S(2)}) collective-permute-start(bf16[64,1024]{1,0:T(8,128)(2,1)S(1)} %get-tuple-element.62), channel_id=1, source_target_pairs={{1,0},{0,1},{3,2},{2,3},{5,4},{4,5},{7,6},{6,7},{9,8},{8,9},{11,10... | collective-permute-start | bytes 393224 | tf_op jit(solution)/shard_map/last_swap/ppermute | solution.py:213
  84.3 1.3 %collective-permute-done.27 = bf16[64,1024]{1,0:T(8,128)(2,1)S(1)} collective-permute-done((bf16[64,1024]{1,0:T(8,128)(2,1)S(1)}, bf16[64,1024]{1,0:T(8,128)(2,1)S(1)}, u32[]{:S(2)}, u32[]{:S(2)}) %collective-permute-start.27) | collective-permute-done | bytes 131104 | tf_op jit(solution)/shard_map/last_swap/ppermute | solution.py:213
  85.6 0.7 maximum_bitcast_fusion
  (55 shorter events, 12.9 us)
Async XLA Ops:
  0.0 17.3 %copy-start.1 = (bf16[1,128,1024]{2,1,0:T(8,128)(2,1)S(1)}, bf16[1,128,1024]{2,1,0:T(8,128)(2,1)}, u32[]{:S(2)}) copy-start(bf16[1,128,1024]{2,1,0:T(8,128)(2,1)} %param.5) | copy-start | bytes 786436
  0.0 22.2 %collective-permute-start.4 = (bf16[128,1024]{1,0:T(8,128)(2,1)}, bf16[128,1024]{1,0:T(8,128)(2,1)S(1)}, u32[]{:S(2)}, u32[]{:S(2)}) collective-permute-start(bf16[128,1024]{1,0:T(8,128)(2,1)} %bitcast.15), channel_id=1, source_target_pairs={{2,0},{3,1},{4,2},{5,3},{6,4},{7,5},{8,6},{9,7},{10,8},{11,9},{12,... | collective-permute-start | bytes 786440 | tf_op jit(solution)/shard_map/init_up/ppermute | solution.py:213
  13.7 11.7 %collective-permute-start.2 = (bf16[128,1024]{1,0:T(8,128)(2,1)}, bf16[128,1024]{1,0:T(8,128)(2,1)S(1)}, u32[]{:S(2)}, u32[]{:S(2)}) collective-permute-start(bf16[128,1024]{1,0:T(8,128)(2,1)} %bitcast.16), channel_id=1, source_target_pairs={{127,0},{1,2},{3,4},{5,6},{7,8},{9,10},{11,12},{13,14},{15,16},{17... | collective-permute-start | bytes 786440 | tf_op jit(solution)/shard_map/init_down/ppermute | solution.py:213
  15.0 0.9 %copy-start.3 = (s32[128,256]{1,0:T(8,128)S(1)}, s32[128,256]{1,0:T(8,128)}, u32[]{:S(2)}) copy-start(s32[128,256]{1,0:T(8,128)} %edges_ref.1) | copy-start | bytes 393220
  17.3 9.0 %copy-start.2 = (bf16[1,1024,1024]{2,1,0:T(8,128)(2,1)S(1)}, bf16[1,1024,1024]{2,1,0:T(8,128)(2,1)}, u32[]{:S(2)}) copy-start(bf16[1,1024,1024]{2,1,0:T(8,128)(2,1)} %param.8) | copy-start | bytes 6291460
  17.3 9.0 %collective-permute-start.1 = (bf16[128,1024]{1,0:T(8,128)(2,1)S(1)}, bf16[128,1024]{1,0:T(8,128)(2,1)S(1)}, u32[]{:S(2)}, u32[]{:S(2)}) collective-permute-start(bf16[128,1024]{1,0:T(8,128)(2,1)S(1)} %bitcast.17), channel_id=1, source_target_pairs={{1,0},{0,1},{3,2},{2,3},{5,4},{4,5},{7,6},{6,7},{9,8},{8,9},{11,10... | collective-permute-start | bytes 786440 | tf_op jit(solution)/shard_map/init_other/ppermute | solution.py:213
  20.3 4.4 %collective-permute-start = (bf16[128,512]{1,0:T(8,128)(2,1)S(1)}, bf16[128,512]{1,0:T(8,128)(2,1)S(1)}, u32[]{:S(2)}, u32[]{:S(2)}) collective-permute-start(bf16[128,512]{1,0:T(8,128)(2,1)S(1)} %tiles.1.mine_ref), channel_id=1, source_target_pairs={{1,0},{0,1},{3,2},{2,3},{5,4},{4,5},{7,6},{6,7},{9,8},{8,9},{11,10... | collective-permute-start | bytes 393224 | tf_op jit(solution)/shard_map/init_tiles/ppermute | solution.py:213
  22.2 4.6 %collective-permute-start.5 = (bf16[128,1024]{1,0:T(8,128)(2,1)S(1)}, bf16[128,1024]{1,0:T(8,128)(2,1)S(1)}, u32[]{:S(2)}, u32[]{:S(2)}) collective-permute-start(bf16[128,1024]{1,0:T(8,128)(2,1)S(1)} %collective-permute-done.4.up_mine_ref), channel_id=1, source_target_pairs={{1,0},{0,1},{3,2},{2,3},{5,4},{4,5},{7,6},{6,7},{9,8},{8,9},{11,10... | collective-permute-start | bytes 786440 | tf_op jit(solution)/shard_map/init_up_other/ppermute | solution.py:213
  25.4 1.6 %copy-start = (bf16[1,1024,1024]{2,1,0:T(8,128)(2,1)S(1)}, bf16[1,1024,1024]{2,1,0:T(8,128)(2,1)}, u32[]{:S(2)}) copy-start(bf16[1,1024,1024]{2,1,0:T(8,128)(2,1)} %param.9) | copy-start | bytes 6291460
  25.4 3.5 %collective-permute-start.3 = (bf16[128,1024]{1,0:T(8,128)(2,1)S(1)}, bf16[128,1024]{1,0:T(8,128)(2,1)S(1)}, u32[]{:S(2)}, u32[]{:S(2)}) collective-permute-start(bf16[128,1024]{1,0:T(8,128)(2,1)S(1)} %collective-permute-done.2.down_ref), channel_id=1, source_target_pairs={{0,1},{2,3},{4,5},{6,7},{8,9},{10,11},{12,13},{14,15},{16,17},{18,... | collective-permute-start | bytes 786440 | tf_op jit(solution)/shard_map/init_down_odd/ppermute | solution.py:213
  27.6 2.6 %collective-permute-start.7 = (bf16[128,1024]{1,0:T(8,128)(2,1)S(1)}, bf16[128,1024]{1,0:T(8,128)(2,1)S(1)}, u32[]{:S(2)}, u32[]{:S(2)}) collective-permute-start(bf16[128,1024]{1,0:T(8,128)(2,1)S(1)} %get-tuple-element.41.refs_0_), channel_id=1, source_target_pairs={{0,128},{2,130},{4,132},{6,134},{8,136},{10,138},{12,140},{14,142}... | collective-permute-start | bytes 786440 | tf_op jit(solution)/shard_map/own_l1c0/ppermute | solution.py:213
  28.3 2.5 %collective-permute-start.9 = (bf16[128,1024]{1,0:T(8,128)(2,1)S(1)}, bf16[128,1024]{1,0:T(8,128)(2,1)S(1)}, u32[]{:S(2)}, u32[]{:S(2)}) collective-permute-start(bf16[128,1024]{1,0:T(8,128)(2,1)S(1)} %get-tuple-element.41.refs_0_), channel_id=1, source_target_pairs={{2,128},{4,130},{6,132},{8,134},{10,136},{12,138},{14,140},{16,142... | collective-permute-start | bytes 786440 | tf_op jit(solution)/shard_map/up_l1c0/ppermute | solution.py:213
  29.0 1.8 %collective-permute-start.8 = (bf16[64,1024]{1,0:T(8,128)(2,1)S(1)}, bf16[64,1024]{1,0:T(8,128)(2,1)S(1)}, u32[]{:S(2)}, u32[]{:S(2)}) collective-permute-start(bf16[64,1024]{1,0:T(8,128)(2,1)S(1)} %get-tuple-element.43), channel_id=1, source_target_pairs={{126,128},{0,130},{2,132},{4,134},{6,136},{8,138},{10,140},{12,142... | collective-permute-start | bytes 393224 | tf_op jit(solution)/shard_map/down_l1c0/ppermute | solution.py:213
  31.3 2.8 %collective-permute-start.14 = (bf16[128,1024]{1,0:T(8,128)(2,1)S(1)}, bf16[128,1024]{1,0:T(8,128)(2,1)S(1)}, u32[]{:S(2)}, u32[]{:S(2)}) collective-permute-start(bf16[128,1024]{1,0:T(8,128)(2,1)S(1)} %get-tuple-element.47.refs_2_), channel_id=1, source_target_pairs={{128,256},{130,258},{132,260},{134,262},{136,264},{138,266},{140,2... | collective-permute-start | bytes 786440 | tf_op jit(solution)/shard_map/own_l2c0/ppermute | solution.py:213
  32.0 2.6 %collective-permute-start.16 = (bf16[128,1024]{1,0:T(8,128)(2,1)S(1)}, bf16[128,1024]{1,0:T(8,128)(2,1)S(1)}, u32[]{:S(2)}, u32[]{:S(2)}) collective-permute-start(bf16[128,1024]{1,0:T(8,128)(2,1)S(1)} %get-tuple-element.47.refs_2_), channel_id=1, source_target_pairs={{130,256},{132,258},{134,260},{136,262},{138,264},{140,266},{142,2... | collective-permute-start | bytes 786440 | tf_op jit(solution)/shard_map/up_l2c0/ppermute | solution.py:213
  32.7 1.9 %collective-permute-start.15 = (bf16[64,1024]{1,0:T(8,128)(2,1)S(1)}, bf16[64,1024]{1,0:T(8,128)(2,1)S(1)}, u32[]{:S(2)}, u32[]{:S(2)}) collective-permute-start(bf16[64,1024]{1,0:T(8,128)(2,1)S(1)} %get-tuple-element.48), channel_id=1, source_target_pairs={{254,256},{128,258},{130,260},{132,262},{134,264},{136,266},{138,2... | collective-permute-start | bytes 393224 | tf_op jit(solution)/shard_map/down_l2c0/ppermute | solution.py:213
  33.4 7.8 %collective-permute-start.10 = (f32[128,1024]{1,0:T(8,128)S(1)}, f32[128,1024]{1,0:T(8,128)S(1)}, u32[]{:S(2)}, u32[]{:S(2)}) collective-permute-start(f32[128,1024]{1,0:T(8,128)S(1)} %get-tuple-element.44), channel_id=1, source_target_pairs={{128,129},{130,131},{132,133},{134,135},{136,137},{138,139},{140,1... | collective-permute-start | bytes 1572872 | tf_op jit(solution)/shard_map/lent_l1/ppermute | solution.py:213
  35.2 4.0 %collective-permute-start.17 = (bf16[128,1024]{1,0:T(8,128)(2,1)S(1)}, bf16[128,1024]{1,0:T(8,128)(2,1)S(1)}, u32[]{:S(2)}, u32[]{:S(2)}) collective-permute-start(bf16[128,1024]{1,0:T(8,128)(2,1)S(1)} %get-tuple-element.50.refs_4_), channel_id=1, source_target_pairs={{256,384},{258,386},{260,388},{262,390},{264,392},{266,394},{268,3... | collective-permute-start | bytes 786440 | tf_op jit(solution)/shard_map/own_l3c0/ppermute | solution.py:213
  35.9 4.0 %collective-permute-start.18 = (bf16[128,1024]{1,0:T(8,128)(2,1)S(1)}, bf16[128,1024]{1,0:T(8,128)(2,1)S(1)}, u32[]{:S(2)}, u32[]{:S(2)}) collective-permute-start(bf16[128,1024]{1,0:T(8,128)(2,1)S(1)} %get-tuple-element.50.refs_4_), channel_id=1, source_target_pairs={{258,384},{260,386},{262,388},{264,390},{266,392},{268,394},{270,3... | collective-permute-start | bytes 786440 | tf_op jit(solution)/shard_map/up_l3c0/ppermute | solution.py:213
  36.6 1.9 %collective-permute-start.19 = (bf16[64,1024]{1,0:T(8,128)(2,1)S(1)}, bf16[64,1024]{1,0:T(8,128)(2,1)S(1)}, u32[]{:S(2)}, u32[]{:S(2)}) collective-permute-start(bf16[64,1024]{1,0:T(8,128)(2,1)S(1)} %get-tuple-element.51), channel_id=1, source_target_pairs={{382,384},{256,386},{258,388},{260,390},{262,392},{264,394},{266,3... | collective-permute-start | bytes 393224 | tf_op jit(solution)/shard_map/down_l3c0/ppermute | solution.py:213
  37.8 2.8 %collective-permute-start.6 = (bf16[128,1024]{1,0:T(8,128)(2,1)S(1)}, bf16[128,1024]{1,0:T(8,128)(2,1)S(1)}, u32[]{:S(2)}, u32[]{:S(2)}) collective-permute-start(bf16[128,1024]{1,0:T(8,128)(2,1)S(1)} %get-tuple-element.39.refs_1_), channel_id=1, source_target_pairs={{1,129},{3,131},{5,133},{7,135},{9,137},{11,139},{13,141},{15,143}... | collective-permute-start | bytes 786440 | tf_op jit(solution)/shard_map/own_l1c1/ppermute | solution.py:213
  38.5 2.7 %collective-permute-start.12 = (bf16[128,1024]{1,0:T(8,128)(2,1)S(1)}, bf16[128,1024]{1,0:T(8,128)(2,1)S(1)}, u32[]{:S(2)}, u32[]{:S(2)}) collective-permute-start(bf16[128,1024]{1,0:T(8,128)(2,1)S(1)} %get-tuple-element.39.refs_1_), channel_id=1, source_target_pairs={{3,129},{5,131},{7,133},{9,135},{11,137},{13,139},{15,141},{17,143... | collective-permute-start | bytes 786440 | tf_op jit(solution)/shard_map/up_l1c1/ppermute | solution.py:213
  39.2 2.0 %collective-permute-start.11 = (bf16[64,1024]{1,0:T(8,128)(2,1)S(1)}, bf16[64,1024]{1,0:T(8,128)(2,1)S(1)}, u32[]{:S(2)}, u32[]{:S(2)}) collective-permute-start(bf16[64,1024]{1,0:T(8,128)(2,1)S(1)} %get-tuple-element.45), channel_id=1, source_target_pairs={{127,129},{1,131},{3,133},{5,135},{7,137},{9,139},{11,141},{13,143... | collective-permute-start | bytes 393224 | tf_op jit(solution)/shard_map/down_l1c1/ppermute | solution.py:213
  39.9 7.6 %collective-permute-start.20 = (f32[128,1024]{1,0:T(8,128)S(1)}, f32[128,1024]{1,0:T(8,128)S(1)}, u32[]{:S(2)}, u32[]{:S(2)}) collective-permute-start(f32[128,1024]{1,0:T(8,128)S(1)} %get-tuple-element.52), channel_id=1, source_target_pairs={{256,257},{258,259},{260,261},{262,263},{264,265},{266,267},{268,2... | collective-permute-start | bytes 1572872 | tf_op jit(solution)/shard_map/lent_l2/ppermute | solution.py:213
  41.8 5.1 %collective-permute-start.13 = (bf16[128,1024]{1,0:T(8,128)(2,1)S(1)}, bf16[128,1024]{1,0:T(8,128)(2,1)S(1)}, u32[]{:S(2)}, u32[]{:S(2)}) collective-permute-start(bf16[128,1024]{1,0:T(8,128)(2,1)S(1)} %get-tuple-element.46.refs_3_), channel_id=1, source_target_pairs={{129,257},{131,259},{133,261},{135,263},{137,265},{139,267},{141,2... | collective-permute-start | bytes 786440 | tf_op jit(solution)/shard_map/slab1_l1/own_l2c1/ppermute | solution.py:213
  42.5 5.0 %collective-permute-start.22 = (bf16[128,1024]{1,0:T(8,128)(2,1)S(1)}, bf16[128,1024]{1,0:T(8,128)(2,1)S(1)}, u32[]{:S(2)}, u32[]{:S(2)}) collective-permute-start(bf16[128,1024]{1,0:T(8,128)(2,1)S(1)} %get-tuple-element.46.refs_3_), channel_id=1, source_target_pairs={{131,257},{133,259},{135,261},{137,263},{139,265},{141,267},{143,2... | collective-permute-start | bytes 786440 | tf_op jit(solution)/shard_map/slab1_l1/up_l2c1/ppermute | solution.py:213
  43.2 4.3 %collective-permute-start.21 = (bf16[64,1024]{1,0:T(8,128)(2,1)S(1)}, bf16[64,1024]{1,0:T(8,128)(2,1)S(1)}, u32[]{:S(2)}, u32[]{:S(2)}) collective-permute-start(bf16[64,1024]{1,0:T(8,128)(2,1)S(1)} %get-tuple-element.53), channel_id=1, source_target_pairs={{255,257},{129,259},{131,261},{133,263},{135,265},{137,267},{139,2... | collective-permute-start | bytes 393224 | tf_op jit(solution)/shard_map/slab1_l1/down_l2c1/ppermute | solution.py:213
  45.6 33.4 %collective-permute-start.24 = (f32[128,1024]{1,0:T(8,128)S(1)}, f32[128,1024]{1,0:T(8,128)S(1)}, u32[]{:S(2)}, u32[]{:S(2)}) collective-permute-start(f32[128,1024]{1,0:T(8,128)S(1)} %get-tuple-element.58), channel_id=1, source_target_pairs={{384,385},{386,387},{388,389},{390,391},{392,393},{394,395},{396,3... | collective-permute-start | bytes 1572872 | tf_op jit(solution)/shard_map/lent_l3/ppermute | solution.py:213
  48.0 27.9 %collective-permute-start.23 = (bf16[128,1024]{1,0:T(8,128)(2,1)S(1)}, bf16[128,1024]{1,0:T(8,128)(2,1)S(1)}, u32[]{:S(2)}, u32[]{:S(2)}) collective-permute-start(bf16[128,1024]{1,0:T(8,128)(2,1)S(1)} %get-tuple-element.54.refs_5_), channel_id=1, source_target_pairs={{257,385},{259,387},{261,389},{263,391},{265,393},{267,395},{269,3... | collective-permute-start | bytes 786440 | tf_op jit(solution)/shard_map/slab1_l2/own_l3c1/ppermute | solution.py:213
  49.4 31.8 %collective-permute-start.26 = (bf16[128,1024]{1,0:T(8,128)(2,1)S(1)}, bf16[128,1024]{1,0:T(8,128)(2,1)S(1)}, u32[]{:S(2)}, u32[]{:S(2)}) collective-permute-start(bf16[128,1024]{1,0:T(8,128)(2,1)S(1)} %get-tuple-element.54.refs_5_), channel_id=1, source_target_pairs={{259,385},{261,387},{263,389},{265,391},{267,393},{269,395},{271,3... | collective-permute-start | bytes 786440 | tf_op jit(solution)/shard_map/slab1_l2/up_l3c1/ppermute | solution.py:213
  50.6 30.5 %collective-permute-start.25 = (bf16[64,1024]{1,0:T(8,128)(2,1)S(1)}, bf16[64,1024]{1,0:T(8,128)(2,1)S(1)}, u32[]{:S(2)}, u32[]{:S(2)}) collective-permute-start(bf16[64,1024]{1,0:T(8,128)(2,1)S(1)} %get-tuple-element.59), channel_id=1, source_target_pairs={{383,385},{257,387},{259,389},{261,391},{263,393},{265,395},{267,3... | collective-permute-start | bytes 393224 | tf_op jit(solution)/shard_map/slab1_l2/down_l3c1/ppermute | solution.py:213
  82.4 3.2 %collective-permute-start.27 = (bf16[64,1024]{1,0:T(8,128)(2,1)S(1)}, bf16[64,1024]{1,0:T(8,128)(2,1)S(1)}, u32[]{:S(2)}, u32[]{:S(2)}) collective-permute-start(bf16[64,1024]{1,0:T(8,128)(2,1)S(1)} %get-tuple-element.62), channel_id=1, source_target_pairs={{1,0},{0,1},{3,2},{2,3},{5,4},{4,5},{7,6},{6,7},{9,8},{8,9},{11,10... | collective-permute-start | bytes 393224 | tf_op jit(solution)/shard_map/last_swap/ppermute | solution.py:213
  (1 other events, 0.7 us)

commit v6 on v5

--- a/solution.py
+++ b/solution.py
@@ -77,9 +77,9 @@
     return jnp.concatenate([ref[pl.ds(slab * BLOCK, BLOCK), :] for ref in order], axis=0)
 
 
-def finish(summed, degree_ref, self_ref, weight_ref):
+def finish(summed, degree_ref, self_part, weight_ref):
     mean_rows = (summed / degree_ref[:, :1]).astype(jnp.bfloat16)
-    hidden = self_ref[...] + dot(mean_rows, weight_ref[...])
+    hidden = self_part + dot(mean_rows, weight_ref[...])
     return jnp.maximum(hidden, 0.0).astype(jnp.bfloat16)
 
 
@@ -104,7 +104,7 @@
     def _():
         summed = dot(near_ref[...], staged_rows(core, core, refs))
         summed = summed + dot(far_ref[...], staged_rows(core, 1 - core, refs))
-        made = finish(summed, degree_ref, self_ref, weight_ref)
+        made = finish(summed, degree_ref, self_ref[...], weight_ref)
         made_ref[...] = made
         tail_ref[...] = made[BLOCK:]
 
@@ -119,46 +119,40 @@
         out_ref[...] = dot(far_ref[...], staged_rows(0, 1, refs))
 
 
-def self_kernel(layer, core, where_ref, weight_ref, own_ref, out_ref):
-    @pl.when(at(where_ref, layer, core))
-    def _():
-        out_ref[...] = dot(own_ref[...], weight_ref[...])
-
-
 def fresh_rows(down_ref, own_ref, up_ref):
     return jnp.concatenate([down_ref[...], own_ref[...], up_ref[...], down_ref[...]], axis=0)
 
 
 def slab0_kernel(
-    layer, where_ref, near_ref, lend_ref, degree_ref, self_ref, base_ref, weight_ref, down_ref,
-    own_ref, up_ref, made_ref, tail_ref, lent_ref,
+    layer, where_ref, near_ref, lend_ref, degree_ref, self_ref, base_ref, weight_ref, up_ref,
+    down_ref, own_ref, made_ref, tail_ref, lent_ref,
 ):
     @pl.when(at(where_ref, layer, 0))
     def _():
         rows = fresh_rows(down_ref, own_ref, up_ref)
         summed = dot(near_ref[...], rows) + base_ref[...]
-        made = finish(summed, degree_ref, self_ref, weight_ref)
+        made = finish(summed, degree_ref, dot(own_ref[...], self_ref[...]), weight_ref)
         made_ref[...] = made
         tail_ref[...] = made[BLOCK:]
         lent_ref[...] = dot(lend_ref[...], rows)
 
 
 def slab1_kernel(
-    layer, where_ref, near_ref, degree_ref, self_ref, base_ref, weight_ref, down_ref, own_ref,
-    up_ref, made_ref, tail_ref,
+    layer, where_ref, near_ref, degree_ref, self_ref, base_ref, weight_ref, up_ref, down_ref,
+    own_ref, made_ref, tail_ref,
 ):
     @pl.when(at(where_ref, layer, 1))
     def _():
         rows = fresh_rows(down_ref, own_ref, up_ref)
         summed = dot(near_ref[...], rows) + base_ref[...]
-        made = finish(summed, degree_ref, self_ref, weight_ref)
+        made = finish(summed, degree_ref, dot(own_ref[...], self_ref[...]), weight_ref)
         made_ref[...] = made
         tail_ref[...] = made[BLOCK:]
 
 
 def last_kernel(
-    layer, where_ref, near_ref, degree_ref, self_ref, base_ref, weight_ref, down_ref, own_ref,
-    up_ref, *refs,
+    layer, where_ref, near_ref, degree_ref, self_ref, base_ref, weight_ref, up_ref, down_ref,
+    own_ref, *refs,
 ):
     done, (home_ref, away_ref) = refs[:-2], refs[-2:]
     for earlier in range(layer + 1):
@@ -176,7 +170,7 @@
     def _():
         rows = fresh_rows(down_ref, own_ref, up_ref)
         summed = dot(near_ref[...], rows) + base_ref[...]
-        made = finish(summed, degree_ref, self_ref, weight_ref)
+        made = finish(summed, degree_ref, dot(own_ref[...], self_ref[...]), weight_ref)
         home_ref[...] = made[BLOCK:]
         away_ref[...] = made[:BLOCK]
 
@@ -262,16 +256,11 @@
     moving = [send(made[core], tail[core], 1, core) for core in range(2)]
     for layer in range(1, layers):
         (own, up, down), (own1, up1, down1) = moving
-        with jax.named_scope(f"self_l{layer}c0"):
-            (part,) = call(
-                functools.partial(self_kernel, layer, 0), [f32(ROWS)], where, weight_self, own,
-                label="self",
-            )
         with jax.named_scope(f"slab0_l{layer}"):
             m0, t0, lent = call(
                 functools.partial(slab0_kernel, layer),
                 [bf16(ROWS), bf16(BLOCK), f32(ROWS)],
-                where, near, lend, degree, part, base, weight_neigh, down, own, up,
+                where, near, lend, degree, weight_self, base, weight_neigh, up, down, own,
                 label="slab0",
             )
         done.append(m0)
@@ -280,12 +269,7 @@
             if layer > 1:
                 lent, *ahead = lax.optimization_barrier((lent, *ahead))
         lent = route(lent, partner, (1,), [layer], 0, f"lent_l{layer}")
-        with jax.named_scope(f"self_l{layer}c1"):
-            (part,) = call(
-                functools.partial(self_kernel, layer, 1), [f32(ROWS)], where, weight_self, own1,
-                label="self",
-            )
-        inputs = (where, near, degree, part, lent, weight_neigh, down1, own1, up1)
+        inputs = (where, near, degree, weight_self, lent, weight_neigh, up1, down1, own1)
         with jax.named_scope(f"slab1_l{layer}"):
             if layer < layers - 1:
                 m1, t1 = call(

time: 86.9 us -> 87.4 us (level)
  waiting for transfers between devices: 29.5 us -> 33.6 us
  Pallas kernels: 11.9 us -> 8.47 us
    ppermute x28, waiting for transfers between devices: 29.5 us -> 33.6 us  [route(): return lax.ppermute(value, ('section', 'dom'), pairs)]
    pallas_call x18 -> x12, Pallas kernels: 11.9 us -> 8.47 us  [call(): pl.pallas_call(kernel, out_shape=outs, in_specs=specs, **options)(*args)]
  transfers between devices with their start and end apart: 28 -> 28, of which waited for: 4 -> 3; matrix products, arithmetic and copies ran while one was open for 0% -> 0% of each run, Pallas kernels for 12% -> 7%
where the time goes in v6:
time: 87.4 us; the launch traced here: 86.8 us
  starting transfers between devices  41.7 us (48%)
  waiting for transfers between devices  33.6 us (38%)
  Pallas kernels  8.47 us (10%)
  local copies, waits for them, and re-layouts  1.75 us (2%)
    ppermute x28, starting transfers between devices, route(): return lax.ppermute(value, ('section', 'dom'), pairs)  41.7 us
    ppermute x28, waiting for transfers between devices, route(): return lax.ppermute(value, ('section', 'dom'), pairs)  33.6 us
    pallas_call x12, Pallas kernels, call(): pl.pallas_call(kernel, out_shape=outs, in_specs=specs, **options)(*args)  8.47 us
  transfers between devices with their start and end apart: 28, of which 3 were waited for; matrix products, arithmetic and copies ran while one was open for 0% of the time, Pallas kernels for 7%

profile of v6, /device:TPU:7, one launch (start us, length us, event | category | flops | bytes accessed | tf_op | source)
XLA Modules:
  0.0 86.8 jit_solution(17069980089066820824)
XLA Ops:
  0.0 13.7 %collective-permute-start.3 = (bf16[128,1024]{1,0:T(8,128)(2,1)}, bf16[128,1024]{1,0:T(8,128)(2,1)S(1)}, u32[]{:S(2)}, u32[]{:S(2)}) collective-permute-start(bf16[128,1024]{1,0:T(8,128)(2,1)} %bitcast.22), channel_id=1, source_target_pairs={{2,0},{3,1},{4,2},{5,3},{6,4},{7,5},{8,6},{9,7},{10,8},{11,9},{12,... | collective-permute-start | bytes 786440 | tf_op jit(solution)/shard_map/init_up/ppermute | solution.py:207
  13.7 1.3 %collective-permute-start.1 = (bf16[128,1024]{1,0:T(8,128)(2,1)}, bf16[128,1024]{1,0:T(8,128)(2,1)S(1)}, u32[]{:S(2)}, u32[]{:S(2)}) collective-permute-start(bf16[128,1024]{1,0:T(8,128)(2,1)} %bitcast.23), channel_id=1, source_target_pairs={{127,0},{1,2},{3,4},{5,6},{7,8},{9,10},{11,12},{13,14},{15,16},{17... | collective-permute-start | bytes 786440 | tf_op jit(solution)/shard_map/init_down/ppermute | solution.py:207
  15.0 0.9 %copy-done.3 = s32[128,256]{1,0:T(8,128)S(1)} copy-done((s32[128,256]{1,0:T(8,128)S(1)}, s32[128,256]{1,0:T(8,128)}, u32[]{:S(2)}) %copy-start.3) | copy-done | bytes 131096
  15.9 0.7 copy-done.4
  17.3 3.0 %collective-permute-start.2 = (bf16[128,1024]{1,0:T(8,128)(2,1)S(1)}, bf16[128,1024]{1,0:T(8,128)(2,1)S(1)}, u32[]{:S(2)}, u32[]{:S(2)}) collective-permute-start(bf16[128,1024]{1,0:T(8,128)(2,1)S(1)} %bitcast.24), channel_id=1, source_target_pairs={{1,0},{0,1},{3,2},{2,3},{5,4},{4,5},{7,6},{6,7},{9,8},{8,9},{11,10... | collective-permute-start | bytes 786440 | tf_op jit(solution)/shard_map/init_other/ppermute | solution.py:207
  20.3 1.9 %collective-permute-start = (bf16[128,512]{1,0:T(8,128)(2,1)S(1)}, bf16[128,512]{1,0:T(8,128)(2,1)S(1)}, u32[]{:S(2)}, u32[]{:S(2)}) collective-permute-start(bf16[128,512]{1,0:T(8,128)(2,1)S(1)} %tiles.1.mine_ref), channel_id=1, source_target_pairs={{1,0},{0,1},{3,2},{2,3},{5,4},{4,5},{7,6},{6,7},{9,8},{8,9},{11,10... | collective-permute-start | bytes 393224 | tf_op jit(solution)/shard_map/init_tiles/ppermute | solution.py:207
  22.2 2.4 %collective-permute-start.4 = (bf16[128,1024]{1,0:T(8,128)(2,1)S(1)}, bf16[128,1024]{1,0:T(8,128)(2,1)S(1)}, u32[]{:S(2)}, u32[]{:S(2)}) collective-permute-start(bf16[128,1024]{1,0:T(8,128)(2,1)S(1)} %collective-permute-done.3.up_mine_ref), channel_id=1, source_target_pairs={{1,0},{0,1},{3,2},{2,3},{5,4},{4,5},{7,6},{6,7},{9,8},{8,9},{11,10... | collective-permute-start | bytes 786440 | tf_op jit(solution)/shard_map/init_up_other/ppermute | solution.py:207
  24.7 0.7 weave.1
  25.4 0.8 collective-permute-start.6
  27.6 0.7 collective-permute-start.8
  28.3 0.7 collective-permute-start.5
  30.8 0.7 collective-permute-start.11
  31.5 0.7 collective-permute-start.9
  32.8 0.7 collective-permute-start.17
  34.1 0.7 collective-permute-start.13
  34.8 0.7 collective-permute-start.12
  36.7 0.7 collective-permute-start.20
  37.4 0.7 collective-permute-start.18
  38.1 0.7 collective-permute-start.16
  40.1 0.7 collective-permute-start.23
  40.8 0.7 collective-permute-start.21
  41.5 1.2 %slab0.5 = (bf16[128,1024]{1,0:T(8,128)(2,1)S(1)}, bf16[64,1024]{1,0:T(8,128)(2,1)}, f32[128,1024]{1,0:T(8,128)S(1)}) custom-call(s32[2]{0:T(128)S(1)} %pad_add_fusion.where_ref, bf16[128,384]{1,0:T(8,128)(2,1)S(1)} %get-tuple-element.35.near_ref, bf16[128,384]{1,0:T(8,128)(2,1)S(1)} %get-tuple-element.37.lend_ref, ...), custom_call_target="tpu_custom_call" | custom-call | flops 1000000000 | tf_op jit(solution)/shard_map/slab0_l3/slab0/pallas_call | solution.py:183
  42.7 1.3 %collective-permute-start.15 = (f32[128,1024]{1,0:T(8,128)S(1)}, f32[128,1024]{1,0:T(8,128)S(1)}, u32[]{:S(2)}, u32[]{:S(2)}) collective-permute-start(f32[128,1024]{1,0:T(8,128)S(1)} %get-tuple-element.51), channel_id=1, source_target_pairs={{384,385},{386,387},{388,389},{390,391},{392,393},{394,395},{396,3... | collective-permute-start | bytes 1572872 | tf_op jit(solution)/shard_map/lent_l3/ppermute | solution.py:207
  45.3 1.3 %collective-permute-start.26 = (bf16[128,1024]{1,0:T(8,128)(2,1)S(1)}, bf16[128,1024]{1,0:T(8,128)(2,1)S(1)}, u32[]{:S(2)}, u32[]{:S(2)}) collective-permute-start(bf16[128,1024]{1,0:T(8,128)(2,1)S(1)} %get-tuple-element.58.refs_5_), channel_id=1, source_target_pairs={{257,385},{259,387},{261,389},{263,391},{265,393},{267,395},{269,3... | collective-permute-start | bytes 786440 | tf_op jit(solution)/shard_map/slab1_l2/own_l3c1/ppermute | solution.py:207
  46.6 1.3 %collective-permute-start.24 = (bf16[128,1024]{1,0:T(8,128)(2,1)S(1)}, bf16[128,1024]{1,0:T(8,128)(2,1)S(1)}, u32[]{:S(2)}, u32[]{:S(2)}) collective-permute-start(bf16[128,1024]{1,0:T(8,128)(2,1)S(1)} %get-tuple-element.58.refs_5_), channel_id=1, source_target_pairs={{259,385},{261,387},{263,389},{265,391},{267,393},{269,395},{271,3... | collective-permute-start | bytes 786440 | tf_op jit(solution)/shard_map/slab1_l2/up_l3c1/ppermute | solution.py:207
  47.9 1.3 %collective-permute-start.25 = (bf16[64,1024]{1,0:T(8,128)(2,1)S(1)}, bf16[64,1024]{1,0:T(8,128)(2,1)S(1)}, u32[]{:S(2)}, u32[]{:S(2)}) collective-permute-start(bf16[64,1024]{1,0:T(8,128)(2,1)S(1)} %get-tuple-element.59), channel_id=1, source_target_pairs={{383,385},{257,387},{259,389},{261,391},{263,393},{265,395},{267,3... | collective-permute-start | bytes 393224 | tf_op jit(solution)/shard_map/slab1_l2/down_l3c1/ppermute | solution.py:207
  49.2 27.4 %collective-permute-done.15.base_ref = f32[128,1024]{1,0:T(8,128)S(1)} collective-permute-done((f32[128,1024]{1,0:T(8,128)S(1)}, f32[128,1024]{1,0:T(8,128)S(1)}, u32[]{:S(2)}, u32[]{:S(2)}) %collective-permute-start.15) | collective-permute-done | bytes 524320 | tf_op jit(solution)/shard_map/lent_l3/ppermute | solution.py:207
  76.6 4.8 %collective-permute-done.25.down_ref = bf16[64,1024]{1,0:T(8,128)(2,1)S(1)} collective-permute-done((bf16[64,1024]{1,0:T(8,128)(2,1)S(1)}, bf16[64,1024]{1,0:T(8,128)(2,1)S(1)}, u32[]{:S(2)}, u32[]{:S(2)}) %collective-permute-start.25) | collective-permute-done | bytes 131104 | tf_op jit(solution)/shard_map/slab1_l2/down_l3c1/ppermute | solution.py:207
  81.4 1.5 %last.1 = (bf16[64,1024]{1,0:T(8,128)(2,1)S(1)}, bf16[64,1024]{1,0:T(8,128)(2,1)S(1)}) custom-call(s32[2]{0:T(128)S(1)} %pad_add_fusion.where_ref, bf16[128,384]{1,0:T(8,128)(2,1)S(1)} %get-tuple-element.35.near_ref, f32[128,128]{1,0:T(8,128)S(1)} %get-tuple-element.36.degree_ref, bf16[1024,1024]{1,0:T(8,128)(2,1)S(1)} %bitcast.21, ...), custom_call_target="tpu_custom_call" | custom-call | flops 1000000000 | tf_op jit(solution)/shard_map/slab1_l3/last/pallas_call | solution.py:183
  82.9 1.9 %collective-permute-start.27 = (bf16[64,1024]{1,0:T(8,128)(2,1)S(1)}, bf16[64,1024]{1,0:T(8,128)(2,1)S(1)}, u32[]{:S(2)}, u32[]{:S(2)}) collective-permute-start(bf16[64,1024]{1,0:T(8,128)(2,1)S(1)} %get-tuple-element.62), channel_id=1, source_target_pairs={{1,0},{0,1},{3,2},{2,3},{5,4},{4,5},{7,6},{6,7},{9,8},{8,9},{11,10... | collective-permute-start | bytes 393224 | tf_op jit(solution)/shard_map/last_swap/ppermute | solution.py:207
  84.8 1.3 %collective-permute-done.27 = bf16[64,1024]{1,0:T(8,128)(2,1)S(1)} collective-permute-done((bf16[64,1024]{1,0:T(8,128)(2,1)S(1)}, bf16[64,1024]{1,0:T(8,128)(2,1)S(1)}, u32[]{:S(2)}, u32[]{:S(2)}) %collective-permute-start.27) | collective-permute-done | bytes 131104 | tf_op jit(solution)/shard_map/last_swap/ppermute | solution.py:207
  86.1 0.7 maximum_bitcast_fusion
  (49 shorter events, 8.8 us)
Async XLA Ops:
  0.0 17.3 %copy-start.2 = (bf16[1,128,1024]{2,1,0:T(8,128)(2,1)S(1)}, bf16[1,128,1024]{2,1,0:T(8,128)(2,1)}, u32[]{:S(2)}) copy-start(bf16[1,128,1024]{2,1,0:T(8,128)(2,1)} %param.5) | copy-start | bytes 786436
  0.0 22.2 %collective-permute-start.3 = (bf16[128,1024]{1,0:T(8,128)(2,1)}, bf16[128,1024]{1,0:T(8,128)(2,1)S(1)}, u32[]{:S(2)}, u32[]{:S(2)}) collective-permute-start(bf16[128,1024]{1,0:T(8,128)(2,1)} %bitcast.22), channel_id=1, source_target_pairs={{2,0},{3,1},{4,2},{5,3},{6,4},{7,5},{8,6},{9,7},{10,8},{11,9},{12,... | collective-permute-start | bytes 786440 | tf_op jit(solution)/shard_map/init_up/ppermute | solution.py:207
  13.7 11.7 %collective-permute-start.1 = (bf16[128,1024]{1,0:T(8,128)(2,1)}, bf16[128,1024]{1,0:T(8,128)(2,1)S(1)}, u32[]{:S(2)}, u32[]{:S(2)}) collective-permute-start(bf16[128,1024]{1,0:T(8,128)(2,1)} %bitcast.23), channel_id=1, source_target_pairs={{127,0},{1,2},{3,4},{5,6},{7,8},{9,10},{11,12},{13,14},{15,16},{17... | collective-permute-start | bytes 786440 | tf_op jit(solution)/shard_map/init_down/ppermute | solution.py:207
  15.0 0.9 %copy-start.3 = (s32[128,256]{1,0:T(8,128)S(1)}, s32[128,256]{1,0:T(8,128)}, u32[]{:S(2)}) copy-start(s32[128,256]{1,0:T(8,128)} %edges_ref.1) | copy-start | bytes 393220
  17.3 9.0 %copy-start.1 = (bf16[1,1024,1024]{2,1,0:T(8,128)(2,1)S(1)}, bf16[1,1024,1024]{2,1,0:T(8,128)(2,1)}, u32[]{:S(2)}) copy-start(bf16[1,1024,1024]{2,1,0:T(8,128)(2,1)} %param.8) | copy-start | bytes 6291460
  17.3 9.0 %collective-permute-start.2 = (bf16[128,1024]{1,0:T(8,128)(2,1)S(1)}, bf16[128,1024]{1,0:T(8,128)(2,1)S(1)}, u32[]{:S(2)}, u32[]{:S(2)}) collective-permute-start(bf16[128,1024]{1,0:T(8,128)(2,1)S(1)} %bitcast.24), channel_id=1, source_target_pairs={{1,0},{0,1},{3,2},{2,3},{5,4},{4,5},{7,6},{6,7},{9,8},{8,9},{11,10... | collective-permute-start | bytes 786440 | tf_op jit(solution)/shard_map/init_other/ppermute | solution.py:207
  20.3 4.4 %collective-permute-start = (bf16[128,512]{1,0:T(8,128)(2,1)S(1)}, bf16[128,512]{1,0:T(8,128)(2,1)S(1)}, u32[]{:S(2)}, u32[]{:S(2)}) collective-permute-start(bf16[128,512]{1,0:T(8,128)(2,1)S(1)} %tiles.1.mine_ref), channel_id=1, source_target_pairs={{1,0},{0,1},{3,2},{2,3},{5,4},{4,5},{7,6},{6,7},{9,8},{8,9},{11,10... | collective-permute-start | bytes 393224 | tf_op jit(solution)/shard_map/init_tiles/ppermute | solution.py:207
  22.2 4.6 %collective-permute-start.4 = (bf16[128,1024]{1,0:T(8,128)(2,1)S(1)}, bf16[128,1024]{1,0:T(8,128)(2,1)S(1)}, u32[]{:S(2)}, u32[]{:S(2)}) collective-permute-start(bf16[128,1024]{1,0:T(8,128)(2,1)S(1)} %collective-permute-done.3.up_mine_ref), channel_id=1, source_target_pairs={{1,0},{0,1},{3,2},{2,3},{5,4},{4,5},{7,6},{6,7},{9,8},{8,9},{11,10... | collective-permute-start | bytes 786440 | tf_op jit(solution)/shard_map/init_up_other/ppermute | solution.py:207
  25.4 1.6 %copy-start = (bf16[1,1024,1024]{2,1,0:T(8,128)(2,1)S(1)}, bf16[1,1024,1024]{2,1,0:T(8,128)(2,1)}, u32[]{:S(2)}) copy-start(bf16[1,1024,1024]{2,1,0:T(8,128)(2,1)} %param.9) | copy-start | bytes 6291460
  25.4 3.5 %collective-permute-start.6 = (bf16[128,1024]{1,0:T(8,128)(2,1)S(1)}, bf16[128,1024]{1,0:T(8,128)(2,1)S(1)}, u32[]{:S(2)}, u32[]{:S(2)}) collective-permute-start(bf16[128,1024]{1,0:T(8,128)(2,1)S(1)} %collective-permute-done.1.down_ref), channel_id=1, source_target_pairs={{0,1},{2,3},{4,5},{6,7},{8,9},{10,11},{12,13},{14,15},{16,17},{18,... | collective-permute-start | bytes 786440 | tf_op jit(solution)/shard_map/init_down_odd/ppermute | solution.py:207
  27.6 2.6 %collective-permute-start.8 = (bf16[128,1024]{1,0:T(8,128)(2,1)S(1)}, bf16[128,1024]{1,0:T(8,128)(2,1)S(1)}, u32[]{:S(2)}, u32[]{:S(2)}) collective-permute-start(bf16[128,1024]{1,0:T(8,128)(2,1)S(1)} %get-tuple-element.40.refs_0_), channel_id=1, source_target_pairs={{0,128},{2,130},{4,132},{6,134},{8,136},{10,138},{12,140},{14,142}... | collective-permute-start | bytes 786440 | tf_op jit(solution)/shard_map/own_l1c0/ppermute | solution.py:207
  28.3 2.0 %collective-permute-start.5 = (bf16[128,1024]{1,0:T(8,128)(2,1)S(1)}, bf16[128,1024]{1,0:T(8,128)(2,1)S(1)}, u32[]{:S(2)}, u32[]{:S(2)}) collective-permute-start(bf16[128,1024]{1,0:T(8,128)(2,1)S(1)} %get-tuple-element.40.refs_0_), channel_id=1, source_target_pairs={{2,128},{4,130},{6,132},{8,134},{10,136},{12,138},{14,140},{16,142... | collective-permute-start | bytes 786440 | tf_op jit(solution)/shard_map/up_l1c0/ppermute | solution.py:207
  29.0 1.2 %collective-permute-start.7 = (bf16[64,1024]{1,0:T(8,128)(2,1)S(1)}, bf16[64,1024]{1,0:T(8,128)(2,1)S(1)}, u32[]{:S(2)}, u32[]{:S(2)}) collective-permute-start(bf16[64,1024]{1,0:T(8,128)(2,1)S(1)} %get-tuple-element.42), channel_id=1, source_target_pairs={{126,128},{0,130},{2,132},{4,134},{6,136},{8,138},{10,140},{12,142... | collective-permute-start | bytes 393224 | tf_op jit(solution)/shard_map/down_l1c0/ppermute | solution.py:207
  30.8 2.8 %collective-permute-start.11 = (bf16[128,1024]{1,0:T(8,128)(2,1)S(1)}, bf16[128,1024]{1,0:T(8,128)(2,1)S(1)}, u32[]{:S(2)}, u32[]{:S(2)}) collective-permute-start(bf16[128,1024]{1,0:T(8,128)(2,1)S(1)} %get-tuple-element.43.refs_2_), channel_id=1, source_target_pairs={{128,256},{130,258},{132,260},{134,262},{136,264},{138,266},{140,2... | collective-permute-start | bytes 786440 | tf_op jit(solution)/shard_map/own_l2c0/ppermute | solution.py:207
  31.5 2.1 %collective-permute-start.9 = (bf16[128,1024]{1,0:T(8,128)(2,1)S(1)}, bf16[128,1024]{1,0:T(8,128)(2,1)S(1)}, u32[]{:S(2)}, u32[]{:S(2)}) collective-permute-start(bf16[128,1024]{1,0:T(8,128)(2,1)S(1)} %get-tuple-element.43.refs_2_), channel_id=1, source_target_pairs={{130,256},{132,258},{134,260},{136,262},{138,264},{140,266},{142,2... | collective-permute-start | bytes 786440 | tf_op jit(solution)/shard_map/up_l2c0/ppermute | solution.py:207
  32.2 1.4 %collective-permute-start.10 = (bf16[64,1024]{1,0:T(8,128)(2,1)S(1)}, bf16[64,1024]{1,0:T(8,128)(2,1)S(1)}, u32[]{:S(2)}, u32[]{:S(2)}) collective-permute-start(bf16[64,1024]{1,0:T(8,128)(2,1)S(1)} %get-tuple-element.44), channel_id=1, source_target_pairs={{254,256},{128,258},{130,260},{132,262},{134,264},{136,266},{138,2... | collective-permute-start | bytes 393224 | tf_op jit(solution)/shard_map/down_l2c0/ppermute | solution.py:207
  32.8 6.7 %collective-permute-start.17 = (f32[128,1024]{1,0:T(8,128)S(1)}, f32[128,1024]{1,0:T(8,128)S(1)}, u32[]{:S(2)}, u32[]{:S(2)}) collective-permute-start(f32[128,1024]{1,0:T(8,128)S(1)} %get-tuple-element.53), channel_id=1, source_target_pairs={{128,129},{130,131},{132,133},{134,135},{136,137},{138,139},{140,1... | collective-permute-start | bytes 1572872 | tf_op jit(solution)/shard_map/lent_l1/ppermute | solution.py:207
  34.1 4.0 %collective-permute-start.13 = (bf16[128,1024]{1,0:T(8,128)(2,1)S(1)}, bf16[128,1024]{1,0:T(8,128)(2,1)S(1)}, u32[]{:S(2)}, u32[]{:S(2)}) collective-permute-start(bf16[128,1024]{1,0:T(8,128)(2,1)S(1)} %get-tuple-element.46.refs_4_), channel_id=1, source_target_pairs={{258,384},{260,386},{262,388},{264,390},{266,392},{268,394},{270,3... | collective-permute-start | bytes 786440 | tf_op jit(solution)/shard_map/up_l3c0/ppermute | solution.py:207
  34.8 3.3 %collective-permute-start.12 = (bf16[128,1024]{1,0:T(8,128)(2,1)S(1)}, bf16[128,1024]{1,0:T(8,128)(2,1)S(1)}, u32[]{:S(2)}, u32[]{:S(2)}) collective-permute-start(bf16[128,1024]{1,0:T(8,128)(2,1)S(1)} %get-tuple-element.46.refs_4_), channel_id=1, source_target_pairs={{256,384},{258,386},{260,388},{262,390},{264,392},{266,394},{268,3... | collective-permute-start | bytes 786440 | tf_op jit(solution)/shard_map/own_l3c0/ppermute | solution.py:207
  35.5 1.9 %collective-permute-start.14 = (bf16[64,1024]{1,0:T(8,128)(2,1)S(1)}, bf16[64,1024]{1,0:T(8,128)(2,1)S(1)}, u32[]{:S(2)}, u32[]{:S(2)}) collective-permute-start(bf16[64,1024]{1,0:T(8,128)(2,1)S(1)} %get-tuple-element.47), channel_id=1, source_target_pairs={{382,384},{256,386},{258,388},{260,390},{262,392},{264,394},{266,3... | collective-permute-start | bytes 393224 | tf_op jit(solution)/shard_map/down_l3c0/ppermute | solution.py:207
  36.7 2.8 %collective-permute-start.20 = (bf16[128,1024]{1,0:T(8,128)(2,1)S(1)}, bf16[128,1024]{1,0:T(8,128)(2,1)S(1)}, u32[]{:S(2)}, u32[]{:S(2)}) collective-permute-start(bf16[128,1024]{1,0:T(8,128)(2,1)S(1)} %get-tuple-element.54.refs_1_), channel_id=1, source_target_pairs={{1,129},{3,131},{5,133},{7,135},{9,137},{11,139},{13,141},{15,143}... | collective-permute-start | bytes 786440 | tf_op jit(solution)/shard_map/own_l1c1/ppermute | solution.py:207
  37.4 2.1 %collective-permute-start.18 = (bf16[128,1024]{1,0:T(8,128)(2,1)S(1)}, bf16[128,1024]{1,0:T(8,128)(2,1)S(1)}, u32[]{:S(2)}, u32[]{:S(2)}) collective-permute-start(bf16[128,1024]{1,0:T(8,128)(2,1)S(1)} %get-tuple-element.54.refs_1_), channel_id=1, source_target_pairs={{3,129},{5,131},{7,133},{9,135},{11,137},{13,139},{15,141},{17,143... | collective-permute-start | bytes 786440 | tf_op jit(solution)/shard_map/up_l1c1/ppermute | solution.py:207
  38.1 6.6 %collective-permute-start.16 = (f32[128,1024]{1,0:T(8,128)S(1)}, f32[128,1024]{1,0:T(8,128)S(1)}, u32[]{:S(2)}, u32[]{:S(2)}) collective-permute-start(f32[128,1024]{1,0:T(8,128)S(1)} %get-tuple-element.52), channel_id=1, source_target_pairs={{256,257},{258,259},{260,261},{262,263},{264,265},{266,267},{268,2... | collective-permute-start | bytes 1572872 | tf_op jit(solution)/shard_map/lent_l2/ppermute | solution.py:207
  38.8 0.7 collective-permute-start.19
  40.1 4.6 %collective-permute-start.23 = (bf16[128,1024]{1,0:T(8,128)(2,1)S(1)}, bf16[128,1024]{1,0:T(8,128)(2,1)S(1)}, u32[]{:S(2)}, u32[]{:S(2)}) collective-permute-start(bf16[128,1024]{1,0:T(8,128)(2,1)S(1)} %get-tuple-element.56.refs_3_), channel_id=1, source_target_pairs={{129,257},{131,259},{133,261},{135,263},{137,265},{139,267},{141,2... | collective-permute-start | bytes 786440 | tf_op jit(solution)/shard_map/slab1_l1/own_l2c1/ppermute | solution.py:207
  40.8 3.9 %collective-permute-start.21 = (bf16[128,1024]{1,0:T(8,128)(2,1)S(1)}, bf16[128,1024]{1,0:T(8,128)(2,1)S(1)}, u32[]{:S(2)}, u32[]{:S(2)}) collective-permute-start(bf16[128,1024]{1,0:T(8,128)(2,1)S(1)} %get-tuple-element.56.refs_3_), channel_id=1, source_target_pairs={{131,257},{133,259},{135,261},{137,263},{139,265},{141,267},{143,2... | collective-permute-start | bytes 786440 | tf_op jit(solution)/shard_map/slab1_l1/up_l2c1/ppermute | solution.py:207
  42.7 33.9 %collective-permute-start.15 = (f32[128,1024]{1,0:T(8,128)S(1)}, f32[128,1024]{1,0:T(8,128)S(1)}, u32[]{:S(2)}, u32[]{:S(2)}) collective-permute-start(f32[128,1024]{1,0:T(8,128)S(1)} %get-tuple-element.51), channel_id=1, source_target_pairs={{384,385},{386,387},{388,389},{390,391},{392,393},{394,395},{396,3... | collective-permute-start | bytes 1572872 | tf_op jit(solution)/shard_map/lent_l3/ppermute | solution.py:207
  44.0 0.7 collective-permute-start.22
  45.3 36.1 %collective-permute-start.26 = (bf16[128,1024]{1,0:T(8,128)(2,1)S(1)}, bf16[128,1024]{1,0:T(8,128)(2,1)S(1)}, u32[]{:S(2)}, u32[]{:S(2)}) collective-permute-start(bf16[128,1024]{1,0:T(8,128)(2,1)S(1)} %get-tuple-element.58.refs_5_), channel_id=1, source_target_pairs={{257,385},{259,387},{261,389},{263,391},{265,393},{267,395},{269,3... | collective-permute-start | bytes 786440 | tf_op jit(solution)/shard_map/slab1_l2/own_l3c1/ppermute | solution.py:207
  46.6 34.8 %collective-permute-start.24 = (bf16[128,1024]{1,0:T(8,128)(2,1)S(1)}, bf16[128,1024]{1,0:T(8,128)(2,1)S(1)}, u32[]{:S(2)}, u32[]{:S(2)}) collective-permute-start(bf16[128,1024]{1,0:T(8,128)(2,1)S(1)} %get-tuple-element.58.refs_5_), channel_id=1, source_target_pairs={{259,385},{261,387},{263,389},{265,391},{267,393},{269,395},{271,3... | collective-permute-start | bytes 786440 | tf_op jit(solution)/shard_map/slab1_l2/up_l3c1/ppermute | solution.py:207
  47.9 33.5 %collective-permute-start.25 = (bf16[64,1024]{1,0:T(8,128)(2,1)S(1)}, bf16[64,1024]{1,0:T(8,128)(2,1)S(1)}, u32[]{:S(2)}, u32[]{:S(2)}) collective-permute-start(bf16[64,1024]{1,0:T(8,128)(2,1)S(1)} %get-tuple-element.59), channel_id=1, source_target_pairs={{383,385},{257,387},{259,389},{261,391},{263,393},{265,395},{267,3... | collective-permute-start | bytes 393224 | tf_op jit(solution)/shard_map/slab1_l2/down_l3c1/ppermute | solution.py:207
  82.9 3.2 %collective-permute-start.27 = (bf16[64,1024]{1,0:T(8,128)(2,1)S(1)}, bf16[64,1024]{1,0:T(8,128)(2,1)S(1)}, u32[]{:S(2)}, u32[]{:S(2)}) collective-permute-start(bf16[64,1024]{1,0:T(8,128)(2,1)S(1)} %get-tuple-element.62), channel_id=1, source_target_pairs={{1,0},{0,1},{3,2},{2,3},{5,4},{4,5},{7,6},{6,7},{9,8},{8,9},{11,10... | collective-permute-start | bytes 393224 | tf_op jit(solution)/shard_map/last_swap/ppermute | solution.py:207
  (1 other events, 0.7 us)

commit v7 on v6

--- a/solution.py
+++ b/solution.py
@@ -266,8 +266,6 @@
         done.append(m0)
         if layer < layers - 1:
             ahead = send(m0, t0, layer + 1, 0)
-            if layer > 1:
-                lent, *ahead = lax.optimization_barrier((lent, *ahead))
         lent = route(lent, partner, (1,), [layer], 0, f"lent_l{layer}")
         inputs = (where, near, degree, weight_self, lent, weight_neigh, up1, down1, own1)
         with jax.named_scope(f"slab1_l{layer}"):

time: 87.4 us -> 88.1 us (level)
  starting transfers between devices: 41.7 us -> 42.8 us
    ppermute x28, starting transfers between devices: 41.7 us -> 42.8 us  [route(): return lax.ppermute(value, ('section', 'dom'), pairs)]
where the time goes in v7:
time: 88.1 us; the launch traced here: 87.6 us
  starting transfers between devices  42.8 us (49%)
  waiting for transfers between devices  33.2 us (38%)
  Pallas kernels  8.47 us (10%)
  local copies, waits for them, and re-layouts  1.75 us (2%)
    ppermute x28, starting transfers between devices, route(): return lax.ppermute(value, ('section', 'dom'), pairs)  42.8 us
    ppermute x28, waiting for transfers between devices, route(): return lax.ppermute(value, ('section', 'dom'), pairs)  33.2 us
    pallas_call x12, Pallas kernels, call(): pl.pallas_call(kernel, out_shape=outs, in_specs=specs, **options)(*args)  8.47 us
  transfers between devices with their start and end apart: 28, of which 3 were waited for; matrix products, arithmetic and copies ran while one was open for 0% of the time, Pallas kernels for 7%

profile of v7, /device:TPU:7, one launch (start us, length us, event | category | flops | bytes accessed | tf_op | source)
XLA Modules:
  0.0 87.6 jit_solution(16127186644698732151)
XLA Ops:
  0.0 13.7 %collective-permute-start.3 = (bf16[128,1024]{1,0:T(8,128)(2,1)}, bf16[128,1024]{1,0:T(8,128)(2,1)S(1)}, u32[]{:S(2)}, u32[]{:S(2)}) collective-permute-start(bf16[128,1024]{1,0:T(8,128)(2,1)} %bitcast.22), channel_id=1, source_target_pairs={{2,0},{3,1},{4,2},{5,3},{6,4},{7,5},{8,6},{9,7},{10,8},{11,9},{12,... | collective-permute-start | bytes 786440 | tf_op jit(solution)/shard_map/init_up/ppermute | solution.py:207
  13.7 1.3 %collective-permute-start.1 = (bf16[128,1024]{1,0:T(8,128)(2,1)}, bf16[128,1024]{1,0:T(8,128)(2,1)S(1)}, u32[]{:S(2)}, u32[]{:S(2)}) collective-permute-start(bf16[128,1024]{1,0:T(8,128)(2,1)} %bitcast.23), channel_id=1, source_target_pairs={{127,0},{1,2},{3,4},{5,6},{7,8},{9,10},{11,12},{13,14},{15,16},{17... | collective-permute-start | bytes 786440 | tf_op jit(solution)/shard_map/init_down/ppermute | solution.py:207
  15.0 0.9 %copy-done.3 = s32[128,256]{1,0:T(8,128)S(1)} copy-done((s32[128,256]{1,0:T(8,128)S(1)}, s32[128,256]{1,0:T(8,128)}, u32[]{:S(2)}) %copy-start.3) | copy-done | bytes 131096
  15.9 0.7 copy-done.4
  17.3 3.0 %collective-permute-start.2 = (bf16[128,1024]{1,0:T(8,128)(2,1)S(1)}, bf16[128,1024]{1,0:T(8,128)(2,1)S(1)}, u32[]{:S(2)}, u32[]{:S(2)}) collective-permute-start(bf16[128,1024]{1,0:T(8,128)(2,1)S(1)} %bitcast.24), channel_id=1, source_target_pairs={{1,0},{0,1},{3,2},{2,3},{5,4},{4,5},{7,6},{6,7},{9,8},{8,9},{11,10... | collective-permute-start | bytes 786440 | tf_op jit(solution)/shard_map/init_other/ppermute | solution.py:207
  20.3 1.9 %collective-permute-start = (bf16[128,512]{1,0:T(8,128)(2,1)S(1)}, bf16[128,512]{1,0:T(8,128)(2,1)S(1)}, u32[]{:S(2)}, u32[]{:S(2)}) collective-permute-start(bf16[128,512]{1,0:T(8,128)(2,1)S(1)} %tiles.1.mine_ref), channel_id=1, source_target_pairs={{1,0},{0,1},{3,2},{2,3},{5,4},{4,5},{7,6},{6,7},{9,8},{8,9},{11,10... | collective-permute-start | bytes 393224 | tf_op jit(solution)/shard_map/init_tiles/ppermute | solution.py:207
  22.2 2.4 %collective-permute-start.4 = (bf16[128,1024]{1,0:T(8,128)(2,1)S(1)}, bf16[128,1024]{1,0:T(8,128)(2,1)S(1)}, u32[]{:S(2)}, u32[]{:S(2)}) collective-permute-start(bf16[128,1024]{1,0:T(8,128)(2,1)S(1)} %collective-permute-done.3.up_mine_ref), channel_id=1, source_target_pairs={{1,0},{0,1},{3,2},{2,3},{5,4},{4,5},{7,6},{6,7},{9,8},{8,9},{11,10... | collective-permute-start | bytes 786440 | tf_op jit(solution)/shard_map/init_up_other/ppermute | solution.py:207
  24.7 0.7 weave.1
  25.4 0.8 collective-permute-start.6
  27.6 0.7 collective-permute-start.8
  28.3 0.7 collective-permute-start.5
  30.8 0.7 collective-permute-start.11
  31.5 0.7 collective-permute-start.9
  32.2 0.7 collective-permute-start.17
  34.1 0.7 collective-permute-start.20
  34.8 0.7 collective-permute-start.18
  36.7 0.7 collective-permute-start.14
  37.4 0.7 collective-permute-start.16
  38.1 0.7 collective-permute-start.12
  40.1 0.7 collective-permute-start.23
  40.8 0.7 collective-permute-start.21
  41.5 1.2 %slab0.5 = (bf16[128,1024]{1,0:T(8,128)(2,1)S(1)}, bf16[64,1024]{1,0:T(8,128)(2,1)}, f32[128,1024]{1,0:T(8,128)S(1)}) custom-call(s32[2]{0:T(128)S(1)} %pad_add_fusion.where_ref, bf16[128,384]{1,0:T(8,128)(2,1)S(1)} %get-tuple-element.31.near_ref, bf16[128,384]{1,0:T(8,128)(2,1)S(1)} %get-tuple-element.33.lend_ref, ...), custom_call_target="tpu_custom_call" | custom-call | flops 1000000000 | tf_op jit(solution)/shard_map/slab0_l3/slab0/pallas_call | solution.py:183
  42.7 1.3 %collective-permute-start.15 = (f32[128,1024]{1,0:T(8,128)S(1)}, f32[128,1024]{1,0:T(8,128)S(1)}, u32[]{:S(2)}, u32[]{:S(2)}) collective-permute-start(f32[128,1024]{1,0:T(8,128)S(1)} %get-tuple-element.43), channel_id=1, source_target_pairs={{384,385},{386,387},{388,389},{390,391},{392,393},{394,395},{396,3... | collective-permute-start | bytes 1572872 | tf_op jit(solution)/shard_map/lent_l3/ppermute | solution.py:207
  45.3 1.3 %collective-permute-start.26 = (bf16[128,1024]{1,0:T(8,128)(2,1)S(1)}, bf16[128,1024]{1,0:T(8,128)(2,1)S(1)}, u32[]{:S(2)}, u32[]{:S(2)}) collective-permute-start(bf16[128,1024]{1,0:T(8,128)(2,1)S(1)} %get-tuple-element.50.refs_5_), channel_id=1, source_target_pairs={{257,385},{259,387},{261,389},{263,391},{265,393},{267,395},{269,3... | collective-permute-start | bytes 786440 | tf_op jit(solution)/shard_map/slab1_l2/own_l3c1/ppermute | solution.py:207
  46.6 1.3 %collective-permute-start.24 = (bf16[128,1024]{1,0:T(8,128)(2,1)S(1)}, bf16[128,1024]{1,0:T(8,128)(2,1)S(1)}, u32[]{:S(2)}, u32[]{:S(2)}) collective-permute-start(bf16[128,1024]{1,0:T(8,128)(2,1)S(1)} %get-tuple-element.50.refs_5_), channel_id=1, source_target_pairs={{259,385},{261,387},{263,389},{265,391},{267,393},{269,395},{271,3... | collective-permute-start | bytes 786440 | tf_op jit(solution)/shard_map/slab1_l2/up_l3c1/ppermute | solution.py:207
  47.9 1.3 %collective-permute-start.25 = (bf16[64,1024]{1,0:T(8,128)(2,1)S(1)}, bf16[64,1024]{1,0:T(8,128)(2,1)S(1)}, u32[]{:S(2)}, u32[]{:S(2)}) collective-permute-start(bf16[64,1024]{1,0:T(8,128)(2,1)S(1)} %get-tuple-element.51), channel_id=1, source_target_pairs={{383,385},{257,387},{259,389},{261,391},{263,393},{265,395},{267,3... | collective-permute-start | bytes 393224 | tf_op jit(solution)/shard_map/slab1_l2/down_l3c1/ppermute | solution.py:207
  49.2 24.7 %collective-permute-done.25.down_ref = bf16[64,1024]{1,0:T(8,128)(2,1)S(1)} collective-permute-done((bf16[64,1024]{1,0:T(8,128)(2,1)S(1)}, bf16[64,1024]{1,0:T(8,128)(2,1)S(1)}, u32[]{:S(2)}, u32[]{:S(2)}) %collective-permute-start.25) | collective-permute-done | bytes 131104 | tf_op jit(solution)/shard_map/slab1_l2/down_l3c1/ppermute | solution.py:207
  73.8 7.4 %collective-permute-done.15.base_ref = f32[128,1024]{1,0:T(8,128)S(1)} collective-permute-done((f32[128,1024]{1,0:T(8,128)S(1)}, f32[128,1024]{1,0:T(8,128)S(1)}, u32[]{:S(2)}, u32[]{:S(2)}) %collective-permute-start.15) | collective-permute-done | bytes 524320 | tf_op jit(solution)/shard_map/lent_l3/ppermute | solution.py:207
  81.3 1.5 %last.1 = (bf16[64,1024]{1,0:T(8,128)(2,1)S(1)}, bf16[64,1024]{1,0:T(8,128)(2,1)S(1)}) custom-call(s32[2]{0:T(128)S(1)} %pad_add_fusion.where_ref, bf16[128,384]{1,0:T(8,128)(2,1)S(1)} %get-tuple-element.31.near_ref, f32[128,128]{1,0:T(8,128)S(1)} %get-tuple-element.32.degree_ref, bf16[1024,1024]{1,0:T(8,128)(2,1)S(1)} %bitcast.21, ...), custom_call_target="tpu_custom_call" | custom-call | flops 1000000000 | tf_op jit(solution)/shard_map/slab1_l3/last/pallas_call | solution.py:183
  82.8 3.1 %collective-permute-start.27 = (bf16[64,1024]{1,0:T(8,128)(2,1)S(1)}, bf16[64,1024]{1,0:T(8,128)(2,1)S(1)}, u32[]{:S(2)}, u32[]{:S(2)}) collective-permute-start(bf16[64,1024]{1,0:T(8,128)(2,1)S(1)} %get-tuple-element.54), channel_id=1, source_target_pairs={{1,0},{0,1},{3,2},{2,3},{5,4},{4,5},{7,6},{6,7},{9,8},{8,9},{11,10... | collective-permute-start | bytes 393224 | tf_op jit(solution)/shard_map/last_swap/ppermute | solution.py:207
  85.9 1.0 %collective-permute-done.27 = bf16[64,1024]{1,0:T(8,128)(2,1)S(1)} collective-permute-done((bf16[64,1024]{1,0:T(8,128)(2,1)S(1)}, bf16[64,1024]{1,0:T(8,128)(2,1)S(1)}, u32[]{:S(2)}, u32[]{:S(2)}) %collective-permute-start.27) | collective-permute-done | bytes 131104 | tf_op jit(solution)/shard_map/last_swap/ppermute | solution.py:207
  86.8 0.7 maximum_bitcast_fusion
  (49 shorter events, 8.8 us)
Async XLA Ops:
  0.0 17.3 %copy-start.2 = (bf16[1,128,1024]{2,1,0:T(8,128)(2,1)S(1)}, bf16[1,128,1024]{2,1,0:T(8,128)(2,1)}, u32[]{:S(2)}) copy-start(bf16[1,128,1024]{2,1,0:T(8,128)(2,1)} %param.5) | copy-start | bytes 786436
  0.0 22.2 %collective-permute-start.3 = (bf16[128,1024]{1,0:T(8,128)(2,1)}, bf16[128,1024]{1,0:T(8,128)(2,1)S(1)}, u32[]{:S(2)}, u32[]{:S(2)}) collective-permute-start(bf16[128,1024]{1,0:T(8,128)(2,1)} %bitcast.22), channel_id=1, source_target_pairs={{2,0},{3,1},{4,2},{5,3},{6,4},{7,5},{8,6},{9,7},{10,8},{11,9},{12,... | collective-permute-start | bytes 786440 | tf_op jit(solution)/shard_map/init_up/ppermute | solution.py:207
  13.7 11.7 %collective-permute-start.1 = (bf16[128,1024]{1,0:T(8,128)(2,1)}, bf16[128,1024]{1,0:T(8,128)(2,1)S(1)}, u32[]{:S(2)}, u32[]{:S(2)}) collective-permute-start(bf16[128,1024]{1,0:T(8,128)(2,1)} %bitcast.23), channel_id=1, source_target_pairs={{127,0},{1,2},{3,4},{5,6},{7,8},{9,10},{11,12},{13,14},{15,16},{17... | collective-permute-start | bytes 786440 | tf_op jit(solution)/shard_map/init_down/ppermute | solution.py:207
  15.0 0.9 %copy-start.3 = (s32[128,256]{1,0:T(8,128)S(1)}, s32[128,256]{1,0:T(8,128)}, u32[]{:S(2)}) copy-start(s32[128,256]{1,0:T(8,128)} %edges_ref.1) | copy-start | bytes 393220
  17.3 9.0 %copy-start.1 = (bf16[1,1024,1024]{2,1,0:T(8,128)(2,1)S(1)}, bf16[1,1024,1024]{2,1,0:T(8,128)(2,1)}, u32[]{:S(2)}) copy-start(bf16[1,1024,1024]{2,1,0:T(8,128)(2,1)} %param.8) | copy-start | bytes 6291460
  17.3 9.0 %collective-permute-start.2 = (bf16[128,1024]{1,0:T(8,128)(2,1)S(1)}, bf16[128,1024]{1,0:T(8,128)(2,1)S(1)}, u32[]{:S(2)}, u32[]{:S(2)}) collective-permute-start(bf16[128,1024]{1,0:T(8,128)(2,1)S(1)} %bitcast.24), channel_id=1, source_target_pairs={{1,0},{0,1},{3,2},{2,3},{5,4},{4,5},{7,6},{6,7},{9,8},{8,9},{11,10... | collective-permute-start | bytes 786440 | tf_op jit(solution)/shard_map/init_other/ppermute | solution.py:207
  20.3 4.4 %collective-permute-start = (bf16[128,512]{1,0:T(8,128)(2,1)S(1)}, bf16[128,512]{1,0:T(8,128)(2,1)S(1)}, u32[]{:S(2)}, u32[]{:S(2)}) collective-permute-start(bf16[128,512]{1,0:T(8,128)(2,1)S(1)} %tiles.1.mine_ref), channel_id=1, source_target_pairs={{1,0},{0,1},{3,2},{2,3},{5,4},{4,5},{7,6},{6,7},{9,8},{8,9},{11,10... | collective-permute-start | bytes 393224 | tf_op jit(solution)/shard_map/init_tiles/ppermute | solution.py:207
  22.2 4.6 %collective-permute-start.4 = (bf16[128,1024]{1,0:T(8,128)(2,1)S(1)}, bf16[128,1024]{1,0:T(8,128)(2,1)S(1)}, u32[]{:S(2)}, u32[]{:S(2)}) collective-permute-start(bf16[128,1024]{1,0:T(8,128)(2,1)S(1)} %collective-permute-done.3.up_mine_ref), channel_id=1, source_target_pairs={{1,0},{0,1},{3,2},{2,3},{5,4},{4,5},{7,6},{6,7},{9,8},{8,9},{11,10... | collective-permute-start | bytes 786440 | tf_op jit(solution)/shard_map/init_up_other/ppermute | solution.py:207
  25.4 1.6 %copy-start = (bf16[1,1024,1024]{2,1,0:T(8,128)(2,1)S(1)}, bf16[1,1024,1024]{2,1,0:T(8,128)(2,1)}, u32[]{:S(2)}) copy-start(bf16[1,1024,1024]{2,1,0:T(8,128)(2,1)} %param.9) | copy-start | bytes 6291460
  25.4 3.5 %collective-permute-start.6 = (bf16[128,1024]{1,0:T(8,128)(2,1)S(1)}, bf16[128,1024]{1,0:T(8,128)(2,1)S(1)}, u32[]{:S(2)}, u32[]{:S(2)}) collective-permute-start(bf16[128,1024]{1,0:T(8,128)(2,1)S(1)} %collective-permute-done.1.down_ref), channel_id=1, source_target_pairs={{0,1},{2,3},{4,5},{6,7},{8,9},{10,11},{12,13},{14,15},{16,17},{18,... | collective-permute-start | bytes 786440 | tf_op jit(solution)/shard_map/init_down_odd/ppermute | solution.py:207
  27.6 2.6 %collective-permute-start.8 = (bf16[128,1024]{1,0:T(8,128)(2,1)S(1)}, bf16[128,1024]{1,0:T(8,128)(2,1)S(1)}, u32[]{:S(2)}, u32[]{:S(2)}) collective-permute-start(bf16[128,1024]{1,0:T(8,128)(2,1)S(1)} %get-tuple-element.36.refs_0_), channel_id=1, source_target_pairs={{0,128},{2,130},{4,132},{6,134},{8,136},{10,138},{12,140},{14,142}... | collective-permute-start | bytes 786440 | tf_op jit(solution)/shard_map/own_l1c0/ppermute | solution.py:207
  28.3 2.0 %collective-permute-start.5 = (bf16[128,1024]{1,0:T(8,128)(2,1)S(1)}, bf16[128,1024]{1,0:T(8,128)(2,1)S(1)}, u32[]{:S(2)}, u32[]{:S(2)}) collective-permute-start(bf16[128,1024]{1,0:T(8,128)(2,1)S(1)} %get-tuple-element.36.refs_0_), channel_id=1, source_target_pairs={{2,128},{4,130},{6,132},{8,134},{10,136},{12,138},{14,140},{16,142... | collective-permute-start | bytes 786440 | tf_op jit(solution)/shard_map/up_l1c0/ppermute | solution.py:207
  29.0 1.2 %collective-permute-start.7 = (bf16[64,1024]{1,0:T(8,128)(2,1)S(1)}, bf16[64,1024]{1,0:T(8,128)(2,1)S(1)}, u32[]{:S(2)}, u32[]{:S(2)}) collective-permute-start(bf16[64,1024]{1,0:T(8,128)(2,1)S(1)} %get-tuple-element.38), channel_id=1, source_target_pairs={{126,128},{0,130},{2,132},{4,134},{6,136},{8,138},{10,140},{12,142... | collective-permute-start | bytes 393224 | tf_op jit(solution)/shard_map/down_l1c0/ppermute | solution.py:207
  30.8 4.7 %collective-permute-start.11 = (bf16[128,1024]{1,0:T(8,128)(2,1)S(1)}, bf16[128,1024]{1,0:T(8,128)(2,1)S(1)}, u32[]{:S(2)}, u32[]{:S(2)}) collective-permute-start(bf16[128,1024]{1,0:T(8,128)(2,1)S(1)} %get-tuple-element.39.refs_2_), channel_id=1, source_target_pairs={{128,256},{130,258},{132,260},{134,262},{136,264},{138,266},{140,2... | collective-permute-start | bytes 786440 | tf_op jit(solution)/shard_map/own_l2c0/ppermute | solution.py:207
  31.5 4.7 %collective-permute-start.9 = (bf16[128,1024]{1,0:T(8,128)(2,1)S(1)}, bf16[128,1024]{1,0:T(8,128)(2,1)S(1)}, u32[]{:S(2)}, u32[]{:S(2)}) collective-permute-start(bf16[128,1024]{1,0:T(8,128)(2,1)S(1)} %get-tuple-element.39.refs_2_), channel_id=1, source_target_pairs={{130,256},{132,258},{134,260},{136,262},{138,264},{140,266},{142,2... | collective-permute-start | bytes 786440 | tf_op jit(solution)/shard_map/up_l2c0/ppermute | solution.py:207
  32.2 7.4 %collective-permute-start.17 = (f32[128,1024]{1,0:T(8,128)S(1)}, f32[128,1024]{1,0:T(8,128)S(1)}, u32[]{:S(2)}, u32[]{:S(2)}) collective-permute-start(f32[128,1024]{1,0:T(8,128)S(1)} %get-tuple-element.45), channel_id=1, source_target_pairs={{128,129},{130,131},{132,133},{134,135},{136,137},{138,139},{140,1... | collective-permute-start | bytes 1572872 | tf_op jit(solution)/shard_map/lent_l1/ppermute | solution.py:207
  32.9 1.9 %collective-permute-start.10 = (bf16[64,1024]{1,0:T(8,128)(2,1)S(1)}, bf16[64,1024]{1,0:T(8,128)(2,1)S(1)}, u32[]{:S(2)}, u32[]{:S(2)}) collective-permute-start(bf16[64,1024]{1,0:T(8,128)(2,1)S(1)} %get-tuple-element.40), channel_id=1, source_target_pairs={{254,256},{128,258},{130,260},{132,262},{134,264},{136,266},{138,2... | collective-permute-start | bytes 393224 | tf_op jit(solution)/shard_map/down_l2c0/ppermute | solution.py:207
  34.1 4.0 %collective-permute-start.20 = (bf16[128,1024]{1,0:T(8,128)(2,1)S(1)}, bf16[128,1024]{1,0:T(8,128)(2,1)S(1)}, u32[]{:S(2)}, u32[]{:S(2)}) collective-permute-start(bf16[128,1024]{1,0:T(8,128)(2,1)S(1)} %get-tuple-element.46.refs_1_), channel_id=1, source_target_pairs={{1,129},{3,131},{5,133},{7,135},{9,137},{11,139},{13,141},{15,143}... | collective-permute-start | bytes 786440 | tf_op jit(solution)/shard_map/own_l1c1/ppermute | solution.py:207
  34.8 4.0 %collective-permute-start.18 = (bf16[128,1024]{1,0:T(8,128)(2,1)S(1)}, bf16[128,1024]{1,0:T(8,128)(2,1)S(1)}, u32[]{:S(2)}, u32[]{:S(2)}) collective-permute-start(bf16[128,1024]{1,0:T(8,128)(2,1)S(1)} %get-tuple-element.46.refs_1_), channel_id=1, source_target_pairs={{3,129},{5,131},{7,133},{9,135},{11,137},{13,139},{15,141},{17,143... | collective-permute-start | bytes 786440 | tf_op jit(solution)/shard_map/up_l1c1/ppermute | solution.py:207
  35.5 1.9 %collective-permute-start.19 = (bf16[64,1024]{1,0:T(8,128)(2,1)S(1)}, bf16[64,1024]{1,0:T(8,128)(2,1)S(1)}, u32[]{:S(2)}, u32[]{:S(2)}) collective-permute-start(bf16[64,1024]{1,0:T(8,128)(2,1)S(1)} %get-tuple-element.47), channel_id=1, source_target_pairs={{127,129},{1,131},{3,133},{5,135},{7,137},{9,139},{11,141},{13,143... | collective-permute-start | bytes 393224 | tf_op jit(solution)/shard_map/down_l1c1/ppermute | solution.py:207
  36.7 4.7 %collective-permute-start.14 = (bf16[128,1024]{1,0:T(8,128)(2,1)S(1)}, bf16[128,1024]{1,0:T(8,128)(2,1)S(1)}, u32[]{:S(2)}, u32[]{:S(2)}) collective-permute-start(bf16[128,1024]{1,0:T(8,128)(2,1)S(1)} %get-tuple-element.41.refs_4_), channel_id=1, source_target_pairs={{256,384},{258,386},{260,388},{262,390},{264,392},{266,394},{268,3... | collective-permute-start | bytes 786440 | tf_op jit(solution)/shard_map/own_l3c0/ppermute | solution.py:207
  37.4 7.2 %collective-permute-start.16 = (f32[128,1024]{1,0:T(8,128)S(1)}, f32[128,1024]{1,0:T(8,128)S(1)}, u32[]{:S(2)}, u32[]{:S(2)}) collective-permute-start(f32[128,1024]{1,0:T(8,128)S(1)} %get-tuple-element.44), channel_id=1, source_target_pairs={{256,257},{258,259},{260,261},{262,263},{264,265},{266,267},{268,2... | collective-permute-start | bytes 1572872 | tf_op jit(solution)/shard_map/lent_l2/ppermute | solution.py:207
  38.1 3.3 %collective-permute-start.12 = (bf16[128,1024]{1,0:T(8,128)(2,1)S(1)}, bf16[128,1024]{1,0:T(8,128)(2,1)S(1)}, u32[]{:S(2)}, u32[]{:S(2)}) collective-permute-start(bf16[128,1024]{1,0:T(8,128)(2,1)S(1)} %get-tuple-element.41.refs_4_), channel_id=1, source_target_pairs={{258,384},{260,386},{262,388},{264,390},{266,392},{268,394},{270,3... | collective-permute-start | bytes 786440 | tf_op jit(solution)/shard_map/up_l3c0/ppermute | solution.py:207
  38.8 1.9 %collective-permute-start.13 = (bf16[64,1024]{1,0:T(8,128)(2,1)S(1)}, bf16[64,1024]{1,0:T(8,128)(2,1)S(1)}, u32[]{:S(2)}, u32[]{:S(2)}) collective-permute-start(bf16[64,1024]{1,0:T(8,128)(2,1)S(1)} %get-tuple-element.42), channel_id=1, source_target_pairs={{382,384},{256,386},{258,388},{260,390},{262,392},{264,394},{266,3... | collective-permute-start | bytes 393224 | tf_op jit(solution)/shard_map/down_l3c0/ppermute | solution.py:207
  40.1 4.6 %collective-permute-start.23 = (bf16[128,1024]{1,0:T(8,128)(2,1)S(1)}, bf16[128,1024]{1,0:T(8,128)(2,1)S(1)}, u32[]{:S(2)}, u32[]{:S(2)}) collective-permute-start(bf16[128,1024]{1,0:T(8,128)(2,1)S(1)} %get-tuple-element.48.refs_3_), channel_id=1, source_target_pairs={{129,257},{131,259},{133,261},{135,263},{137,265},{139,267},{141,2... | collective-permute-start | bytes 786440 | tf_op jit(solution)/shard_map/slab1_l1/own_l2c1/ppermute | solution.py:207
  40.8 3.9 %collective-permute-start.21 = (bf16[128,1024]{1,0:T(8,128)(2,1)S(1)}, bf16[128,1024]{1,0:T(8,128)(2,1)S(1)}, u32[]{:S(2)}, u32[]{:S(2)}) collective-permute-start(bf16[128,1024]{1,0:T(8,128)(2,1)S(1)} %get-tuple-element.48.refs_3_), channel_id=1, source_target_pairs={{131,257},{133,259},{135,261},{137,263},{139,265},{141,267},{143,2... | collective-permute-start | bytes 786440 | tf_op jit(solution)/shard_map/slab1_l1/up_l2c1/ppermute | solution.py:207
  42.7 38.6 %collective-permute-start.15 = (f32[128,1024]{1,0:T(8,128)S(1)}, f32[128,1024]{1,0:T(8,128)S(1)}, u32[]{:S(2)}, u32[]{:S(2)}) collective-permute-start(f32[128,1024]{1,0:T(8,128)S(1)} %get-tuple-element.43), channel_id=1, source_target_pairs={{384,385},{386,387},{388,389},{390,391},{392,393},{394,395},{396,3... | collective-permute-start | bytes 1572872 | tf_op jit(solution)/shard_map/lent_l3/ppermute | solution.py:207
  44.0 0.7 collective-permute-start.22
  45.3 36.0 %collective-permute-start.26 = (bf16[128,1024]{1,0:T(8,128)(2,1)S(1)}, bf16[128,1024]{1,0:T(8,128)(2,1)S(1)}, u32[]{:S(2)}, u32[]{:S(2)}) collective-permute-start(bf16[128,1024]{1,0:T(8,128)(2,1)S(1)} %get-tuple-element.50.refs_5_), channel_id=1, source_target_pairs={{257,385},{259,387},{261,389},{263,391},{265,393},{267,395},{269,3... | collective-permute-start | bytes 786440 | tf_op jit(solution)/shard_map/slab1_l2/own_l3c1/ppermute | solution.py:207
  46.6 34.7 %collective-permute-start.24 = (bf16[128,1024]{1,0:T(8,128)(2,1)S(1)}, bf16[128,1024]{1,0:T(8,128)(2,1)S(1)}, u32[]{:S(2)}, u32[]{:S(2)}) collective-permute-start(bf16[128,1024]{1,0:T(8,128)(2,1)S(1)} %get-tuple-element.50.refs_5_), channel_id=1, source_target_pairs={{259,385},{261,387},{263,389},{265,391},{267,393},{269,395},{271,3... | collective-permute-start | bytes 786440 | tf_op jit(solution)/shard_map/slab1_l2/up_l3c1/ppermute | solution.py:207
  47.9 26.0 %collective-permute-start.25 = (bf16[64,1024]{1,0:T(8,128)(2,1)S(1)}, bf16[64,1024]{1,0:T(8,128)(2,1)S(1)}, u32[]{:S(2)}, u32[]{:S(2)}) collective-permute-start(bf16[64,1024]{1,0:T(8,128)(2,1)S(1)} %get-tuple-element.51), channel_id=1, source_target_pairs={{383,385},{257,387},{259,389},{261,391},{263,393},{265,395},{267,3... | collective-permute-start | bytes 393224 | tf_op jit(solution)/shard_map/slab1_l2/down_l3c1/ppermute | solution.py:207
  82.8 4.0 %collective-permute-start.27 = (bf16[64,1024]{1,0:T(8,128)(2,1)S(1)}, bf16[64,1024]{1,0:T(8,128)(2,1)S(1)}, u32[]{:S(2)}, u32[]{:S(2)}) collective-permute-start(bf16[64,1024]{1,0:T(8,128)(2,1)S(1)} %get-tuple-element.54), channel_id=1, source_target_pairs={{1,0},{0,1},{3,2},{2,3},{5,4},{4,5},{7,6},{6,7},{9,8},{8,9},{11,10... | collective-permute-start | bytes 393224 | tf_op jit(solution)/shard_map/last_swap/ppermute | solution.py:207
  (1 other events, 0.7 us)
